TPU v7x, 32 devices: a whole 2x2x4 slice. The times are simulated.
32 devices in a mesh: dp: 4 (over y, core), row: 2 (over x), col: 4 (over z).
Axes of the slice: x: 2, y: 2, z: 4, core: 2. Of those that a mesh axis runs over, the one named last changes fastest.
Arguments:
- block_input: bfloat16 [8192, 2048], P(('dp', 'row'), 'col'), may hold values from -7.2 to 7.2
- cotangent: bfloat16 [8192, 2048], P(('dp', 'row'), 'col'), may hold values from -7.2 to 7.2
- segments: int32 [4, 2048], P('dp'), may hold values from 0 to 3, never falling along the last dimension, each value on 1 to 1024 neighbouring positions
- norm_gains: float32 [2, 2048], P(None, 'col'), may hold values from 0.5 to 1.5
- w_query: float32 [2048, 2048], P('col', 'row'), may hold values from -0.125 to 0.125
- w_keyvalue: float32 [2048, 512], P('col'), may hold values from -0.125 to 0.125
- w_output: float32 [2048, 2048], P('row', 'col'), may hold values from -1 to 1
- w_gateup: float32 [2048, 2, 5632], P('col', None, 'row'), may hold values from -0.125 to 0.125
- w_down: float32 [5632, 2048], P('row', 'col'), may hold values from -0.078125 to 0.078125
- gains_moment: float32 [2, 2048], P(None, 'col'), may hold values from -64 to 64
- gains_square: float32 [2, 2048], P(None, 'col'), may hold values from 4.096 to 65.536
- query_moment: float32 [2048, 2048], P('col', 'row'), may hold values from -128 to 128
- query_square: float32 [2048, 2048], P('col', 'row'), may hold values from 16.384 to 262.144
- keyvalue_moment: float32 [2048, 512], P('col'), may hold values from -160 to 160
- keyvalue_square: float32 [2048, 512], P('col'), may hold values from 32.768 to 524.288
- output_moment: float32 [2048, 2048], P('row', 'col'), may hold values from -6 to 6
- output_square: float32 [2048, 2048], P('row', 'col'), may hold values from 0.04096 to 0.65536
- gateup_moment: float32 [2048, 2, 5632], P('col', None, 'row'), may hold values from -20 to 20
- gateup_square: float32 [2048, 2, 5632], P('col', None, 'row'), may hold values from 0.4096 to 6.5536
- down_moment: float32 [5632, 2048], P('row', 'col'), may hold values from -40 to 40
- down_square: float32 [5632, 2048], P('row', 'col'), may hold values from 1.6384 to 26.2144
Outputs:
- layer_output: bfloat16 [8192, 2048], P(('dp', 'row'), 'col')
- input_grad: float32 [8192, 2048], P(('dp', 'row'), 'col')
- new_gains_moment: float32 [2, 2048], P(None, 'col')
- new_gains_square: float32 [2, 2048], P(None, 'col')
- new_gains: float32 [2, 2048], P(None, 'col')
- new_query_moment: float32 [2048, 2048], P('col', 'row')
- new_query_square: float32 [2048, 2048], P('col', 'row')
- new_query: float32 [2048, 2048], P('col', 'row')
- new_keyvalue_moment: float32 [2048, 512], P('col')
- new_keyvalue_square: float32 [2048, 512], P('col')
- new_keyvalue: float32 [2048, 512], P('col')
- new_output_moment: float32 [2048, 2048], P('row', 'col')
- new_output_square: float32 [2048, 2048], P('row', 'col')
- new_output: float32 [2048, 2048], P('row', 'col')
- new_gateup_moment: float32 [2048, 2, 5632], P('col', None, 'row')
- new_gateup_square: float32 [2048, 2, 5632], P('col', None, 'row')
- new_gateup: float32 [2048, 2, 5632], P('col', None, 'row')
- new_down_moment: float32 [5632, 2048], P('row', 'col')
- new_down_square: float32 [5632, 2048], P('row', 'col')
- new_down: float32 [5632, 2048], P('row', 'col')
All inputs are finite; a program needn't handle non-finite values.
Results may differ from a plain program's by a relative error of at most 0.025.
Values may be sent and summed in bfloat16 or wider, within the bound.
No kernel may reach another device: no remote copies, remote signals or barrier semaphores. Data moves between devices by JAX's collectives and lax.ppermute only.
A program may use at most 448 MiB of HBM per device.

v0:
```python
import functools

import jax
import jax.numpy as jnp
from jax import lax
from jax.experimental import pallas as pl
from jax.experimental.pallas import tpu as pltpu
from jax.sharding import Mesh, PartitionSpec as P

D = 2048
HEADS = 32
KV_HEADS = 4
HEAD_DIM = 64
FF = 5632
STEP = 10

EPSILON = 1e-05
BETA_ONE = 0.9
BETA_TWO = 0.999
ADAM_EPS = 1e-08
MASKED = -1e30
SCORE_SCALE = HEAD_DIM ** (-0.5)
LANES = 128
VMEM_LIMIT = 48 * 1024 * 1024


def dot_nn(left, right):
    return lax.dot_general(left, right, (((1,), (0,)), ((), ())), preferred_element_type=jnp.float32)


def dot_nt(left, right):
    return lax.dot_general(left, right, (((1,), (1,)), ((), ())), preferred_element_type=jnp.float32)


def dot_tn(left, right):
    return lax.dot_general(left, right, (((0,), (0,)), ((), ())), preferred_element_type=jnp.float32)


def adamw_step(weight, gradient, moment, square, step_rate, decay_rate):
    moment_new = BETA_ONE * moment + (1.0 - BETA_ONE) * gradient
    square_new = BETA_TWO * square + (1.0 - BETA_TWO) * gradient * gradient
    fixed_one = moment_new / (1.0 - BETA_ONE**STEP)
    fixed_two = square_new / (1.0 - BETA_TWO**STEP)
    weight_new = weight - step_rate * (
        fixed_one / (jnp.sqrt(fixed_two) + ADAM_EPS) + decay_rate * weight
    )
    return (moment_new, square_new, weight_new)


def document_starts(segment_ids):
    places = jnp.arange(segment_ids.shape[0], dtype=jnp.int32)
    starts = jnp.concatenate([jnp.ones((1,), jnp.bool_), segment_ids[1:] != segment_ids[:-1]])
    return lax.cummax(jnp.where(starts, places, 0), axis=0)


def turn(values):
    lane = lax.broadcasted_iota(jnp.int32, values.shape, 1)
    ahead = pltpu.roll(values, LANES - HEAD_DIM // 2, 1)
    behind = pltpu.roll(values, HEAD_DIM // 2, 1)
    return jnp.where(lane % HEAD_DIM < HEAD_DIM // 2, -ahead, behind)


def take_chunk(rows_refs, held_ref):
    for at, ref in enumerate(rows_refs):

        @pl.when(pl.program_id(0) == at)
        def _(ref=ref):
            held_ref[...] = ref[...]


def project_kernel(slots, *refs):
    rows_refs, (weight_ref, cos_ref, sin_ref, query_ref, pair_ref, held_ref) = (refs[:slots], refs[slots:])
    take_chunk(rows_refs, held_ref)
    sums = dot_nn(held_ref[...], weight_ref[...])
    cosine, sine = cos_ref[...], sin_ref[...]
    width = query_ref.shape[1]
    lane = lax.broadcasted_iota(jnp.int32, cosine.shape, 1)
    for start in range(0, width, LANES):
        part = sums[:, start : start + LANES]
        turned = (part * cosine + turn(part) * sine).astype(jnp.bfloat16)
        query_ref[:, start : start + LANES] = turned * jnp.bfloat16(SCORE_SCALE)
    for which in range(2):
        part = sums[:, width + which * LANES : width + (which + 1) * LANES]
        is_key = (lane < HEAD_DIM) if which == 0 else (lane >= HEAD_DIM)
        turned = jnp.where(is_key, part * cosine + turn(part) * sine, part)
        pair_ref[:, which * LANES : (which + 1) * LANES] = turned.astype(jnp.bfloat16)


def project(chunks, weight, total, cosine, sine, width):
    slots = len(chunks)
    block, depth = chunks[0].shape
    rows = slots * block
    whole = pl.BlockSpec((block, depth), lambda i: (0, 0))
    return pl.pallas_call(
        functools.partial(project_kernel, slots),
        grid=(slots,),
        in_specs=[whole] * slots
        + [
            pl.BlockSpec((depth, total), lambda i: (0, 0)),
            pl.BlockSpec((block, LANES), lambda i: (i, 0)),
            pl.BlockSpec((block, LANES), lambda i: (i, 0)),
        ],
        out_specs=[
            pl.BlockSpec((block, width), lambda i: (i, 0)),
            pl.BlockSpec((block, total - width), lambda i: (i, 0)),
        ],
        out_shape=[
            jax.ShapeDtypeStruct((rows, width), jnp.bfloat16),
            jax.ShapeDtypeStruct((rows, total - width), jnp.bfloat16),
        ],
        scratch_shapes=[pltpu.VMEM((block, depth), jnp.bfloat16)],
        compiler_params=pltpu.CompilerParams(vmem_limit_bytes=VMEM_LIMIT),
        cost_estimate=pl.CostEstimate(
            flops=2 * rows * depth * total,
            bytes_accessed=(rows + total) * depth * 2,
            transcendentals=0,
        ),
        name="project",
    )(*chunks, weight, cosine, sine)


def widen_kernel(slots, *refs):
    rows_refs, (weight_ref, hidden_ref, factor_ref, silu_ref, held_ref) = (refs[:slots], refs[slots:])
    take_chunk(rows_refs, held_ref)
    sums = dot_nn(held_ref[...], weight_ref[...])
    width = hidden_ref.shape[1]
    gate, upward = (sums[:, :width], sums[:, width:])
    sigmoid = jax.nn.sigmoid(gate)
    silu = gate * sigmoid
    hidden_ref[...] = (silu * upward).astype(jnp.bfloat16)
    factor_ref[...] = (upward * sigmoid * (1.0 + gate * (1.0 - sigmoid))).astype(jnp.bfloat16)
    silu_ref[...] = silu.astype(jnp.bfloat16)


def widen(chunks, weight):
    slots = len(chunks)
    block, depth = chunks[0].shape
    width = weight.shape[1] // 2
    rows = slots * block
    once = pl.Buffered(1)
    return pl.pallas_call(
        functools.partial(widen_kernel, slots),
        grid=(slots,),
        in_specs=[pl.BlockSpec((block, depth), lambda i: (0, 0), pipeline_mode=once)] * slots
        + [pl.BlockSpec(weight.shape, lambda i: (0, 0), pipeline_mode=once)],
        out_specs=[pl.BlockSpec((block, width), lambda i: (i, 0))] * 3,
        out_shape=[jax.ShapeDtypeStruct((rows, width), jnp.bfloat16)] * 3,
        scratch_shapes=[pltpu.VMEM((block, depth), jnp.bfloat16)],
        compiler_params=pltpu.CompilerParams(vmem_limit_bytes=VMEM_LIMIT),
        cost_estimate=pl.CostEstimate(
            flops=4 * rows * depth * width,
            bytes_accessed=(rows + 2 * width) * depth * 2 + 6 * rows * width,
            transcendentals=rows * width,
        ),
        name="widen",
    )(*chunks, weight)


def widen_back_kernel(slots, kept, *refs):
    rows_refs, refs = (refs[:slots], refs[slots:])
    down_ref, gateup_ref, factor_ref, silu_ref = refs[:4]
    gate_ref, up_ref, partial_ref, held_ref = refs[4 + kept :]
    take_chunk(rows_refs, held_ref)
    grad_hidden = dot_nn(held_ref[...], down_ref[...])
    gate = (grad_hidden * factor_ref[...].astype(jnp.float32)).astype(jnp.bfloat16)
    up = (grad_hidden * silu_ref[...].astype(jnp.float32)).astype(jnp.bfloat16)
    gate_ref[...] = gate
    up_ref[...] = up
    both = jnp.concatenate([gate, up], axis=1)
    partial_ref[...] = dot_nt(both, gateup_ref[...]).astype(jnp.bfloat16)


def widen_back(chunks, down, gateup, factor, silu, first, kept):
    slots = len(chunks)
    block, depth = chunks[0].shape
    width = down.shape[1]
    once = pl.Buffered(1)
    tile = pl.BlockSpec((block, width), lambda i: (first + i, 0))
    return pl.pallas_call(
        functools.partial(widen_back_kernel, slots, len(kept)),
        grid=(slots,),
        in_specs=[pl.BlockSpec((block, depth), lambda i: (0, 0), pipeline_mode=once)] * slots
        + [
            pl.BlockSpec(down.shape, lambda i: (0, 0), pipeline_mode=once),
            pl.BlockSpec(gateup.shape, lambda i: (0, 0), pipeline_mode=once),
            tile,
            tile,
        ]
        + [pl.BlockSpec(memory_space=pl.ANY)] * len(kept),
        out_specs=[tile, tile, pl.BlockSpec((block, depth), lambda i: (i, 0))],
        out_shape=[jax.ShapeDtypeStruct(factor.shape, jnp.bfloat16)] * 2
        + [jax.ShapeDtypeStruct((slots * block, depth), jnp.bfloat16)],
        scratch_shapes=[pltpu.VMEM((block, depth), jnp.bfloat16)],
        input_output_aliases={slots + 4 + i: i for i in range(len(kept))},
        compiler_params=pltpu.CompilerParams(vmem_limit_bytes=VMEM_LIMIT),
        cost_estimate=pl.CostEstimate(
            flops=6 * slots * block * depth * width,
            bytes_accessed=3 * width * depth * 2 + 8 * slots * block * width,
            transcendentals=0,
        ),
        name="widen_back",
    )(*chunks, down, gateup, factor, silu, *kept)


def stack_heads(values):
    return jnp.concatenate(
        [values[:, start : start + LANES] for start in range(0, values.shape[1], LANES)], axis=0
    )


def block_of(meta_ref, chunk, step, parts, lines):
    base = chunk * (2 + parts)
    key_block = meta_ref[base + 1] - step
    slot = meta_ref[base + 2 + key_block // lines]
    own_line = meta_ref[pl.num_programs(0) * (2 + parts)]
    line = lax.rem(key_block, lines)
    return (key_block, slot, line, lax.rem(own_line - line + lines, lines))


def attend_kernel(parts, lines, meta_ref, query_ref, pair_ref, info_ref, out_ref, log_ref):
    chunk = pl.program_id(0)
    block = query_ref.shape[0]
    heads = query_ref.shape[1] // LANES
    stacked = stack_heads(query_ref[...])
    lane = lax.broadcasted_iota(jnp.int32, stacked.shape, 1)
    place = jnp.concatenate([info_ref[0, 0:1, :]] * heads, axis=1)
    start = jnp.concatenate([info_ref[0, 1:2, :]] * heads, axis=1)
    base = chunk * (2 + parts)
    steps = meta_ref[base + 1] - meta_ref[base] + 1
    width = heads * block
    outs = []
    for which in range(2):
        is_key = (lane < HEAD_DIM) if which == 0 else (lane >= HEAD_DIM)
        queries = jnp.where(is_key, stacked, jnp.zeros_like(stacked))

        def body(step, carry):
            peak, total, mixed = carry
            key_block, slot, at, _ = block_of(meta_ref, chunk, step, parts, lines)
            pair = pair_ref[at, slot, :, which * LANES : (which + 1) * LANES]
            scores = dot_nt(pair, queries)
            key_place = key_block * block + lax.broadcasted_iota(jnp.int32, (block, width), 0)
            scores = jnp.where((key_place <= place) & (key_place >= start), scores, MASKED)
            new_peak = jnp.maximum(peak, jnp.max(scores, axis=0, keepdims=True))
            weights = jnp.exp(scores - new_peak)
            shrink = jnp.exp(peak - new_peak)
            total = total * shrink + jnp.sum(weights, axis=0, keepdims=True)
            mixed = mixed * shrink + dot_tn(pair, weights.astype(jnp.bfloat16))
            return (new_peak, total, mixed)

        peak, total, mixed = lax.fori_loop(
            0,
            steps,
            body,
            (
                jnp.full((1, width), MASKED, jnp.float32),
                jnp.zeros((1, width), jnp.float32),
                jnp.zeros((LANES, width), jnp.float32),
            ),
        )
        log_ref[0, which : which + 1, :] = peak + jnp.log(total)
        outs.append(mixed / total)
    joined = jnp.concatenate([outs[1][:HEAD_DIM], outs[0][HEAD_DIM:]], axis=0)
    rows = joined.T.astype(jnp.bfloat16)
    for head in range(heads):
        out_ref[:, head * LANES : (head + 1) * LANES] = rows[head * block : (head + 1) * block]


def attend(meta, queries, pairs, info, parts):
    chunks, block = (info.shape[0], info.shape[2])
    width = queries.shape[1]
    heads = width // LANES
    lines = pairs.shape[0]
    steps = 3 * chunks
    return pl.pallas_call(
        functools.partial(attend_kernel, parts, lines),
        grid_spec=pltpu.PrefetchScalarGridSpec(
            num_scalar_prefetch=1,
            grid=(chunks,),
            in_specs=[
                pl.BlockSpec((block, width), lambda i, m: (i, 0)),
                pl.BlockSpec(pairs.shape, lambda i, m: (0, 0, 0, 0)),
                pl.BlockSpec((1, 2, block), lambda i, m: (i, 0, 0)),
            ],
            out_specs=[
                pl.BlockSpec((block, width), lambda i, m: (i, 0)),
                pl.BlockSpec((1, 2, heads * block), lambda i, m: (i, 0, 0)),
            ],
        ),
        out_shape=[
            jax.ShapeDtypeStruct(queries.shape, jnp.bfloat16),
            jax.ShapeDtypeStruct((chunks, 2, heads * block), jnp.float32),
        ],
        compiler_params=pltpu.CompilerParams(vmem_limit_bytes=VMEM_LIMIT),
        cost_estimate=pl.CostEstimate(
            flops=steps * 2 * 2 * 2 * heads * block * block * LANES,
            bytes_accessed=queries.size * 4 + pairs.size * 2,
            transcendentals=steps * 2 * heads * block * block,
        ),
        name="attend",
    )(meta, queries, pairs, info)


def attend_back_kernel(parts, lines, meta_ref, query_ref, *refs):
    pair_ref, grad_ref, mixed_ref, log_ref, info_ref, cos_ref, sin_ref, query_out = refs[:8]
    pair_outs = refs[8 : 8 + lines]
    sums = refs[8 + lines]
    chunk = pl.program_id(0)
    block = query_ref.shape[0]
    heads = query_ref.shape[1] // LANES

    @pl.when(chunk == 0)
    def _():
        sums[...] = jnp.zeros_like(sums)

    stacked = stack_heads(query_ref[...])
    stacked_grad = stack_heads(grad_ref[...])
    product = stacked_grad.astype(jnp.float32) * stack_heads(mixed_ref[...]).astype(jnp.float32)
    lane = lax.broadcasted_iota(jnp.int32, stacked.shape, 1)
    place = jnp.concatenate([info_ref[0, 0:1, :]] * heads, axis=1)
    start = jnp.concatenate([info_ref[0, 1:2, :]] * heads, axis=1)
    base = chunk * (2 + parts)
    steps = meta_ref[base + 1] - meta_ref[base] + 1
    width = heads * block
    grads = []
    for which in range(2):
        is_key = (lane < HEAD_DIM) if which == 0 else (lane >= HEAD_DIM)
        queries = jnp.where(is_key, stacked, jnp.zeros_like(stacked))
        grad = jnp.where(is_key, jnp.zeros_like(stacked_grad), stacked_grad)
        own = jnp.where(is_key, 0.0, product)
        centre = lax.dot_general(
            jnp.ones((8, LANES), jnp.float32),
            own,
            (((1,), (1,)), ((), ())),
            precision=lax.Precision.HIGHEST,
            preferred_element_type=jnp.float32,
        )[0:1]
        logs = log_ref[0, which : which + 1, :]

        def body(step, grad_query):
            key_block, slot, at, shift = block_of(meta_ref, chunk, step, parts, lines)
            columns = slice(which * LANES, (which + 1) * LANES)
            pair = pair_ref[at, slot, :, columns]
            scores = dot_nt(pair, queries)
            key_place = key_block * block + lax.broadcasted_iota(jnp.int32, (block, width), 0)
            scores = jnp.where((key_place <= place) & (key_place >= start), scores, MASKED)
            weights = jnp.exp(scores - logs)
            grad_scores = (weights * (dot_nt(pair, grad) - centre)).astype(jnp.bfloat16)
            sums[shift, slot, :, columns] += dot_nn(grad_scores, queries) + dot_nn(
                weights.astype(jnp.bfloat16), grad
            )
            return grad_query + dot_tn(pair, grad_scores)

        grads.append(lax.fori_loop(0, steps, body, jnp.zeros((LANES, width), jnp.float32)))
    joined = jnp.concatenate([grads[0][:HEAD_DIM], grads[1][HEAD_DIM:]], axis=0)
    rows = joined.T * SCORE_SCALE
    cosine, sine = cos_ref[...], sin_ref[...]
    for head in range(heads):
        part = rows[head * block : (head + 1) * block]
        back = part * cosine - turn(part) * sine
        query_out[:, head * LANES : (head + 1) * LANES] = back.astype(jnp.bfloat16)

    @pl.when(chunk == pl.num_programs(0) - 1)
    def _():
        for line in range(lines):
            pair_outs[line][...] = sums[line].astype(jnp.bfloat16)


def attend_back(meta, queries, pairs, grad_mixed, mixed, logs, info, cosine, sine, parts):
    chunks, block = (info.shape[0], info.shape[2])
    width = queries.shape[1]
    heads = width // LANES
    lines = pairs.shape[0]
    shape = pairs.shape[1:]
    steps = 3 * chunks
    wide = pl.BlockSpec((block, width), lambda i, m: (i, 0))
    table = pl.BlockSpec((block, LANES), lambda i, m: (i, 0))
    whole = pl.BlockSpec(shape, lambda i, m: (0, 0, 0))
    outs = pl.pallas_call(
        functools.partial(attend_back_kernel, parts, lines),
        grid_spec=pltpu.PrefetchScalarGridSpec(
            num_scalar_prefetch=1,
            grid=(chunks,),
            in_specs=[
                wide,
                pl.BlockSpec(pairs.shape, lambda i, m: (0, 0, 0, 0)),
                wide,
                wide,
                pl.BlockSpec((1, 2, heads * block), lambda i, m: (i, 0, 0)),
                pl.BlockSpec((1, 2, block), lambda i, m: (i, 0, 0)),
                table,
                table,
            ],
            out_specs=[wide] + [whole] * lines,
            scratch_shapes=[pltpu.VMEM(pairs.shape, jnp.float32)],
        ),
        out_shape=[jax.ShapeDtypeStruct(queries.shape, jnp.bfloat16)]
        + [jax.ShapeDtypeStruct(shape, jnp.bfloat16)] * lines,
        compiler_params=pltpu.CompilerParams(vmem_limit_bytes=VMEM_LIMIT),
        cost_estimate=pl.CostEstimate(
            flops=steps * 2 * 5 * 2 * heads * block * block * LANES,
            bytes_accessed=queries.size * 8 + 2 * pairs.size * 2,
            transcendentals=steps * 2 * heads * block * block,
        ),
        name="attend_back",
    )(
        meta,
        queries,
        pairs,
        grad_mixed,
        mixed,
        logs,
        info,
        cosine,
        sine,
    )
    return (outs[0], [out.reshape(chunks * block, 2 * LANES) for out in outs[1:]])


def pair_back_kernel(*refs):
    *part_refs, cos_ref, sin_ref, out_ref = refs
    cosine, sine = cos_ref[...], sin_ref[...]
    lane = lax.broadcasted_iota(jnp.int32, cosine.shape, 1)
    for which in range(2):
        columns = slice(which * LANES, (which + 1) * LANES)
        total = part_refs[0][:, columns].astype(jnp.float32)
        for ref in part_refs[1:]:
            total = total + ref[:, columns].astype(jnp.float32)
        is_key = (lane < HEAD_DIM) if which == 0 else (lane >= HEAD_DIM)
        total = jnp.where(is_key, total * cosine - turn(total) * sine, total)
        out_ref[:, columns] = total.astype(jnp.bfloat16)


def pair_back(parts, cosine, sine, block):
    rows, columns = parts[0].shape
    tile = pl.BlockSpec((block, columns), lambda i: (i, 0))
    table = pl.BlockSpec((block, LANES), lambda i: (i, 0))
    return pl.pallas_call(
        pair_back_kernel,
        grid=(rows // block,),
        in_specs=[tile] * len(parts) + [table, table],
        out_specs=tile,
        out_shape=jax.ShapeDtypeStruct((rows, columns), jnp.bfloat16),
        compiler_params=pltpu.CompilerParams(vmem_limit_bytes=VMEM_LIMIT),
        name="pair_back",
    )(*parts, cosine, sine)


def update(refs, index, gradient, rate):
    weight, moment, square = [ref[index] for ref in refs[:3]]
    moment_new, square_new, weight_new = adamw_step(weight, gradient, moment, square, rate, 0.1)
    for ref, value in zip(refs[3:], (moment_new, square_new, weight_new)):
        ref[index] = value


def chosen(meta_ref, grad_refs, at, rows, columns):
    own_y = meta_ref[0] == at
    first = pl.program_id(0) == 0
    near = jnp.where(first, grad_refs[0][rows, columns], grad_refs[2][rows, columns])
    far = jnp.where(first, grad_refs[1][rows, columns], grad_refs[3][rows, columns])
    return jnp.where(own_y, near, far).astype(jnp.float32)


def joint_update_kernel(meta_ref, *refs):
    grad_refs, query_refs, pair_refs = (refs[:4], refs[4:7] + refs[10:13], refs[7:10] + refs[13:16])
    groups = query_refs[0].shape[1] // (2 * LANES)
    every = slice(None)
    for at in range(2):
        for j in range(groups):
            gradient = chosen(meta_ref, grad_refs, at, every, slice(j * LANES, (j + 1) * LANES))
            place = slice((2 * j + at) * LANES, (2 * j + at + 1) * LANES)
            update(query_refs, (every, place), gradient, D ** (-0.5))
        for which in range(2):
            start = (groups + which) * LANES
            gradient = chosen(meta_ref, grad_refs, at, every, slice(start, start + LANES))
            if which == 1:
                gradient = pltpu.roll(gradient, HEAD_DIM, 1)
            place = slice((2 * at + which) * LANES, (2 * at + which + 1) * LANES)
            update(pair_refs, (every, place), gradient, D ** (-0.5))


def joint_update(meta, grads, query, pair):
    half = grads[0].shape[0]

    def rows_of(array):
        return pl.BlockSpec((half, array.shape[1]), lambda i, m: ((m[1] + i) % 2, 0))

    whole = pl.BlockSpec(grads[0].shape, lambda i, m: (0, 0))
    blocks = [rows_of(array) for array in (*query, *pair)]
    return pl.pallas_call(
        joint_update_kernel,
        grid_spec=pltpu.PrefetchScalarGridSpec(
            num_scalar_prefetch=1, grid=(2,), in_specs=[whole] * 4 + blocks, out_specs=blocks
        ),
        out_shape=[jax.ShapeDtypeStruct(array.shape, array.dtype) for array in (*query, *pair)],
        compiler_params=pltpu.CompilerParams(vmem_limit_bytes=VMEM_LIMIT),
        cost_estimate=pl.CostEstimate(
            flops=20 * (query[0].size + pair[0].size),
            bytes_accessed=24 * (query[0].size + pair[0].size),
            transcendentals=0,
        ),
        name="joint_update",
    )(meta, *grads, *query, *pair)


def turned_update_kernel(rate, swapped, meta_ref, *refs):
    grad_refs, weight_refs = (refs[:4], refs[4:10])
    at = pl.program_id(1)
    width = grad_refs[0].shape[1]
    every = slice(None)
    for j, start in enumerate(range(0, width, LANES)):
        strip = slice(start, min(start + LANES, width))
        gradient = chosen(meta_ref, grad_refs, at, every, strip).T
        if swapped:
            gradient = jnp.concatenate([gradient[HEAD_DIM:], gradient[:HEAD_DIM]], axis=0)
            index = (j, 0)
        else:
            index = (strip, every)
        update(weight_refs, index, gradient, rate)


def turned_update(meta, grads, weights, rate, swapped):
    shape = weights[0].shape
    half, width = (shape[1] // 2, grads[0].shape[1])
    if swapped:
        weights = [w.reshape(width // LANES, 2, LANES, shape[1]) for w in weights]
        block = pl.BlockSpec(
            (width // LANES, 1, LANES, half), lambda i, at, m: (0, at, 0, (m[1] + i) % 2)
        )
    else:
        block = pl.BlockSpec((width, half), lambda i, at, m: (at, (m[1] + i) % 2))
    outs = pl.pallas_call(
        functools.partial(turned_update_kernel, rate, swapped),
        grid_spec=pltpu.PrefetchScalarGridSpec(
            num_scalar_prefetch=1,
            grid=(2, 2),
            in_specs=[pl.BlockSpec((half, width), lambda i, at, m: (0, 0))] * 4 + [block] * 3,
            out_specs=[block] * 3,
        ),
        out_shape=[jax.ShapeDtypeStruct(weights[0].shape, jnp.float32)] * 3,
        compiler_params=pltpu.CompilerParams(vmem_limit_bytes=VMEM_LIMIT),
        cost_estimate=pl.CostEstimate(
            flops=20 * weights[0].size, bytes_accessed=24 * weights[0].size, transcendentals=0
        ),
        name="turned_update",
    )(meta, *grads, *weights)
    return [out.reshape(shape) for out in outs]


def gateup_update_kernel(meta_ref, *refs):
    gate_refs, up_refs, weight_refs = (refs[:4], refs[4:8], refs[8:14])
    every = slice(None)
    gate, up = [
        jnp.concatenate([chosen(meta_ref, grads, at, every, every) for at in range(2)], axis=1)
        for grads in (gate_refs, up_refs)
    ]
    update(weight_refs, every, jnp.stack([gate, up], axis=1), D ** (-0.5))


def gateup_update(meta, shards, weights, rows):
    half, width = (shards[0].shape[0] // 3, shards[0].shape[1])
    shape = weights[0].shape
    tiles = half // rows
    gate = pl.BlockSpec((rows, width), lambda i, j, m: (tiles + j, 0))
    up = pl.BlockSpec((rows, width), lambda i, j, m: (2 * tiles + j, 0))
    block = pl.BlockSpec(
        (rows, 2, shape[2]), lambda i, j, m: (((m[1] + i) % 2) * tiles + j, 0, 0)
    )
    return pl.pallas_call(
        gateup_update_kernel,
        grid_spec=pltpu.PrefetchScalarGridSpec(
            num_scalar_prefetch=1,
            grid=(2, tiles),
            in_specs=[gate] * 4 + [up] * 4 + [block] * 3,
            out_specs=[block] * 3,
        ),
        out_shape=[jax.ShapeDtypeStruct(shape, jnp.float32)] * 3,
        compiler_params=pltpu.CompilerParams(vmem_limit_bytes=VMEM_LIMIT),
        cost_estimate=pl.CostEstimate(
            flops=20 * weights[0].size, bytes_accessed=28 * weights[0].size, transcendentals=0
        ),
        name="gateup_update",
    )(meta, *shards, *shards, *weights)


def on_device(
    sizes,
    block_input,
    cotangent,
    segments,
    norm_gains,
    w_query,
    w_keyvalue,
    w_output,
    w_gateup,
    w_down,
    gains_moment,
    gains_square,
    query_moment,
    query_square,
    keyvalue_moment,
    keyvalue_square,
    output_moment,
    output_square,
    gateup_moment,
    gateup_square,
    down_moment,
    down_square,
):
    rows_on, lines = sizes
    y, core, row, line = [lax.axis_index(name) for name in ("y", "core", "row", "col")]
    length = segments.shape[1]
    block = block_input.shape[0] // lines
    wide = block_input.shape[1]
    half = wide // 2
    slots = 2 * rows_on
    per_row = w_query.shape[1] // (KV_HEADS * HEAD_DIM)
    query_width = per_row * LANES
    hidden_here = w_gateup.shape[2] // 2

    def shift(value, axis, size, by):
        return lax.ppermute(value, axis, [(i, (i + by) % size) for i in range(size)])

    def other_core(value):
        return lax.ppermute(value, "core", [(0, 1), (1, 0)])

    def other_y(value):
        return lax.ppermute(value, "y", [(0, 1), (1, 0)])

    def place_of(y_at, core_at, row_at):
        return (y_at * 2 + core_at) * rows_on + row_at

    first_pairs, second_pairs = ([], [])
    for y_at in range(2):
        for core_at in range(2):
            for row_at in range(rows_on):
                over_row = (
                    place_of(y_at, core_at, row_at),
                    place_of(y_at, core_at, (row_at + 1) % rows_on),
                )
                over_y = (place_of(y_at, core_at, row_at), place_of(1 - y_at, core_at, row_at))
                first_pairs.append(over_row if core_at == 0 else over_y)
                second_pairs.append(over_y if core_at == 0 else over_row)
    near = ("y", "core", "row")

    def gather_tokens(own):
        if rows_on == 2:
            first = lax.ppermute(own, near, first_pairs)
            second = lax.ppermute(own, near, second_pairs)
            first, second = lax.optimization_barrier((first, second))
            third = lax.ppermute(first, near, second_pairs)
            return [own, first, second, third]
        parts = [own] + [shift(own, "row", rows_on, by) for by in range(1, rows_on)]
        return parts + [other_y(part) for part in parts]

    def reduce_tokens(
        rows_of, after_close=None, after_first=None, before_last=None, far_here=None, ready=None
    ):
        def same(value):
            return value

        after_close, after_first, before_last = [f or same for f in (after_close, after_first, before_last)]
        if rows_on == 2:
            far = rows_of(2, 4)
            if ready:
                far, close = ready((far, rows_of(0, 2)))
            third = lax.ppermute(far[block:], near, second_pairs)
            second = lax.ppermute(far[:block], near, second_pairs)
            if not ready:
                close = after_close(rows_of(0, 2))
            third, second = (far_here or lax.optimization_barrier)((third, second))
            key = (close[block:].astype(jnp.float32) + third.astype(jnp.float32)).astype(jnp.bfloat16)
            first = before_last(lax.ppermute(after_first(key), near, first_pairs))
            own = close[:block].astype(jnp.float32) + second.astype(jnp.float32)
            return own + first.astype(jnp.float32)
        partial = after_close(rows_of(0, slots))
        parts = [partial[i * block : (i + 1) * block] for i in range(slots)]
        sums = [
            parts[i].astype(jnp.float32) + other_y(parts[rows_on + i]).astype(jnp.float32)
            for i in range(rows_on)
        ]
        sums[0] = after_first(sums[0])
        total = sums[0]
        for by in range(1, rows_on):
            moved = shift(sums[by].astype(jnp.bfloat16), "row", rows_on, -by)
            total = total + moved.astype(jnp.float32)
        return before_last(total)

    def product(left, right):
        def rows_of(first, last):
            return dot_nt(left[first * block : last * block], right).astype(jnp.bfloat16)

        return rows_of

    if rows_on == 2:
        slot_y = [y, jnp.where(core == 0, y, 1 - y), jnp.where(core == 0, 1 - y, y), 1 - y]
        slot_row = [row, jnp.where(core == 0, 1 - row, row), jnp.where(core == 0, row, 1 - row), 1 - row]
    else:
        slot_y = [y] * rows_on + [1 - y] * rows_on
        slot_row = [(row - by) % rows_on for by in range(rows_on)] * 2

    def pick(parts, index):
        return lax.dynamic_index_in_dim(jnp.stack(parts), index, 0, keepdims=False)

    def tokens_sent(values):
        parts = []
        for by in range(lines):
            part = lax.dynamic_slice_in_dim(values, ((line + by) % lines) * block, block, 0)
            parts.append(part if by == 0 else shift(part, "col", lines, by))
        return parts

    def tokens_of(parts):
        blocks = [pick(parts, (line - at) % lines) for at in range(lines)]
        return jnp.concatenate([b[:, :half] for b in blocks] + [b[:, half:] for b in blocks], axis=1)

    def features_sent(values):
        blocks = [
            jnp.concatenate(
                [
                    values[:, at * half : (at + 1) * half],
                    values[:, D // 2 + at * half : D // 2 + (at + 1) * half],
                ],
                axis=1,
            )
            for at in range(lines)
        ]
        parts = []
        for by in range(lines):
            part = pick(blocks, (line + by) % lines)
            parts.append(part if by == 0 else shift(part, "col", lines, by))
        return parts

    def features_of(parts):
        return jnp.concatenate([pick(parts, (line - at) % lines) for at in range(lines)], axis=0)

    def half_rows(values):
        return lax.dynamic_slice_in_dim(values, core * half, half, 0)

    def half_columns(values):
        return lax.dynamic_slice_in_dim(values, core * half, half, 1)

    def gather_weight(piece):
        return lax.all_gather(piece, ("core", "col"), axis=0, tiled=True)

    query_rows = half_rows(w_query).astype(jnp.bfloat16)
    pair_rows = half_rows(w_keyvalue).astype(jnp.bfloat16)

    def joint_of(at):
        pieces = [
            query_rows[:, (2 * j + at) * LANES : (2 * j + at + 1) * LANES] for j in range(per_row)
        ]
        pair = pair_rows[:, at * 2 * LANES : (at + 1) * 2 * LANES]
        pieces += [
            pair[:, :LANES],
            pair[:, LANES + HEAD_DIM :],
            pair[:, LANES : LANES + HEAD_DIM],
        ]
        return jnp.concatenate(pieces, axis=1)

    joint_mine = jnp.where(y == 0, joint_of(0), joint_of(1))
    output_columns = half_columns(w_output).astype(jnp.bfloat16)

    def output_of(at):
        pieces = []
        for j in range(per_row):
            base = (2 * j + at) * LANES
            pieces += [
                output_columns[base + HEAD_DIM : base + LANES],
                output_columns[base : base + HEAD_DIM],
            ]
        return jnp.concatenate(pieces, axis=0)

    output_mine = jnp.where(y == 0, output_of(0), output_of(1)).T
    gateup_mine = lax.dynamic_slice(
        w_gateup, (core * half, 0, y * hidden_here), (half, 2, hidden_here)
    ).astype(jnp.bfloat16)
    gateup_mine = jnp.concatenate([gateup_mine[:, 0], gateup_mine[:, 1]], axis=1)
    down_mine = lax.dynamic_slice(
        w_down, (y * hidden_here, core * half), (hidden_here, half)
    ).astype(jnp.bfloat16).T

    gain_parts = [norm_gains] + [shift(norm_gains, "col", lines, by) for by in range(1, lines)]
    gain_blocks = [pick(gain_parts, (line - at) % lines) for at in range(lines)]
    gains = jnp.concatenate(
        [b[:, :half] for b in gain_blocks] + [b[:, half:] for b in gain_blocks], axis=1
    )

    own_starts = document_starts(segments[0])
    other_starts = document_starts(other_y(segments)[0])
    frequency = 10000.0 ** (-2.0 * jnp.arange(HEAD_DIM // 2, dtype=jnp.float32) / HEAD_DIM)
    starts, places, meta = ([], [], [])
    for slot in range(slots):
        begin = slot_row[slot] * (lines * block) + line * block
        of_chunk = lax.dynamic_slice_in_dim(
            jnp.where(slot_y[slot] == y, own_starts, other_starts), begin, block, 0
        )
        starts.append(of_chunk)
        places.append(begin + jnp.arange(block, dtype=jnp.int32))
        meta += [of_chunk[0] // block, begin // block]
        for row_at in range(rows_on):
            found = jnp.int32(0)
            for other in range(slots):
                same = (slot_y[other] == slot_y[slot]) & (slot_row[other] == row_at)
                found = found + jnp.where(same, other, 0)
            meta.append(found)
    meta = jnp.stack([jnp.asarray(m, jnp.int32) for m in meta + [line]])
    starts, places = (jnp.stack(starts), jnp.stack(places))
    info = jnp.stack([places, starts], axis=1)
    offsets = (places - starts).astype(jnp.float32).reshape(-1)
    phases = offsets[:, None] * jnp.tile(frequency, LANES // (HEAD_DIM // 2))[None, :]
    cosine, sine = (jnp.cos(phases), jnp.sin(phases))

    residual_low = tokens_of(tokens_sent(block_input))
    residual_low, late_cotangent, joint_mine, output_mine = lax.optimization_barrier(
        (residual_low, cotangent, joint_mine, output_mine)
    )
    cot_parts = tokens_sent(late_cotangent)
    first_weight = gather_weight(jnp.concatenate([joint_mine, output_mine], axis=1))
    joint_width = joint_mine.shape[1]
    joint_weight, output_weight = (first_weight[:, :joint_width], first_weight[:, joint_width:])
    residual = residual_low.astype(jnp.float32)
    scale_one = lax.rsqrt(jnp.mean(residual * residual, axis=1, keepdims=True) + EPSILON)
    normed_parts = gather_tokens((residual * scale_one * gains[0]).astype(jnp.bfloat16))
    normed_parts, cot_parts = lax.optimization_barrier((normed_parts, cot_parts))
    cot_low = tokens_of(cot_parts)
    cot_chunks = gather_tokens(cot_low)
    queries, pair = project(normed_parts, first_weight, joint_width, cosine, sine, query_width)
    pairs = lax.all_gather(pair.reshape(slots, block, 2 * LANES), "col", axis=0, tiled=False)
    pairs, cot_chunks, gateup_mine, down_mine = lax.optimization_barrier(
        (pairs, cot_chunks, gateup_mine, down_mine)
    )
    gateup_weight = gather_weight(gateup_mine)
    down_weight = gather_weight(down_mine)
    mixed, logs = attend(meta, queries, pairs, info, rows_on)
    attn_sum = reduce_tokens(product(mixed, output_weight))
    middle = residual + attn_sum
    scale_two = lax.rsqrt(jnp.mean(middle * middle, axis=1, keepdims=True) + EPSILON)
    two_parts = gather_tokens((middle * scale_two * gains[1]).astype(jnp.bfloat16))
    hidden, factor, silu_gate = widen(two_parts, gateup_weight)
    normed_two, cot = (jnp.concatenate(two_parts, axis=0), jnp.concatenate(cot_chunks, axis=0))

    def other_half(rows, grad):
        rows = lax.dynamic_slice_in_dim(rows, (1 - core) * (D // 2), D // 2, 1)
        return other_core(dot_tn(rows, grad).astype(jnp.bfloat16))

    def own_half(rows, grad, received):
        rows = lax.dynamic_slice_in_dim(rows, core * (D // 2), D // 2, 1)
        total = dot_tn(rows, grad) + received.astype(jnp.float32)
        return total.astype(jnp.bfloat16)

    def scatter(total):
        return lax.psum_scatter(total, "col", scatter_dimension=0, tiled=True)

    def collect(piece):
        near_y = other_y(piece)
        return [piece, near_y, other_core(piece), other_core(near_y)]

    down_total = own_half(cot, hidden, other_half(cot, hidden))
    down_total, down_weight = lax.optimization_barrier((down_total, down_weight))
    down_piece = scatter(down_total)
    work = {}

    def feed_back(first, last):
        work["grad_gate"], work["grad_up"], partial = widen_back(
            cot_chunks[first:last],
            down_weight,
            gateup_weight,
            factor,
            silu_gate,
            first,
            [work[name] for name in ("grad_gate", "grad_up") if name in work],
        )
        return partial

    def feed_others(close):
        close, rows, gate, up = lax.optimization_barrier(
            (close, normed_two, work["grad_gate"], work["grad_up"])
        )
        work["feed"] = (rows, gate, up, other_half(rows, gate), other_half(rows, up))
        return close

    def feed_owns(key):
        key, rows, gate, up, gate_other, up_other = lax.optimization_barrier((key, *work["feed"]))
        work["totals"] = (own_half(rows, gate, gate_other), own_half(rows, up, up_other))
        return key

    def feed_ends(first):
        first, work["down_piece"] = lax.optimization_barrier((first, down_piece))
        return first

    grad_normed_two = reduce_tokens(feed_back, feed_others, feed_owns, feed_ends)
    gate_piece, up_piece = [scatter(total) for total in work["totals"]]

    def norm_back(values, scale, grad_normed, gain):
        scaled = grad_normed * gain
        total = jnp.sum(scaled * values, axis=1, keepdims=True)
        return scale * scaled - values * (scale**3 * total / D)

    grad_middle = cot_low.astype(jnp.float32) + norm_back(
        middle, scale_two, grad_normed_two, gains[1]
    )
    gain_two = jnp.sum(grad_normed_two * middle * scale_two, axis=0)

    grad_middle_low, late_hidden = lax.optimization_barrier(
        (grad_middle.astype(jnp.bfloat16), hidden)
    )
    back = jnp.concatenate(gather_tokens(grad_middle_low), axis=0)

    def back_here(products):
        products, work["back"] = lax.optimization_barrier((products, back))
        return products

    def attention_back(far):
        here = work.get("back", back)
        grad_query, grad_parts = attend_back(
            meta,
            queries,
            pairs,
            dot_nn(here, output_weight).astype(jnp.bfloat16),
            mixed,
            logs,
            info,
            cosine,
            sine,
            rows_on,
        )
        work["grad_parts"] = [grad_parts[0]] + [
            shift(grad_parts[by], "col", lines, -by) for by in range(1, lines)
        ]
        names = ("grad_query", "gate_piece", "back", "mixed")
        far, *values = lax.optimization_barrier((far, grad_query, gate_piece, here, mixed))
        work.update(zip(names, values))
        return far

    def keys_arrive(first):
        first, work["grad_parts"] = lax.optimization_barrier((first, work["grad_parts"]))
        return first

    if rows_on == 2:
        ffn_sum = reduce_tokens(
            product(late_hidden, down_weight), None, None, keys_arrive, attention_back, back_here
        )
    else:
        ffn_sum = attention_back(reduce_tokens(product(late_hidden, down_weight)))
    grad_query, gate_piece, back, mixed = [
        work[name] for name in ("grad_query", "gate_piece", "back", "mixed")
    ]
    output_total = own_half(back, mixed, other_half(back, mixed))
    layer_output = features_of(features_sent((middle + ffn_sum).astype(jnp.bfloat16)))
    grad_keyvalue = pair_back(work["grad_parts"], cosine, sine, block)
    grad_joint = jnp.concatenate([grad_query, grad_keyvalue], axis=1)
    normed_one = jnp.concatenate(normed_parts, axis=0)
    def joint_others(close):
        close, up_done, work["output"], rows, grad = lax.optimization_barrier(
            (close, up_piece, output_total, normed_one, grad_joint)
        )
        work["feed_shards"] = collect(
            jnp.concatenate([work["down_piece"], gate_piece, up_done], axis=0)
        )
        work["joint"] = (rows, grad, other_half(rows, grad))
        return close

    def joint_owns(key):
        key, rows, grad, other = lax.optimization_barrier((key, *work["joint"]))
        work["joint_total"] = own_half(rows, grad, other)
        return key

    grad_normed_one = reduce_tokens(product(grad_joint, joint_weight), joint_others, joint_owns)
    joint_piece, output_piece = (scatter(work["joint_total"]), scatter(work["output"]))
    meta_core = jnp.stack([y, core]).astype(jnp.int32)
    gateup_new = gateup_update(
        meta_core, work["feed_shards"], [w_gateup, gateup_moment, gateup_square], 32
    )
    down_new = turned_update(
        meta_core,
        work["feed_shards"],
        [w_down, down_moment, down_square],
        FF ** (-0.5),
        False,
    )
    input_grad = grad_middle + norm_back(residual, scale_one, grad_normed_one, gains[0])
    gain_one = jnp.sum(grad_normed_one * residual * scale_one, axis=0)
    input_grad, layer_output = lax.optimization_barrier(
        (input_grad.astype(jnp.bfloat16), layer_output)
    )
    input_parts, gateup_new, down_new = lax.optimization_barrier(
        (features_sent(input_grad), gateup_new, down_new)
    )
    input_grad = features_of(input_parts).astype(jnp.float32)
    pair_piece = joint_piece[:, query_width:]
    pair_total = pair_piece.astype(jnp.float32)
    for by in range(1, rows_on):
        pair_total = pair_total + shift(pair_piece, "row", rows_on, by).astype(jnp.float32)
    joint_piece = jnp.concatenate(
        [joint_piece[:, :query_width], pair_total.astype(jnp.bfloat16)], axis=1
    )
    joint_new = joint_update(
        meta_core,
        collect(joint_piece),
        [w_query, query_moment, query_square],
        [w_keyvalue, keyvalue_moment, keyvalue_square],
    )
    output_new = turned_update(
        meta_core,
        collect(output_piece),
        [w_output, output_moment, output_square],
        (HEADS * HEAD_DIM // 64) ** (-0.5),
        True,
    )

    gain_sums = jnp.stack([gain_one, gain_two])
    blocks = [
        jnp.concatenate(
            [
                gain_sums[:, at * half : (at + 1) * half],
                gain_sums[:, D // 2 + at * half : D // 2 + (at + 1) * half],
            ],
            axis=1,
        )
        for at in range(lines)
    ]
    grad_gains = pick(blocks, line)
    for by in range(1, lines):
        grad_gains = grad_gains + shift(pick(blocks, (line + by) % lines), "col", lines, by)
    for axis, size in (("core", 2), ("y", 2), ("row", rows_on)):
        blocks_total = grad_gains
        for by in range(1, size):
            grad_gains = grad_gains + shift(blocks_total, axis, size, by)

    gains_new = adamw_step(norm_gains, grad_gains, gains_moment, gains_square, 0.6, 0.0)
    return (
        layer_output,
        input_grad,
        *gains_new,
        *joint_new,
        *output_new,
        *gateup_new,
        *down_new,
    )


def solution(mesh):
    dp, rows_on, lines = (mesh.shape["dp"], mesh.shape["row"], mesh.shape["col"])
    split = Mesh(mesh.devices.reshape(dp // 2, 2, rows_on, lines), ("y", "core", "row", "col"))
    tokens = P(("y", "core", "row"), "col")
    narrow, wide = (P("col", "row"), P("row", "col"))
    gains, pair, gateup = (P(None, "col"), P("col", None), P("col", None, "row"))
    return jax.shard_map(
        functools.partial(on_device, (rows_on, lines)),
        mesh=split,
        in_specs=(
            tokens,
            tokens,
            P(("y", "core"), None),
            gains,
            narrow,
            pair,
            wide,
            gateup,
            wide,
            gains,
            gains,
            narrow,
            narrow,
            pair,
            pair,
            wide,
            wide,
            gateup,
            gateup,
            wide,
            wide,
        ),
        out_specs=(tokens, tokens)
        + (gains,) * 3
        + (narrow,) * 3
        + (pair,) * 3
        + (wide,) * 3
        + (gateup,) * 3
        + (wide,) * 3,
        check_vma=False,
    )
```

profile of v0, /device:TPU:11, one launch (start us, length us, event | category | flops | bytes accessed | tf_op | source)
XLA Modules:
  0.0 791.1 jit_solution(13075436675362144252)
XLA Ops:
  45.4 19.2 %collective-permute-done.12 = s32[1,2048]{1,0:T(1,128)S(1)} collective-permute-done((s32[1,2048]{1,0:T(1,128)S(1)}, s32[1,2048]{1,0:T(1,128)S(1)}, u32[]{:S(2)}, u32[]{:S(2)}) %collective-permute-start.12) | collective-permute-done | bytes 8224 | tf_op jit(solution)/shard_map/ppermute | solution.py:627
  75.9 12.0 %collective-permute-done.9 = bf16[256,512]{1,0:T(8,128)(2,1)S(1)} collective-permute-done((bf16[256,512]{1,0:T(8,128)(2,1)S(1)}, bf16[256,512]{1,0:T(8,128)(2,1)S(1)}, u32[]{:S(2)}, u32[]{:S(2)}) %collective-permute-start.9) | collective-permute-done | bytes 262176 | tf_op jit(solution)/shard_map/ppermute | solution.py:621
  87.9 23.0 %collective-permute-done.10 = bf16[256,512]{1,0:T(8,128)(2,1)S(1)} collective-permute-done((bf16[256,512]{1,0:T(8,128)(2,1)S(1)}, bf16[256,512]{1,0:T(8,128)(2,1)S(1)}, u32[]{:S(2)}, u32[]{:S(2)}) %collective-permute-start.10) | collective-permute-done | bytes 262176 | tf_op jit(solution)/shard_map/ppermute | solution.py:621
  131.7 21.9 %collective-permute-done.13.refs_1_ = bf16[256,2048]{1,0:T(8,128)(2,1)S(1)} collective-permute-done((bf16[256,2048]{1,0:T(8,128)(2,1)S(1)}, bf16[256,2048]{1,0:T(8,128)(2,1)S(1)}, u32[]{:S(2)}, u32[]{:S(2)}) %collective-permute-start.13) | collective-permute-done | bytes 1048608 | tf_op jit(solution)/shard_map/ppermute | solution.py:647
  186.5 19.6 %attend.1 = (bf16[1024,512]{1,0:T(8,128)(2,1)S(1)}, f32[4,2,1024]{2,1,0:T(2,128)S(1)}) custom-call(s32[17]{0:T(128)S(1)} %stack.176.meta_ref, bf16[1024,512]{1,0:T(8,128)(2,1)S(1)} %copy-done.40, bf16[4,4,256,256]{3,2,1,0:T(8,128)(2,1)S(1)} %copy-done.32, s32[4,2,256]{2,1,0:T(2,128)S(1)} %pad_add_fusion.2.info_ref.refs_4_), custom_call_target="tpu_custom_call" | custom-call | flops 3221225472 | bytes 4194304 | tf_op jit(solution)/shard_map/attend/pallas_call | solution.py:274
  215.6 9.6 %collective-permute-done.16 = bf16[256,2048]{1,0:T(8,128)(2,1)} collective-permute-done((bf16[256,2048]{1,0:T(8,128)(2,1)}, bf16[256,2048]{1,0:T(8,128)(2,1)}, u32[]{:S(2)}, u32[]{:S(2)}) %collective-permute-start.16) | collective-permute-done | bytes 1048608 | tf_op jit(solution)/shard_map/ppermute | solution.py:666
  225.2 11.4 %collective-permute-done.17 = bf16[256,2048]{1,0:T(8,128)(2,1)} collective-permute-done((bf16[256,2048]{1,0:T(8,128)(2,1)}, bf16[256,2048]{1,0:T(8,128)(2,1)}, u32[]{:S(2)}, u32[]{:S(2)}) %collective-permute-start.17) | collective-permute-done | bytes 1048608 | tf_op jit(solution)/shard_map/ppermute | solution.py:667
  239.5 12.9 %collective-permute-done.18 = bf16[256,2048]{1,0:T(8,128)(2,1)S(1)} collective-permute-done((bf16[256,2048]{1,0:T(8,128)(2,1)S(1)}, bf16[256,2048]{1,0:T(8,128)(2,1)S(1)}, u32[]{:S(2)}, u32[]{:S(2)}) %collective-permute-start.18) | collective-permute-done | bytes 1048608 | tf_op jit(solution)/shard_map/ppermute | solution.py:672
  256.1 20.5 %collective-permute-done.19.refs_1_ = bf16[256,2048]{1,0:T(8,128)(2,1)} collective-permute-done((bf16[256,2048]{1,0:T(8,128)(2,1)S(1)}, bf16[256,2048]{1,0:T(8,128)(2,1)}, u32[]{:S(2)}, u32[]{:S(2)}) %collective-permute-start.19) | collective-permute-done | bytes 1048608 | tf_op jit(solution)/shard_map/ppermute | solution.py:647
  291.5 19.9 %widen.1 = (bf16[1024,1408]{1,0:T(8,128)(2,1)}, bf16[1024,1408]{1,0:T(8,128)(2,1)}, bf16[1024,1408]{1,0:T(8,128)(2,1)}) custom-call(bf16[256,2048]{1,0:T(8,128)(2,1)S(1)} %multiply_convert_fusion.refs_0_, bf16[256,2048]{1,0:T(8,128)(2,1)} %collective-permute-done.19.refs_1_, bf16[256,2048]{1,0:T(8,128)(2,1)S(1)} %copy-done.27, ...), custom_call_target="tpu_custom_call" | custom-call | flops 11811160064 | bytes 24379392 | tf_op jit(solution)/shard_map/widen/pallas_call | solution.py:141
  349.3 17.1 %widen_back.2 = (bf16[1024,1408]{1,0:T(8,128)(2,1)}, bf16[1024,1408]{1,0:T(8,128)(2,1)}, bf16[512,2048]{1,0:T(8,128)(2,1)S(1)}) custom-call(bf16[256,2048]{1,0:T(8,128)(2,1)S(1)} %copy-done.17, bf16[256,2048]{1,0:T(8,128)(2,1)} %collective-permute-done.15.refs_1_, bf16[2048,1408]{1,0:T(8,128)(2,1)} %all-gather.11.cloned.1.call-done.refs_2_, ...), custom_call_target="tpu_custom_call" | custom-call | flops 8858370048 | bytes 23068672 | tf_op jit(solution)/shard_map/widen_back/pallas_call | solution.py:179
  366.3 16.6 %widen_back.3 = (bf16[1024,1408]{1,0:T(8,128)(2,1)}, bf16[1024,1408]{1,0:T(8,128)(2,1)}, bf16[512,2048]{1,0:T(8,128)(2,1)S(1)}) custom-call(bf16[256,2048]{1,0:T(8,128)(2,1)S(1)} %slice_dynamic-update-slice_fusion.refs_0_, bf16[256,2048]{1,0:T(8,128)(2,1)S(1)} %copy-done.14, ...), custom_call_target="tpu_custom_call", output_to_operand_aliasing={{0}: (6, {}), {1}: (7, {})} | custom-call | flops 8858370048 | bytes 23068672 | tf_op jit(solution)/shard_map/widen_back/pallas_call | solution.py:179
  394.9 12.5 %collective-permute-done.23 = bf16[256,2048]{1,0:T(8,128)(2,1)S(1)} collective-permute-done((bf16[256,2048]{1,0:T(8,128)(2,1)S(1)}, bf16[256,2048]{1,0:T(8,128)(2,1)S(1)}, u32[]{:S(2)}, u32[]{:S(2)}) %collective-permute-start.23) | collective-permute-done | bytes 1048608 | tf_op jit(solution)/shard_map/ppermute | solution.py:666
  407.3 11.3 %collective-permute-done.24 = bf16[256,2048]{1,0:T(8,128)(2,1)} collective-permute-done((bf16[256,2048]{1,0:T(8,128)(2,1)S(1)}, bf16[256,2048]{1,0:T(8,128)(2,1)}, u32[]{:S(2)}, u32[]{:S(2)}) %collective-permute-start.24) | collective-permute-done | bytes 1048608 | tf_op jit(solution)/shard_map/ppermute | solution.py:667
  426.5 13.1 %collective-permute-done.27 = bf16[256,2048]{1,0:T(8,128)(2,1)} collective-permute-done((bf16[256,2048]{1,0:T(8,128)(2,1)}, bf16[256,2048]{1,0:T(8,128)(2,1)}, u32[]{:S(2)}, u32[]{:S(2)}) %collective-permute-start.27) | collective-permute-done | bytes 1048608 | tf_op jit(solution)/shard_map/ppermute | solution.py:672
  457.1 12.5 %collective-permute-done.28 = bf16[256,2048]{1,0:T(8,128)(2,1)S(1)} collective-permute-done((bf16[256,2048]{1,0:T(8,128)(2,1)}, bf16[256,2048]{1,0:T(8,128)(2,1)S(1)}, u32[]{:S(2)}, u32[]{:S(2)}) %collective-permute-start.28) | collective-permute-done | bytes 1048608 | tf_op jit(solution)/shard_map/ppermute | solution.py:647
  497.4 31.7 %attend_back.1 = (bf16[1024,512]{1,0:T(8,128)(2,1)S(1)}, bf16[4,256,256]{2,1,0:T(8,128)(2,1)S(1)}, bf16[4,256,256]{2,1,0:T(8,128)(2,1)S(1)}, bf16[4,256,256]{2,1,0:T(8,128)(2,1)S(1)}, bf16[4,256,256]{2,1,0:T(8,128)(2,1)S(1)}) custom-call(s32[17]{0:T(128)S(1)} %stack.176.meta_ref, bf16[1024,512]{1,0:T(8,128)(2,1)S(1)} %copy-done.41, ...), custom_call_target="tpu_custom_call" | custom-call | flops 8053063680 | bytes 8388608 | tf_op jit(solution)/shard_map/attend_back/pallas_call | solution.py:378
  555.4 16.7 %collective-permute-done.35.refs_2_ = bf16[1024,256]{1,0:T(8,128)(2,1)S(1)} collective-permute-done((bf16[1024,256]{1,0:T(8,128)(2,1)S(1)}, bf16[1024,256]{1,0:T(8,128)(2,1)S(1)}, u32[]{:S(2)}, u32[]{:S(2)}) %collective-permute-start.35) | collective-permute-done | bytes 524320 | tf_op jit(solution)/shard_map/ppermute | solution.py:621
  572.1 11.2 %collective-permute-done.36.refs_3_ = bf16[1024,256]{1,0:T(8,128)(2,1)S(1)} collective-permute-done((bf16[1024,256]{1,0:T(8,128)(2,1)S(1)}, bf16[1024,256]{1,0:T(8,128)(2,1)S(1)}, u32[]{:S(2)}, u32[]{:S(2)}) %collective-permute-start.36) | collective-permute-done | bytes 524320 | tf_op jit(solution)/shard_map/ppermute | solution.py:621
  623.6 9.7 %collective-permute-done.44 = bf16[256,512]{1,0:T(8,128)(2,1)S(1)} collective-permute-done((bf16[256,512]{1,0:T(8,128)(2,1)S(1)}, bf16[256,512]{1,0:T(8,128)(2,1)S(1)}, u32[]{:S(2)}, u32[]{:S(2)}) %collective-permute-start.44) | collective-permute-done | bytes 262176 | tf_op jit(solution)/shard_map/ppermute | solution.py:621
  634.6 13.4 %collective-permute-done.43 = bf16[256,512]{1,0:T(8,128)(2,1)} collective-permute-done((bf16[256,512]{1,0:T(8,128)(2,1)S(1)}, bf16[256,512]{1,0:T(8,128)(2,1)}, u32[]{:S(2)}, u32[]{:S(2)}) %collective-permute-start.43) | collective-permute-done | bytes 262176 | tf_op jit(solution)/shard_map/ppermute | solution.py:621
  648.0 10.0 %collective-permute-done.42 = bf16[256,512]{1,0:T(8,128)(2,1)} collective-permute-done((bf16[256,512]{1,0:T(8,128)(2,1)S(1)}, bf16[256,512]{1,0:T(8,128)(2,1)}, u32[]{:S(2)}, u32[]{:S(2)}) %collective-permute-start.42) | collective-permute-done | bytes 262176 | tf_op jit(solution)/shard_map/ppermute | solution.py:621
  717.2 15.2 %turned_update.2 = (f32[2816,512]{1,0:T(8,128)}, f32[2816,512]{1,0:T(8,128)}, f32[2816,512]{1,0:T(8,128)}) custom-call(s32[2]{0:T(128)S(1)} %pad_add_fusion.5.meta_ref, bf16[768,1408]{1,0:T(8,128)(2,1)S(1)} %constant_dynamic-update-slice_fusion.12.refs_0_.refs_4_, bf16[768,1408]{1,0:T(8,128)(2,1)} %collective-permute-done.48.refs_1_.refs_5_, ...), custom_call_target="tpu_custom_call" | custom-call | flops 28835840 | bytes 34603008 | tf_op jit(solution)/shard_map/turned_update/pallas_call | solution.py:531
  732.4 36.5 %gateup_update.1 = (f32[512,2,2816]{2,1,0:T(2,128)}, f32[512,2,2816]{2,1,0:T(2,128)}, f32[512,2,2816]{2,1,0:T(2,128)}) custom-call(s32[2]{0:T(128)S(1)} %pad_add_fusion.5.meta_ref, bf16[768,1408]{1,0:T(8,128)(2,1)S(1)} %constant_dynamic-update-slice_fusion.12.refs_0_.refs_4_, bf16[768,1408]{1,0:T(8,128)(2,1)} %collective-permute-done.48.refs_1_.refs_5_, ...), custom_call_target="tpu_custom_call" | custom-call | flops 57671680 | bytes 80740352 | tf_op jit(solution)/shard_map/gateup_update/pallas_call | solution.py:568
  (497 shorter events, 366.8 us)
Async XLA Ops:
  7.2 108.3 %all-gather.5.cloned.1.call-start = ((), (), s32[]{:S(2)}) async-start(), calls=%async_computation.5 | async-start | bytes 5898240 | tf_op jit(solution)/shard_map/all_gather | solution.py:742
  35.7 135.5 %all-gather.7.cloned.1.call-start = ((), (), s32[]{:S(2)}) async-start(), calls=%async_computation.6 | async-start | bytes 2621440 | tf_op jit(solution)/shard_map/all_gather | solution.py:827
  68.5 44.9 %collective-permute-start.8 = (bf16[256,2048]{1,0:T(8,128)(2,1)S(1)}, bf16[256,2048]{1,0:T(8,128)(2,1)S(1)}, u32[]{:S(2)}, u32[]{:S(2)}) collective-permute-start(bf16[256,2048]{1,0:T(8,128)(2,1)S(1)} %collective-permute-done.6.refs_1_), channel_id=1, source_target_pairs={{0,16},{4,20},{8,12},{12,8},{16,0},{20,4},{24,28},{28,24},{1,17},{... | collective-permute-start | bytes 3145736 | tf_op jit(solution)/shard_map/ppermute | solution.py:650
  70.4 40.5 %collective-permute-start.10 = (bf16[256,512]{1,0:T(8,128)(2,1)S(1)}, bf16[256,512]{1,0:T(8,128)(2,1)S(1)}, u32[]{:S(2)}, u32[]{:S(2)}) collective-permute-start(bf16[256,512]{1,0:T(8,128)(2,1)S(1)} %get-tuple-element.312), channel_id=1, source_target_pairs={{0,2},{1,3},{2,0},{3,1},{4,6},{5,7},{6,4},{7,5},{8,10},{9,11},{10,... | collective-permute-start | bytes 786440 | tf_op jit(solution)/shard_map/ppermute | solution.py:621
  127.4 164.2 %all-gather.9.cloned.1.call-start = ((), (), s32[]{:S(2)}) async-start(), calls=%async_computation.7 | async-start | bytes 12976128 | tf_op jit(solution)/shard_map/all_gather | solution.py:742
  171.2 169.5 %all-gather.11.cloned.1.call-start = ((), (), s32[]{:S(2)}) async-start(), calls=%async_computation.8 | async-start | bytes 6488064 | tf_op jit(solution)/shard_map/all_gather | solution.py:742
  212.5 227.1 %reduce-scatter.6.cloned.1.call-start = ((), (), s32[]{:S(2)}) async-start(), calls=%async_computation.9 | async-start | bytes 3604480 | tf_op jit(solution)/shard_map/reduce_scatter | solution.py:851
  340.8 192.4 %reduce-scatter.8.cloned.1.call-start = ((), (), s32[]{:S(2)}) async-start(), calls=%async_computation.10 | async-start | bytes 3604480 | tf_op jit(solution)/shard_map/reduce_scatter | solution.py:851
  425.1 176.2 %reduce-scatter.10.cloned.1.call-start = ((), (), s32[]{:S(2)}) async-start(), calls=%async_computation.11 | async-start | bytes 3604480 | tf_op jit(solution)/shard_map/reduce_scatter | solution.py:851
  457.1 229.6 %reduce-scatter.14.cloned.1.call-start = ((), (), s32[]{:S(2)}) async-start(), calls=%async_computation.13 | async-start | bytes 1310720 | tf_op jit(solution)/shard_map/reduce_scatter | solution.py:851
  490.5 42.6 %collective-permute-start.31 = (bf16[256,2048]{1,0:T(8,128)(2,1)}, bf16[256,2048]{1,0:T(8,128)(2,1)}, u32[]{:S(2)}, u32[]{:S(2)}) collective-permute-start(bf16[256,2048]{1,0:T(8,128)(2,1)} %get-tuple-element.268), channel_id=1, source_target_pairs={{0,16},{4,20},{8,12},{12,8},{16,0},{20,4},{24,28},{28,24},{1,17},{... | collective-permute-start | bytes 3145736 | tf_op jit(solution)/shard_map/ppermute | solution.py:666
  491.7 41.5 %collective-permute-start.32 = (bf16[256,2048]{1,0:T(8,128)(2,1)}, bf16[256,2048]{1,0:T(8,128)(2,1)}, u32[]{:S(2)}, u32[]{:S(2)}) collective-permute-start(bf16[256,2048]{1,0:T(8,128)(2,1)} %get-tuple-element.267), channel_id=1, source_target_pairs={{0,16},{4,20},{8,12},{12,8},{16,0},{20,4},{24,28},{28,24},{1,17},{... | collective-permute-start | bytes 3145736 | tf_op jit(solution)/shard_map/ppermute | solution.py:667
  535.4 48.0 %collective-permute-start.33 = (bf16[256,2048]{1,0:T(8,128)(2,1)S(1)}, bf16[256,2048]{1,0:T(8,128)(2,1)S(1)}, u32[]{:S(2)}, u32[]{:S(2)}) collective-permute-start(bf16[256,2048]{1,0:T(8,128)(2,1)S(1)} %add_convert_fusion.7), channel_id=1, source_target_pairs={{0,4},{4,0},{8,24},{12,28},{16,20},{20,16},{24,8},{28,12},{1,5},{5... | collective-permute-start | bytes 3145736 | tf_op jit(solution)/shard_map/ppermute | solution.py:672
  539.5 43.8 %collective-permute-start.36 = (bf16[1024,256]{1,0:T(8,128)(2,1)S(1)}, bf16[1024,256]{1,0:T(8,128)(2,1)S(1)}, u32[]{:S(2)}, u32[]{:S(2)}) collective-permute-start(bf16[1024,256]{1,0:T(8,128)(2,1)S(1)} %bitcast.197), channel_id=1, source_target_pairs={{0,1},{1,2},{2,3},{3,0},{4,5},{5,6},{6,7},{7,4},{8,9},{9,10},{10,1... | collective-permute-start | bytes 1572872 | tf_op jit(solution)/shard_map/ppermute | solution.py:621
  543.2 49.5 %collective-permute-start.37 = (bf16[1024,512]{1,0:T(8,128)(2,1)}, bf16[1024,512]{1,0:T(8,128)(2,1)}, u32[]{:S(2)}, u32[]{:S(2)}) collective-permute-start(bf16[1024,512]{1,0:T(8,128)(2,1)} %fusion.34), channel_id=1, source_target_pairs={{0,8},{8,0},{1,9},{9,1},{2,10},{10,2},{3,11},{11,3},{4,12},{12,4},... | collective-permute-start | bytes 3145736 | tf_op jit(solution)/shard_map/ppermute | solution.py:624
  610.4 88.7 %reduce-scatter.12.cloned.1.call-start = ((), (), s32[]{:S(2)}) async-start(), calls=%async_computation.12 | async-start | bytes 1966080 | tf_op jit(solution)/shard_map/reduce_scatter | solution.py:851
  610.9 54.7 %collective-permute-start.48 = (bf16[768,1408]{1,0:T(8,128)(2,1)S(1)}, bf16[768,1408]{1,0:T(8,128)(2,1)}, u32[]{:S(2)}, u32[]{:S(2)}) collective-permute-start(bf16[768,1408]{1,0:T(8,128)(2,1)S(1)} %constant_dynamic-update-slice_fusion.12.refs_0_.refs_4_), channel_id=1, source_target_pairs={{0,16},{16,0},{1,17},{17,1},{2,18},{18,2},{3,19},{19,3},{4,20},{20... | collective-permute-start | bytes 6488072 | tf_op jit(solution)/shard_map/ppermute | solution.py:627
  623.0 50.9 %collective-permute-start.41 = (bf16[256,2048]{1,0:T(8,128)(2,1)}, bf16[256,2048]{1,0:T(8,128)(2,1)}, u32[]{:S(2)}, u32[]{:S(2)}) collective-permute-start(bf16[256,2048]{1,0:T(8,128)(2,1)} %add_convert_fusion.5), channel_id=1, source_target_pairs={{0,4},{4,0},{8,24},{12,28},{16,20},{20,16},{24,8},{28,12},{1,5},{5... | collective-permute-start | bytes 3145736 | tf_op jit(solution)/shard_map/ppermute | solution.py:672
  633.2 71.6 %collective-permute-start.49 = (bf16[768,1408]{1,0:T(8,128)(2,1)S(1)}, bf16[768,1408]{1,0:T(8,128)(2,1)}, u32[]{:S(2)}, u32[]{:S(2)}) collective-permute-start(bf16[768,1408]{1,0:T(8,128)(2,1)S(1)} %constant_dynamic-update-slice_fusion.12.refs_0_.refs_4_), channel_id=1, source_target_pairs={{0,8},{8,0},{1,9},{9,1},{2,10},{10,2},{3,11},{11,3},{4,12},{12,4},... | collective-permute-start | bytes 6488072 | tf_op jit(solution)/shard_map/ppermute | solution.py:624
  665.6 51.6 %collective-permute-start.50 = (bf16[768,1408]{1,0:T(8,128)(2,1)}, bf16[768,1408]{1,0:T(8,128)(2,1)}, u32[]{:S(2)}, u32[]{:S(2)}) collective-permute-start(bf16[768,1408]{1,0:T(8,128)(2,1)} %collective-permute-done.48.refs_1_.refs_5_), channel_id=1, source_target_pairs={{0,8},{8,0},{1,9},{9,1},{2,10},{10,2},{3,11},{11,3},{4,12},{12,4},... | collective-permute-start | bytes 6488072 | tf_op jit(solution)/shard_map/ppermute | solution.py:624
  704.9 67.0 %collective-permute-start.58 = (bf16[256,768]{1,0:T(8,128)(2,1)S(1)}, bf16[256,768]{1,0:T(8,128)(2,1)S(1)}, u32[]{:S(2)}, u32[]{:S(2)}) collective-permute-start(bf16[256,768]{1,0:T(8,128)(2,1)S(1)} %pad_maximum_fusion.13.refs_0_), channel_id=1, source_target_pairs={{0,16},{16,0},{1,17},{17,1},{2,18},{18,2},{3,19},{19,3},{4,20},{20... | collective-permute-start | bytes 1179656 | tf_op jit(solution)/shard_map/ppermute | solution.py:627
  706.2 62.7 %collective-permute-start.45 = (bf16[256,512]{1,0:T(8,128)(2,1)S(1)}, bf16[256,512]{1,0:T(8,128)(2,1)S(1)}, u32[]{:S(2)}, u32[]{:S(2)}) collective-permute-start(bf16[256,512]{1,0:T(8,128)(2,1)S(1)} %get-tuple-element.281), channel_id=1, source_target_pairs={{0,1},{1,2},{2,3},{3,0},{4,5},{5,6},{6,7},{7,4},{8,9},{9,10},{10,1... | collective-permute-start | bytes 786440 | tf_op jit(solution)/shard_map/ppermute | solution.py:621
  708.2 60.7 %collective-permute-start.46 = (bf16[256,512]{1,0:T(8,128)(2,1)S(1)}, bf16[256,512]{1,0:T(8,128)(2,1)S(1)}, u32[]{:S(2)}, u32[]{:S(2)}) collective-permute-start(bf16[256,512]{1,0:T(8,128)(2,1)S(1)} %get-tuple-element.280), channel_id=1, source_target_pairs={{0,2},{1,3},{2,0},{3,1},{4,6},{5,7},{6,4},{7,5},{8,10},{9,11},{10,... | collective-permute-start | bytes 786440 | tf_op jit(solution)/shard_map/ppermute | solution.py:621
  710.0 59.0 %collective-permute-start.47 = (bf16[256,512]{1,0:T(8,128)(2,1)S(1)}, bf16[256,512]{1,0:T(8,128)(2,1)S(1)}, u32[]{:S(2)}, u32[]{:S(2)}) collective-permute-start(bf16[256,512]{1,0:T(8,128)(2,1)S(1)} %get-tuple-element.279), channel_id=1, source_target_pairs={{0,3},{1,0},{2,1},{3,2},{4,7},{5,4},{6,5},{7,6},{8,11},{9,8},{10,9... | collective-permute-start | bytes 786440 | tf_op jit(solution)/shard_map/ppermute | solution.py:621
  (142 other events, 1789.5 us)
Sparse Core Ops, SparseCore 0:
  35.8 73.0 all-gather.4
  127.5 43.6 all-gather.6
  173.4 106.3 all-gather.8
  281.3 59.4 all-gather.10
  342.9 55.8 reduce-scatter.5
  425.3 56.6 reduce-scatter.7
  484.8 56.0 reduce-scatter.9
  610.5 47.5 reduce-scatter.13
  664.5 34.4 reduce-scatter.11
where the time goes:
time: 800 us; the launch traced here: 791 us
  waiting for transfers between devices  312 us (39%)
  Pallas kernels  181 us (23%)
  matrix products  88.7 us (11%)
  starting transfers between devices  74.7 us (9%)
  local copies, waits for them, and re-layouts  55.3 us (7%)
  other arithmetic  52.2 us (7%)
  between operations  26.8 us (3%)
    ppermute x25, waiting for transfers between devices, shift(): lax.ppermute(value, axis, [(i, (i + by) % size) for i in range(size)])  122 us
    ppermute x4, waiting for transfers between devices, gather_tokens(): first = lax.ppermute(own, near, first_pairs)  54.9 us
    dot_general x10, matrix products, dot_tn(): lax.dot_general(left, right, (((0,), (0,)), ((), ())), preferred_element_...  53.6 us
    pallas_call x1, Pallas kernels, gateup_update(): pl.pallas_call(gateup_update_kernel, grid_spec=pltpu.PrefetchScalarGridSp...  36.5 us
    ppermute x4, waiting for transfers between devices, reduce_tokens(): first = before_last(lax.ppermute(after_first(key), near, first_pairs))  33.8 us
    pallas_call x2, Pallas kernels, widen_back(): pl.pallas_call(functools.partial(widen_back_kernel, slots, len(kept)), gr...  33.7 us
    ppermute x25, starting transfers between devices, shift(): lax.ppermute(value, axis, [(i, (i + by) % size) for i in range(size)])  31.9 us
    pallas_call x1, Pallas kernels, attend_back(): pl.pallas_call(functools.partial(attend_back_kernel, parts, lines), grid_...  31.7 us
  transfers between devices with their start and end apart: 73, of which 35 were waited for; matrix products, arithmetic and copies ran while one was open for 22% of the time, Pallas kernels for 21%

commit v1 on v0

--- a/solution.py
+++ b/solution.py
@@ -556,12 +556,12 @@
     update(weight_refs, every, jnp.stack([gate, up], axis=1), D ** (-0.5))
 
 
-def gateup_update(meta, shards, weights, rows):
-    half, width = (shards[0].shape[0] // 3, shards[0].shape[1])
+def gateup_update(meta, gates, ups, weights, rows):
+    half, width = ups[0].shape
     shape = weights[0].shape
     tiles = half // rows
     gate = pl.BlockSpec((rows, width), lambda i, j, m: (tiles + j, 0))
-    up = pl.BlockSpec((rows, width), lambda i, j, m: (2 * tiles + j, 0))
+    up = pl.BlockSpec((rows, width), lambda i, j, m: (j, 0))
     block = pl.BlockSpec(
         (rows, 2, shape[2]), lambda i, j, m: (((m[1] + i) % 2) * tiles + j, 0, 0)
     )
@@ -579,7 +579,7 @@
             flops=20 * weights[0].size, bytes_accessed=28 * weights[0].size, transcendentals=0
         ),
         name="gateup_update",
-    )(meta, *shards, *shards, *weights)
+    )(meta, *gates, *ups, *weights)
 
 
 def on_device(
@@ -642,23 +642,21 @@
                 second_pairs.append(over_y if core_at == 0 else over_row)
     near = ("y", "core", "row")
 
-    def gather_tokens(own):
+    def gather_tokens(own, beside=()):
         if rows_on == 2:
             first = lax.ppermute(own, near, first_pairs)
             second = lax.ppermute(own, near, second_pairs)
-            first, second = lax.optimization_barrier((first, second))
+            first, second, *_ = lax.optimization_barrier((first, second, *beside))
             third = lax.ppermute(first, near, second_pairs)
             return [own, first, second, third]
         parts = [own] + [shift(own, "row", rows_on, by) for by in range(1, rows_on)]
         return parts + [other_y(part) for part in parts]
 
-    def reduce_tokens(
-        rows_of, after_close=None, after_first=None, before_last=None, far_here=None, ready=None
-    ):
+    def reduce_tokens(rows_of, middle=None, before_last=None, far_here=None, ready=None):
         def same(value):
             return value
 
-        after_close, after_first, before_last = [f or same for f in (after_close, after_first, before_last)]
+        middle, before_last = (middle or same, before_last or same)
         if rows_on == 2:
             far = rows_of(2, 4)
             if ready:
@@ -666,19 +664,19 @@
             third = lax.ppermute(far[block:], near, second_pairs)
             second = lax.ppermute(far[:block], near, second_pairs)
             if not ready:
-                close = after_close(rows_of(0, 2))
-            third, second = (far_here or lax.optimization_barrier)((third, second))
+                close = rows_of(0, 2)
+            third, second, close = (far_here or lax.optimization_barrier)((third, second, close))
             key = (close[block:].astype(jnp.float32) + third.astype(jnp.float32)).astype(jnp.bfloat16)
-            first = before_last(lax.ppermute(after_first(key), near, first_pairs))
+            first = before_last(lax.ppermute(middle(key), near, first_pairs))
             own = close[:block].astype(jnp.float32) + second.astype(jnp.float32)
             return own + first.astype(jnp.float32)
-        partial = after_close(rows_of(0, slots))
+        partial = rows_of(0, slots)
         parts = [partial[i * block : (i + 1) * block] for i in range(slots)]
         sums = [
             parts[i].astype(jnp.float32) + other_y(parts[rows_on + i]).astype(jnp.float32)
             for i in range(rows_on)
         ]
-        sums[0] = after_first(sums[0])
+        sums[0] = middle(sums[0])
         total = sums[0]
         for by in range(1, rows_on):
             moved = shift(sums[by].astype(jnp.bfloat16), "row", rows_on, -by)
@@ -784,8 +782,13 @@
         [b[:, :half] for b in gain_blocks] + [b[:, half:] for b in gain_blocks], axis=1
     )
 
+    residual_low = tokens_of(tokens_sent(block_input))
+    residual_low, late_cotangent, other_segments, joint_mine, output_mine = lax.optimization_barrier(
+        (residual_low, cotangent, other_y(segments), joint_mine, output_mine)
+    )
+
     own_starts = document_starts(segments[0])
-    other_starts = document_starts(other_y(segments)[0])
+    other_starts = document_starts(other_segments[0])
     frequency = 10000.0 ** (-2.0 * jnp.arange(HEAD_DIM // 2, dtype=jnp.float32) / HEAD_DIM)
     starts, places, meta = ([], [], [])
     for slot in range(slots):
@@ -809,10 +812,6 @@
     phases = offsets[:, None] * jnp.tile(frequency, LANES // (HEAD_DIM // 2))[None, :]
     cosine, sine = (jnp.cos(phases), jnp.sin(phases))
 
-    residual_low = tokens_of(tokens_sent(block_input))
-    residual_low, late_cotangent, joint_mine, output_mine = lax.optimization_barrier(
-        (residual_low, cotangent, joint_mine, output_mine)
-    )
     cot_parts = tokens_sent(late_cotangent)
     first_weight = gather_weight(jnp.concatenate([joint_mine, output_mine], axis=1))
     joint_width = joint_mine.shape[1]
@@ -871,23 +870,21 @@
         )
         return partial
 
-    def feed_others(close):
-        close, rows, gate, up = lax.optimization_barrier(
-            (close, normed_two, work["grad_gate"], work["grad_up"])
+    def feed_others(key):
+        key, rows, gate, up = lax.optimization_barrier(
+            (key, normed_two, work["grad_gate"], work["grad_up"])
         )
         work["feed"] = (rows, gate, up, other_half(rows, gate), other_half(rows, up))
-        return close
-
-    def feed_owns(key):
-        key, rows, gate, up, gate_other, up_other = lax.optimization_barrier((key, *work["feed"]))
+        return key
+
+    def feed_owns(first):
+        first, work["down_piece"], rows, gate, up, gate_other, up_other = lax.optimization_barrier(
+            (first, down_piece, *work["feed"])
+        )
         work["totals"] = (own_half(rows, gate, gate_other), own_half(rows, up, up_other))
-        return key
-
-    def feed_ends(first):
-        first, work["down_piece"] = lax.optimization_barrier((first, down_piece))
         return first
 
-    grad_normed_two = reduce_tokens(feed_back, feed_others, feed_owns, feed_ends)
+    grad_normed_two = reduce_tokens(feed_back, feed_others, feed_owns)
     gate_piece, up_piece = [scatter(total) for total in work["totals"]]
 
     def norm_back(values, scale, grad_normed, gain):
@@ -903,7 +900,8 @@
     grad_middle_low, late_hidden = lax.optimization_barrier(
         (grad_middle.astype(jnp.bfloat16), hidden)
     )
-    back = jnp.concatenate(gather_tokens(grad_middle_low), axis=0)
+    gate_total, up_total = work["totals"]
+    back = jnp.concatenate(gather_tokens(grad_middle_low, (gate_total, up_total)), axis=0)
 
     def back_here(products):
         products, work["back"] = lax.optimization_barrier((products, back))
@@ -932,59 +930,71 @@
         return far
 
     def keys_arrive(first):
-        first, work["grad_parts"] = lax.optimization_barrier((first, work["grad_parts"]))
+        first, work["grad_parts"], work["up_piece"] = lax.optimization_barrier(
+            (first, work["grad_parts"], up_piece)
+        )
         return first
 
     if rows_on == 2:
         ffn_sum = reduce_tokens(
-            product(late_hidden, down_weight), None, None, keys_arrive, attention_back, back_here
+            product(late_hidden, down_weight), None, keys_arrive, attention_back, back_here
         )
     else:
-        ffn_sum = attention_back(reduce_tokens(product(late_hidden, down_weight)))
+        ffn_sum = keys_arrive(attention_back(reduce_tokens(product(late_hidden, down_weight))))
     grad_query, gate_piece, back, mixed = [
         work[name] for name in ("grad_query", "gate_piece", "back", "mixed")
     ]
     output_total = own_half(back, mixed, other_half(back, mixed))
-    layer_output = features_of(features_sent((middle + ffn_sum).astype(jnp.bfloat16)))
+    output_parts = features_sent((middle + ffn_sum).astype(jnp.bfloat16))
     grad_keyvalue = pair_back(work["grad_parts"], cosine, sine, block)
     grad_joint = jnp.concatenate([grad_query, grad_keyvalue], axis=1)
     normed_one = jnp.concatenate(normed_parts, axis=0)
-    def joint_others(close):
-        close, up_done, work["output"], rows, grad = lax.optimization_barrier(
-            (close, up_piece, output_total, normed_one, grad_joint)
-        )
-        work["feed_shards"] = collect(
-            jnp.concatenate([work["down_piece"], gate_piece, up_done], axis=0)
-        )
+    meta_core = jnp.stack([y, core]).astype(jnp.int32)
+
+    def joint_products(first, last):
+        if first:
+            return product(grad_joint, joint_weight)(first, last)
+        work["shards"] = collect(jnp.concatenate([work["down_piece"], gate_piece], axis=0))
+        down_new = turned_update(
+            meta_core,
+            work["shards"],
+            [w_down, down_moment, down_square],
+            FF ** (-0.5),
+            False,
+        )
+        close, work["output"], work["down_new"] = lax.optimization_barrier(
+            (product(grad_joint, joint_weight)(first, last), output_total, down_new)
+        )
+        return close
+
+    def joint_others(key):
+        key, rows, grad = lax.optimization_barrier((key, normed_one, grad_joint))
         work["joint"] = (rows, grad, other_half(rows, grad))
-        return close
-
-    def joint_owns(key):
-        key, rows, grad, other = lax.optimization_barrier((key, *work["joint"]))
+        work["output_piece"] = scatter(work["output"])
+        return key
+
+    def joint_owns(first):
+        first, work["output_piece"], work["output_parts"], rows, grad, other = (
+            lax.optimization_barrier((first, work["output_piece"], output_parts, *work["joint"]))
+        )
         work["joint_total"] = own_half(rows, grad, other)
-        return key
-
-    grad_normed_one = reduce_tokens(product(grad_joint, joint_weight), joint_others, joint_owns)
-    joint_piece, output_piece = (scatter(work["joint_total"]), scatter(work["output"]))
-    meta_core = jnp.stack([y, core]).astype(jnp.int32)
+        return first
+
+    grad_normed_one = reduce_tokens(joint_products, joint_others, joint_owns)
+    joint_piece = scatter(work["joint_total"])
     gateup_new = gateup_update(
-        meta_core, work["feed_shards"], [w_gateup, gateup_moment, gateup_square], 32
-    )
-    down_new = turned_update(
         meta_core,
-        work["feed_shards"],
-        [w_down, down_moment, down_square],
-        FF ** (-0.5),
-        False,
+        work["shards"],
+        collect(work["up_piece"]),
+        [w_gateup, gateup_moment, gateup_square],
+        32,
     )
     input_grad = grad_middle + norm_back(residual, scale_one, grad_normed_one, gains[0])
     gain_one = jnp.sum(grad_normed_one * residual * scale_one, axis=0)
-    input_grad, layer_output = lax.optimization_barrier(
-        (input_grad.astype(jnp.bfloat16), layer_output)
-    )
-    input_parts, gateup_new, down_new = lax.optimization_barrier(
-        (features_sent(input_grad), gateup_new, down_new)
-    )
+    input_parts, gateup_new = lax.optimization_barrier(
+        (features_sent(input_grad.astype(jnp.bfloat16)), gateup_new)
+    )
+    layer_output = features_of(work["output_parts"])
     input_grad = features_of(input_parts).astype(jnp.float32)
     pair_piece = joint_piece[:, query_width:]
     pair_total = pair_piece.astype(jnp.float32)
@@ -1001,7 +1011,7 @@
     )
     output_new = turned_update(
         meta_core,
-        collect(output_piece),
+        collect(work["output_piece"]),
         [w_output, output_moment, output_square],
         (HEADS * HEAD_DIM // 64) ** (-0.5),
         True,
@@ -1034,7 +1044,7 @@
         *joint_new,
         *output_new,
         *gateup_new,
-        *down_new,
+        *work["down_new"],
     )
 
 

time: 800 us -> 799 us (level)
  waiting for transfers between devices: 312 us -> 294 us
  starting transfers between devices: 74.7 us -> 91.3 us
    ppermute x4, waiting for transfers between devices: 54.9 us -> 76.9 us  [gather_tokens(): first = lax.ppermute(own, near, first_pairs)]
    reduce_scatter x5, waiting for transfers between devices: 8.05 us -> 27.4 us  [scatter(): return lax.psum_scatter(total, 'col', scatter_dimension=0, tiled=True)]
    ppermute x4 -> x5, waiting for transfers between devices: 19.2 us -> 0.01 us  [other_y(): return lax.ppermute(value, 'y', [(0, 1), (1, 0)])]
    ppermute x11 -> x13, starting transfers between devices: 12.4 us -> 31.3 us  [other_core(): return lax.ppermute(value, 'core', [(0, 1), (1, 0)])]
    ppermute x25, waiting for transfers between devices: 122 us -> 106 us  [shift(): lax.ppermute(value, axis, [(i, (i + by) % size) for i in range(size)])]
    ppermute x4, waiting for transfers between devices: 22.1 us -> 9.64 us  [reduce_tokens(): third = lax.ppermute(far[block:], near, second_pairs)]
    reduce_scatter x5, starting transfers between devices: 8.65 us -> 0.42 us  [scatter(): return lax.psum_scatter(total, 'col', scatter_dimension=0, tiled=True)]
    ppermute x4, waiting for transfers between devices: 33.8 us -> 25.7 us  [reduce_tokens(): first = before_last(lax.ppermute(middle(key), near, first_pairs))]
  transfers between devices with their start and end apart: 73 -> 76, of which waited for: 35 -> 35; matrix products, arithmetic and copies ran while one was open for 22% -> 20% of each run, Pallas kernels for 21% -> 19%
where the time goes in v1:
time: 799 us; the launch traced here: 785 us
  waiting for transfers between devices  294 us (37%)
  Pallas kernels  179 us (22%)
  starting transfers between devices  91.3 us (11%)
  matrix products  89.5 us (11%)
  local copies, waits for them, and re-layouts  55.8 us (7%)
  other arithmetic  48.1 us (6%)
  between operations  26.7 us (3%)
    ppermute x25, waiting for transfers between devices, shift(): lax.ppermute(value, axis, [(i, (i + by) % size) for i in range(size)])  106 us
    ppermute x4, waiting for transfers between devices, gather_tokens(): first = lax.ppermute(own, near, first_pairs)  76.9 us
    dot_general x10, matrix products, dot_tn(): lax.dot_general(left, right, (((0,), (0,)), ((), ())), preferred_element_...  56.4 us
    ppermute x25, starting transfers between devices, shift(): lax.ppermute(value, axis, [(i, (i + by) % size) for i in range(size)])  36.8 us
    pallas_call x1, Pallas kernels, gateup_update(): pl.pallas_call(gateup_update_kernel, grid_spec=pltpu.PrefetchScalarGridSp...  36.5 us
    pallas_call x2, Pallas kernels, widen_back(): pl.pallas_call(functools.partial(widen_back_kernel, slots, len(kept)), gr...  35 us
    ppermute x13, starting transfers between devices, other_core(): return lax.ppermute(value, 'core', [(0, 1), (1, 0)])  31.3 us
    pallas_call x1, Pallas kernels, attend_back(): pl.pallas_call(functools.partial(attend_back_kernel, parts, lines), grid_...  29.4 us
  transfers between devices with their start and end apart: 76, of which 35 were waited for; matrix products, arithmetic and copies ran while one was open for 20% of the time, Pallas kernels for 19%

profile of v1, /device:TPU:11, one launch (start us, length us, event | category | flops | bytes accessed | tf_op | source)
XLA Modules:
  0.0 784.5 jit_solution(7577746679006673812)
XLA Ops:
  47.5 17.0 %collective-permute-done.7.refs_1_ = bf16[256,2048]{1,0:T(8,128)(2,1)S(1)} collective-permute-done((bf16[256,2048]{1,0:T(8,128)(2,1)S(1)}, bf16[256,2048]{1,0:T(8,128)(2,1)S(1)}, u32[]{:S(2)}, u32[]{:S(2)}) %collective-permute-start.7) | collective-permute-done | bytes 1048608 | tf_op jit(solution)/shard_map/ppermute | solution.py:647
  75.2 9.1 %collective-permute-done.10 = bf16[256,512]{1,0:T(8,128)(2,1)S(1)} collective-permute-done((bf16[256,512]{1,0:T(8,128)(2,1)}, bf16[256,512]{1,0:T(8,128)(2,1)S(1)}, u32[]{:S(2)}, u32[]{:S(2)}) %collective-permute-start.10) | collective-permute-done | bytes 262176 | tf_op jit(solution)/shard_map/ppermute | solution.py:621
  84.3 26.6 %collective-permute-done.11 = bf16[256,512]{1,0:T(8,128)(2,1)S(1)} collective-permute-done((bf16[256,512]{1,0:T(8,128)(2,1)}, bf16[256,512]{1,0:T(8,128)(2,1)S(1)}, u32[]{:S(2)}, u32[]{:S(2)}) %collective-permute-start.11) | collective-permute-done | bytes 262176 | tf_op jit(solution)/shard_map/ppermute | solution.py:621
  130.7 22.4 %collective-permute-done.13.refs_1_ = bf16[256,2048]{1,0:T(8,128)(2,1)S(1)} collective-permute-done((bf16[256,2048]{1,0:T(8,128)(2,1)S(1)}, bf16[256,2048]{1,0:T(8,128)(2,1)S(1)}, u32[]{:S(2)}, u32[]{:S(2)}) %collective-permute-start.13) | collective-permute-done | bytes 1048608 | tf_op jit(solution)/shard_map/ppermute | solution.py:647
  185.6 16.8 %attend.1 = (bf16[1024,512]{1,0:T(8,128)(2,1)S(1)}, f32[4,2,1024]{2,1,0:T(2,128)S(1)}) custom-call(s32[17]{0:T(128)S(1)} %stack.178.meta_ref, bf16[1024,512]{1,0:T(8,128)(2,1)S(1)} %copy-done.38, bf16[4,4,256,256]{3,2,1,0:T(8,128)(2,1)S(1)} %copy-done.36, s32[4,2,256]{2,1,0:T(2,128)S(1)} %pad_add_fusion.2.info_ref.refs_4_), custom_call_target="tpu_custom_call" | custom-call | flops 3221225472 | bytes 4194304 | tf_op jit(solution)/shard_map/attend/pallas_call | solution.py:274
  212.0 9.6 %collective-permute-done.16 = bf16[256,2048]{1,0:T(8,128)(2,1)} collective-permute-done((bf16[256,2048]{1,0:T(8,128)(2,1)}, bf16[256,2048]{1,0:T(8,128)(2,1)}, u32[]{:S(2)}, u32[]{:S(2)}) %collective-permute-start.16) | collective-permute-done | bytes 1048608 | tf_op jit(solution)/shard_map/ppermute | solution.py:664
  221.6 11.2 %collective-permute-done.17 = bf16[256,2048]{1,0:T(8,128)(2,1)} collective-permute-done((bf16[256,2048]{1,0:T(8,128)(2,1)}, bf16[256,2048]{1,0:T(8,128)(2,1)}, u32[]{:S(2)}, u32[]{:S(2)}) %collective-permute-start.17) | collective-permute-done | bytes 1048608 | tf_op jit(solution)/shard_map/ppermute | solution.py:665
  235.7 12.9 %collective-permute-done.18 = bf16[256,2048]{1,0:T(8,128)(2,1)S(1)} collective-permute-done((bf16[256,2048]{1,0:T(8,128)(2,1)S(1)}, bf16[256,2048]{1,0:T(8,128)(2,1)S(1)}, u32[]{:S(2)}, u32[]{:S(2)}) %collective-permute-start.18) | collective-permute-done | bytes 1048608 | tf_op jit(solution)/shard_map/ppermute | solution.py:670
  252.3 21.6 %collective-permute-done.19.refs_1_ = bf16[256,2048]{1,0:T(8,128)(2,1)} collective-permute-done((bf16[256,2048]{1,0:T(8,128)(2,1)S(1)}, bf16[256,2048]{1,0:T(8,128)(2,1)}, u32[]{:S(2)}, u32[]{:S(2)}) %collective-permute-start.19) | collective-permute-done | bytes 1048608 | tf_op jit(solution)/shard_map/ppermute | solution.py:647
  283.7 8.5 %collective-permute-done.21.refs_3_ = bf16[256,2048]{1,0:T(8,128)(2,1)} collective-permute-done((bf16[256,2048]{1,0:T(8,128)(2,1)}, bf16[256,2048]{1,0:T(8,128)(2,1)}, u32[]{:S(2)}, u32[]{:S(2)}) %collective-permute-start.21) | collective-permute-done | bytes 1048608 | tf_op jit(solution)/shard_map/ppermute | solution.py:650
  292.3 19.9 %widen.1 = (bf16[1024,1408]{1,0:T(8,128)(2,1)}, bf16[1024,1408]{1,0:T(8,128)(2,1)}, bf16[1024,1408]{1,0:T(8,128)(2,1)}) custom-call(bf16[256,2048]{1,0:T(8,128)(2,1)S(1)} %multiply_convert_fusion.refs_0_, bf16[256,2048]{1,0:T(8,128)(2,1)} %collective-permute-done.19.refs_1_, bf16[256,2048]{1,0:T(8,128)(2,1)S(1)} %copy-done.28, ...), custom_call_target="tpu_custom_call" | custom-call | flops 11811160064 | bytes 24379392 | tf_op jit(solution)/shard_map/widen/pallas_call | solution.py:141
  340.4 16.7 %widen_back.2 = (bf16[1024,1408]{1,0:T(8,128)(2,1)}, bf16[1024,1408]{1,0:T(8,128)(2,1)}, bf16[512,2048]{1,0:T(8,128)(2,1)S(1)}) custom-call(bf16[256,2048]{1,0:T(8,128)(2,1)S(1)} %copy-done.18, bf16[256,2048]{1,0:T(8,128)(2,1)} %collective-permute-done.15.refs_1_, bf16[2048,1408]{1,0:T(8,128)(2,1)} %all-gather.11.cloned.1.call-done.refs_2_, ...), custom_call_target="tpu_custom_call" | custom-call | flops 8858370048 | bytes 23068672 | tf_op jit(solution)/shard_map/widen_back/pallas_call | solution.py:179
  362.2 18.4 %widen_back.3 = (bf16[1024,1408]{1,0:T(8,128)(2,1)}, bf16[1024,1408]{1,0:T(8,128)(2,1)}, bf16[512,2048]{1,0:T(8,128)(2,1)S(1)}) custom-call(bf16[256,2048]{1,0:T(8,128)(2,1)S(1)} %slice_dynamic-update-slice_fusion.refs_0_, bf16[256,2048]{1,0:T(8,128)(2,1)S(1)} %copy-done.15, ...), custom_call_target="tpu_custom_call", output_to_operand_aliasing={{0}: (6, {}), {1}: (7, {})} | custom-call | flops 8858370048 | bytes 23068672 | tf_op jit(solution)/shard_map/widen_back/pallas_call | solution.py:179
  395.7 12.9 %collective-permute-done.25 = bf16[256,2048]{1,0:T(8,128)(2,1)} collective-permute-done((bf16[256,2048]{1,0:T(8,128)(2,1)S(1)}, bf16[256,2048]{1,0:T(8,128)(2,1)}, u32[]{:S(2)}, u32[]{:S(2)}) %collective-permute-start.25) | collective-permute-done | bytes 1048608 | tf_op jit(solution)/shard_map/ppermute | solution.py:670
  440.9 16.0 %collective-permute-done.28 = bf16[256,2048]{1,0:T(8,128)(2,1)S(1)} collective-permute-done((bf16[256,2048]{1,0:T(8,128)(2,1)}, bf16[256,2048]{1,0:T(8,128)(2,1)S(1)}, u32[]{:S(2)}, u32[]{:S(2)}) %collective-permute-start.28) | collective-permute-done | bytes 1048608 | tf_op jit(solution)/shard_map/ppermute | solution.py:647
  483.4 29.4 %attend_back.1 = (bf16[1024,512]{1,0:T(8,128)(2,1)S(1)}, bf16[4,256,256]{2,1,0:T(8,128)(2,1)S(1)}, bf16[4,256,256]{2,1,0:T(8,128)(2,1)}, bf16[4,256,256]{2,1,0:T(8,128)(2,1)}, bf16[4,256,256]{2,1,0:T(8,128)(2,1)}) custom-call(s32[17]{0:T(128)S(1)} %stack.178.meta_ref, bf16[1024,512]{1,0:T(8,128)(2,1)S(1)} %copy-done.39, ...), custom_call_target="tpu_custom_call" | custom-call | flops 8053063680 | bytes 8388608 | tf_op jit(solution)/shard_map/attend_back/pallas_call | solution.py:378
  530.4 19.4 %collective-permute-done.34.refs_1_ = bf16[1024,256]{1,0:T(8,128)(2,1)} collective-permute-done((bf16[1024,256]{1,0:T(8,128)(2,1)}, bf16[1024,256]{1,0:T(8,128)(2,1)}, u32[]{:S(2)}, u32[]{:S(2)}) %collective-permute-start.34) | collective-permute-done | bytes 524320 | tf_op jit(solution)/shard_map/ppermute | solution.py:621
  554.4 16.4 %collective-permute-done.35.refs_2_ = bf16[1024,256]{1,0:T(8,128)(2,1)} collective-permute-done((bf16[1024,256]{1,0:T(8,128)(2,1)}, bf16[1024,256]{1,0:T(8,128)(2,1)}, u32[]{:S(2)}, u32[]{:S(2)}) %collective-permute-start.35) | collective-permute-done | bytes 524320 | tf_op jit(solution)/shard_map/ppermute | solution.py:621
  571.7 10.3 %collective-permute-done.36.refs_3_ = bf16[1024,256]{1,0:T(8,128)(2,1)} collective-permute-done((bf16[1024,256]{1,0:T(8,128)(2,1)}, bf16[1024,256]{1,0:T(8,128)(2,1)}, u32[]{:S(2)}, u32[]{:S(2)}) %collective-permute-start.36) | collective-permute-done | bytes 524320 | tf_op jit(solution)/shard_map/ppermute | solution.py:621
  609.0 15.0 %turned_update.2 = (f32[2816,512]{1,0:T(8,128)}, f32[2816,512]{1,0:T(8,128)}, f32[2816,512]{1,0:T(8,128)}) custom-call(s32[2]{0:T(128)S(1)} %pad_add_fusion.5.meta_ref, bf16[512,1408]{1,0:T(8,128)(2,1)S(1)} %constant_dynamic-update-slice_fusion.12.refs_0_, bf16[512,1408]{1,0:T(8,128)(2,1)S(1)} %collective-permute-done.40.refs_1_, ...), custom_call_target="tpu_custom_call" | custom-call | flops 28835840 | bytes 34603008 | tf_op jit(solution)/shard_map/turned_update/pallas_call | solution.py:531
  647.9 36.5 %gateup_update.1 = (f32[512,2,2816]{2,1,0:T(2,128)}, f32[512,2,2816]{2,1,0:T(2,128)}, f32[512,2,2816]{2,1,0:T(2,128)}) custom-call(s32[2]{0:T(128)S(1)} %pad_add_fusion.5.meta_ref, bf16[512,1408]{1,0:T(8,128)(2,1)S(1)} %constant_dynamic-update-slice_fusion.12.refs_0_, bf16[512,1408]{1,0:T(8,128)(2,1)S(1)} %collective-permute-done.40.refs_1_, ...), custom_call_target="tpu_custom_call" | custom-call | flops 57671680 | bytes 80740352 | tf_op jit(solution)/shard_map/gateup_update/pallas_call | solution.py:568
  704.7 19.3 %reduce-scatter.14.cloned.1.call-done = bf16[256,768]{1,0:T(8,128)(2,1)} async-done(((bf16[1024,768]{1,0:T(8,128)(2,1)}), bf16[256,768]{1,0:T(8,128)(2,1)}) %reduce-scatter.14.cloned.1.call-update) | async-done | bytes 393232 | tf_op jit(solution)/shard_map/reduce_scatter | solution.py:850
  737.2 15.8 %collective-permute-start.65 = (bf16[256,512]{1,0:T(8,128)(2,1)S(1)}, bf16[256,512]{1,0:T(8,128)(2,1)S(1)}, u32[]{:S(2)}, u32[]{:S(2)}) collective-permute-start(bf16[256,512]{1,0:T(8,128)(2,1)S(1)} %copy-done.35), channel_id=1, source_target_pairs={{0,8},{8,0},{1,9},{9,1},{2,10},{10,2},{3,11},{11,3},{4,12},{12,4},... | collective-permute-start | bytes 786440 | tf_op jit(solution)/shard_map/ppermute | solution.py:624
  768.3 9.5 %joint_update.1 = (f32[512,1024]{1,0:T(8,128)}, f32[512,1024]{1,0:T(8,128)}, f32[512,1024]{1,0:T(8,128)}, f32[512,512]{1,0:T(8,128)}, f32[512,512]{1,0:T(8,128)}, /*index=5*/f32[512,512]{1,0:T(8,128)}) custom-call(s32[2]{0:T(128)S(1)} %pad_add_fusion.5.meta_ref, bf16[256,768]{1,0:T(8,128)(2,1)S(1)} %pad_maximum_fusion.13.refs_0_, ...), custom_call_target="tpu_custom_call" | custom-call | flops 15728640 | bytes 18874368 | tf_op jit(solution)/shard_map/joint_update/pallas_call | solution.py:489
  (477 shorter events, 346.8 us)
Async XLA Ops:
  7.2 107.5 %all-gather.5.cloned.1.call-start = ((), (), s32[]{:S(2)}) async-start(), calls=%async_computation.5 | async-start | bytes 5898240 | tf_op jit(solution)/shard_map/all_gather | solution.py:740
  35.7 134.5 %all-gather.7.cloned.1.call-start = ((), (), s32[]{:S(2)}) async-start(), calls=%async_computation.6 | async-start | bytes 2621440 | tf_op jit(solution)/shard_map/all_gather | solution.py:826
  68.5 45.0 %collective-permute-start.9 = (bf16[256,2048]{1,0:T(8,128)(2,1)S(1)}, bf16[256,2048]{1,0:T(8,128)(2,1)}, u32[]{:S(2)}, u32[]{:S(2)}) collective-permute-start(bf16[256,2048]{1,0:T(8,128)(2,1)S(1)} %collective-permute-done.7.refs_1_), channel_id=1, source_target_pairs={{0,16},{4,20},{8,12},{12,8},{16,0},{20,4},{24,28},{28,24},{1,17},{... | collective-permute-start | bytes 3145736 | tf_op jit(solution)/shard_map/ppermute | solution.py:650
  69.3 41.6 %collective-permute-start.11 = (bf16[256,512]{1,0:T(8,128)(2,1)}, bf16[256,512]{1,0:T(8,128)(2,1)S(1)}, u32[]{:S(2)}, u32[]{:S(2)}) collective-permute-start(bf16[256,512]{1,0:T(8,128)(2,1)} %get-tuple-element.328), channel_id=1, source_target_pairs={{0,2},{1,3},{2,0},{3,1},{4,6},{5,7},{6,4},{7,5},{8,10},{9,11},{10,... | collective-permute-start | bytes 786440 | tf_op jit(solution)/shard_map/ppermute | solution.py:621
  72.9 40.6 %collective-permute-start.12 = (bf16[256,512]{1,0:T(8,128)(2,1)}, bf16[256,512]{1,0:T(8,128)(2,1)S(1)}, u32[]{:S(2)}, u32[]{:S(2)}) collective-permute-start(bf16[256,512]{1,0:T(8,128)(2,1)} %get-tuple-element.327), channel_id=1, source_target_pairs={{0,3},{1,0},{2,1},{3,2},{4,7},{5,4},{6,5},{7,6},{8,11},{9,8},{10,9... | collective-permute-start | bytes 786440 | tf_op jit(solution)/shard_map/ppermute | solution.py:621
  126.6 165.7 %all-gather.9.cloned.1.call-start = ((), (), s32[]{:S(2)}) async-start(), calls=%async_computation.7 | async-start | bytes 12976128 | tf_op jit(solution)/shard_map/all_gather | solution.py:740
  170.3 170.1 %all-gather.11.cloned.1.call-start = ((), (), s32[]{:S(2)}) async-start(), calls=%async_computation.8 | async-start | bytes 6488064 | tf_op jit(solution)/shard_map/all_gather | solution.py:740
  208.8 207.8 %reduce-scatter.6.cloned.1.call-start = ((), (), s32[]{:S(2)}) async-start(), calls=%async_computation.9 | async-start | bytes 3604480 | tf_op jit(solution)/shard_map/reduce_scatter | solution.py:850
  360.1 153.7 %reduce-scatter.8.cloned.1.call-start = ((), (), s32[]{:S(2)}) async-start(), calls=%async_computation.10 | async-start | bytes 3604480 | tf_op jit(solution)/shard_map/reduce_scatter | solution.py:850
  425.0 157.0 %reduce-scatter.10.cloned.1.call-start = ((), (), s32[]{:S(2)}) async-start(), calls=%async_computation.11 | async-start | bytes 3604480 | tf_op jit(solution)/shard_map/reduce_scatter | solution.py:850
  440.8 243.6 %reduce-scatter.12.cloned.1.call-start = ((), (), s32[]{:S(2)}) async-start(), calls=%async_computation.12 | async-start | bytes 1310720 | tf_op jit(solution)/shard_map/reduce_scatter | solution.py:850
  476.6 37.1 %collective-permute-start.31 = (bf16[256,2048]{1,0:T(8,128)(2,1)S(1)}, bf16[256,2048]{1,0:T(8,128)(2,1)}, u32[]{:S(2)}, u32[]{:S(2)}) collective-permute-start(bf16[256,2048]{1,0:T(8,128)(2,1)S(1)} %get-tuple-element.284), channel_id=1, source_target_pairs={{0,16},{4,20},{8,12},{12,8},{16,0},{20,4},{24,28},{28,24},{1,17},{... | collective-permute-start | bytes 3145736 | tf_op jit(solution)/shard_map/ppermute | solution.py:664
  516.9 65.1 %collective-permute-start.33 = (bf16[256,2048]{1,0:T(8,128)(2,1)}, bf16[256,2048]{1,0:T(8,128)(2,1)}, u32[]{:S(2)}, u32[]{:S(2)}) collective-permute-start(bf16[256,2048]{1,0:T(8,128)(2,1)} %add_convert_fusion.7), channel_id=1, source_target_pairs={{0,4},{4,0},{8,24},{12,28},{16,20},{20,16},{24,8},{28,12},{1,5},{5... | collective-permute-start | bytes 3145736 | tf_op jit(solution)/shard_map/ppermute | solution.py:670
  517.0 73.9 %collective-permute-start.40 = (bf16[512,1408]{1,0:T(8,128)(2,1)S(1)}, bf16[512,1408]{1,0:T(8,128)(2,1)S(1)}, u32[]{:S(2)}, u32[]{:S(2)}) collective-permute-start(bf16[512,1408]{1,0:T(8,128)(2,1)S(1)} %constant_dynamic-update-slice_fusion.12.refs_0_), channel_id=1, source_target_pairs={{0,16},{16,0},{1,17},{17,1},{2,18},{18,2},{3,19},{19,3},{4,20},{20... | collective-permute-start | bytes 4325384 | tf_op jit(solution)/shard_map/ppermute | solution.py:627
  518.5 52.3 %collective-permute-start.35 = (bf16[1024,256]{1,0:T(8,128)(2,1)}, bf16[1024,256]{1,0:T(8,128)(2,1)}, u32[]{:S(2)}, u32[]{:S(2)}) collective-permute-start(bf16[1024,256]{1,0:T(8,128)(2,1)} %bitcast.63), channel_id=1, source_target_pairs={{0,2},{1,3},{2,0},{3,1},{4,6},{5,7},{6,4},{7,5},{8,10},{9,11},{10,... | collective-permute-start | bytes 1572872 | tf_op jit(solution)/shard_map/ppermute | solution.py:621
  523.5 58.6 %collective-permute-start.36 = (bf16[1024,256]{1,0:T(8,128)(2,1)}, bf16[1024,256]{1,0:T(8,128)(2,1)}, u32[]{:S(2)}, u32[]{:S(2)}) collective-permute-start(bf16[1024,256]{1,0:T(8,128)(2,1)} %bitcast.64), channel_id=1, source_target_pairs={{0,1},{1,2},{2,3},{3,0},{4,5},{5,6},{6,7},{7,4},{8,9},{9,10},{10,1... | collective-permute-start | bytes 1572872 | tf_op jit(solution)/shard_map/ppermute | solution.py:621
  549.7 58.3 %collective-permute-start.41 = (bf16[512,1408]{1,0:T(8,128)(2,1)S(1)}, bf16[512,1408]{1,0:T(8,128)(2,1)}, u32[]{:S(2)}, u32[]{:S(2)}) collective-permute-start(bf16[512,1408]{1,0:T(8,128)(2,1)S(1)} %constant_dynamic-update-slice_fusion.12.refs_0_), channel_id=1, source_target_pairs={{0,8},{8,0},{1,9},{9,1},{2,10},{10,2},{3,11},{11,3},{4,12},{12,4},... | collective-permute-start | bytes 4325384 | tf_op jit(solution)/shard_map/ppermute | solution.py:624
  599.5 39.3 %collective-permute-start.51 = (bf16[256,1408]{1,0:T(8,128)(2,1)}, bf16[256,1408]{1,0:T(8,128)(2,1)}, u32[]{:S(2)}, u32[]{:S(2)}) collective-permute-start(bf16[256,1408]{1,0:T(8,128)(2,1)} %reduce-scatter.10.cloned.1.call-done.refs_4_), channel_id=1, source_target_pairs={{0,16},{16,0},{1,17},{17,1},{2,18},{18,2},{3,19},{19,3},{4,20},{20... | collective-permute-start | bytes 2162696 | tf_op jit(solution)/shard_map/ppermute | solution.py:627
  626.6 97.4 %reduce-scatter.14.cloned.1.call-start = ((), (), s32[]{:S(2)}) async-start(), calls=%async_computation.13 | async-start | bytes 1966080 | tf_op jit(solution)/shard_map/reduce_scatter | solution.py:850
  631.9 52.5 %collective-permute-start.47 = (bf16[1024,768]{1,0:T(8,128)(2,1)}, bf16[1024,768]{1,0:T(8,128)(2,1)}, u32[]{:S(2)}, u32[]{:S(2)}) collective-permute-start(bf16[1024,768]{1,0:T(8,128)(2,1)} %fusion.25), channel_id=1, source_target_pairs={{0,8},{8,0},{1,9},{9,1},{2,10},{10,2},{3,11},{11,3},{4,12},{12,4},... | collective-permute-start | bytes 4718600 | tf_op jit(solution)/shard_map/ppermute | solution.py:624
  637.4 46.9 %collective-permute-start.43 = (bf16[256,2048]{1,0:T(8,128)(2,1)}, bf16[256,2048]{1,0:T(8,128)(2,1)}, u32[]{:S(2)}, u32[]{:S(2)}) collective-permute-start(bf16[256,2048]{1,0:T(8,128)(2,1)} %add_convert_fusion.5), channel_id=1, source_target_pairs={{0,4},{4,0},{8,24},{12,28},{16,20},{20,16},{24,8},{28,12},{1,5},{5... | collective-permute-start | bytes 3145736 | tf_op jit(solution)/shard_map/ppermute | solution.py:670
  640.0 44.3 %collective-permute-start.44 = (bf16[256,512]{1,0:T(8,128)(2,1)}, bf16[256,512]{1,0:T(8,128)(2,1)}, u32[]{:S(2)}, u32[]{:S(2)}) collective-permute-start(bf16[256,512]{1,0:T(8,128)(2,1)} %get-tuple-element.313), channel_id=1, source_target_pairs={{0,1},{1,2},{2,3},{3,0},{4,5},{5,6},{6,7},{7,4},{8,9},{9,10},{10,1... | collective-permute-start | bytes 786440 | tf_op jit(solution)/shard_map/ppermute | solution.py:621
  642.3 42.1 %collective-permute-start.45 = (bf16[256,512]{1,0:T(8,128)(2,1)}, bf16[256,512]{1,0:T(8,128)(2,1)}, u32[]{:S(2)}, u32[]{:S(2)}) collective-permute-start(bf16[256,512]{1,0:T(8,128)(2,1)} %get-tuple-element.312), channel_id=1, source_target_pairs={{0,2},{1,3},{2,0},{3,1},{4,6},{5,7},{6,4},{7,5},{8,10},{9,11},{10,... | collective-permute-start | bytes 786440 | tf_op jit(solution)/shard_map/ppermute | solution.py:621
  646.6 37.8 %collective-permute-start.46 = (bf16[256,512]{1,0:T(8,128)(2,1)S(1)}, bf16[256,512]{1,0:T(8,128)(2,1)}, u32[]{:S(2)}, u32[]{:S(2)}) collective-permute-start(bf16[256,512]{1,0:T(8,128)(2,1)S(1)} %get-tuple-element.311), channel_id=1, source_target_pairs={{0,3},{1,0},{2,1},{3,2},{4,7},{5,4},{6,5},{7,6},{8,11},{9,8},{10,9... | collective-permute-start | bytes 786440 | tf_op jit(solution)/shard_map/ppermute | solution.py:621
  (132 other events, 1713.3 us)
Sparse Core Ops, SparseCore 0:
  35.9 73.9 all-gather.4
  126.7 43.5 all-gather.6
  172.4 106.4 all-gather.8
  280.9 59.3 all-gather.10
  360.2 56.3 reduce-scatter.5
  425.1 56.0 reduce-scatter.7
  484.1 82.4 reduce-scatter.9
  626.7 45.3 reduce-scatter.11
  690.1 33.8 reduce-scatter.13

commit v2 on v1

--- a/solution.py
+++ b/solution.py
@@ -194,8 +194,8 @@
         input_output_aliases={slots + 4 + i: i for i in range(len(kept))},
         compiler_params=pltpu.CompilerParams(vmem_limit_bytes=VMEM_LIMIT),
         cost_estimate=pl.CostEstimate(
-            flops=6 * slots * block * depth * width,
-            bytes_accessed=3 * width * depth * 2 + 8 * slots * block * width,
+            flops=slots * block * depth * width,
+            bytes_accessed=8 * slots * block * width,
             transcendentals=0,
         ),
         name="widen_back",
@@ -790,23 +790,25 @@
     own_starts = document_starts(segments[0])
     other_starts = document_starts(other_segments[0])
     frequency = 10000.0 ** (-2.0 * jnp.arange(HEAD_DIM // 2, dtype=jnp.float32) / HEAD_DIM)
-    starts, places, meta = ([], [], [])
-    for slot in range(slots):
-        begin = slot_row[slot] * (lines * block) + line * block
-        of_chunk = lax.dynamic_slice_in_dim(
-            jnp.where(slot_y[slot] == y, own_starts, other_starts), begin, block, 0
-        )
-        starts.append(of_chunk)
-        places.append(begin + jnp.arange(block, dtype=jnp.int32))
-        meta += [of_chunk[0] // block, begin // block]
+    slot_y, slot_row = (jnp.stack(slot_y).astype(jnp.int32), jnp.stack(slot_row).astype(jnp.int32))
+    begins = slot_row * (lines * block) + line * block
+    places = begins[:, None] + jnp.arange(block, dtype=jnp.int32)[None, :]
+    both_starts = jnp.stack([own_starts, other_starts]).reshape(2, rows_on, lines, block)
+    both_starts = lax.dynamic_index_in_dim(both_starts, line, 2, keepdims=False)
+    starts = jnp.zeros((slots, block), jnp.int32)
+    for which in range(2):
         for row_at in range(rows_on):
-            found = jnp.int32(0)
-            for other in range(slots):
-                same = (slot_y[other] == slot_y[slot]) & (slot_row[other] == row_at)
-                found = found + jnp.where(same, other, 0)
-            meta.append(found)
-    meta = jnp.stack([jnp.asarray(m, jnp.int32) for m in meta + [line]])
-    starts, places = (jnp.stack(starts), jnp.stack(places))
+            here = ((slot_y != y) == bool(which)) & (slot_row == row_at)
+            starts = jnp.where(here[:, None], both_starts[which, row_at][None, :], starts)
+    same_y = slot_y[:, None] == slot_y[None, :]
+    at_row = slot_row[None, :] == jnp.arange(rows_on, dtype=jnp.int32)[:, None]
+    found = jnp.where(
+        same_y[:, None, :] & at_row[None, :, :], jnp.arange(slots, dtype=jnp.int32), 0
+    ).sum(axis=2)
+    meta = jnp.concatenate(
+        [(starts[:, :1] // block), (begins // block)[:, None], found.astype(jnp.int32)], axis=1
+    )
+    meta = jnp.concatenate([meta.reshape(-1), line[None].astype(jnp.int32)])
     info = jnp.stack([places, starts], axis=1)
     offsets = (places - starts).astype(jnp.float32).reshape(-1)
     phases = offsets[:, None] * jnp.tile(frequency, LANES // (HEAD_DIM // 2))[None, :]
@@ -824,8 +826,8 @@
     cot_chunks = gather_tokens(cot_low)
     queries, pair = project(normed_parts, first_weight, joint_width, cosine, sine, query_width)
     pairs = lax.all_gather(pair.reshape(slots, block, 2 * LANES), "col", axis=0, tiled=False)
-    pairs, cot_chunks, gateup_mine, down_mine = lax.optimization_barrier(
-        (pairs, cot_chunks, gateup_mine, down_mine)
+    pairs, cot_chunks, gateup_mine, down_mine, meta, info = lax.optimization_barrier(
+        (pairs, cot_chunks, gateup_mine, down_mine, meta, info)
     )
     gateup_weight = gather_weight(gateup_mine)
     down_weight = gather_weight(down_mine)
@@ -839,7 +841,7 @@
 
     def other_half(rows, grad):
         rows = lax.dynamic_slice_in_dim(rows, (1 - core) * (D // 2), D // 2, 1)
-        return other_core(dot_tn(rows, grad).astype(jnp.bfloat16))
+        return dot_tn(rows, grad).astype(jnp.bfloat16)
 
     def own_half(rows, grad, received):
         rows = lax.dynamic_slice_in_dim(rows, core * (D // 2), D // 2, 1)
@@ -853,7 +855,7 @@
         near_y = other_y(piece)
         return [piece, near_y, other_core(piece), other_core(near_y)]
 
-    down_total = own_half(cot, hidden, other_half(cot, hidden))
+    down_total = own_half(cot, hidden, other_core(other_half(cot, hidden)))
     down_total, down_weight = lax.optimization_barrier((down_total, down_weight))
     down_piece = scatter(down_total)
     work = {}
@@ -871,10 +873,11 @@
         return partial
 
     def feed_others(key):
-        key, rows, gate, up = lax.optimization_barrier(
-            (key, normed_two, work["grad_gate"], work["grad_up"])
-        )
-        work["feed"] = (rows, gate, up, other_half(rows, gate), other_half(rows, up))
+        gate, up = (work["grad_gate"], work["grad_up"])
+        key, gate_other, up_other = lax.optimization_barrier(
+            (key, other_half(normed_two, gate), other_half(normed_two, up))
+        )
+        work["feed"] = (normed_two, gate, up, other_core(gate_other), other_core(up_other))
         return key
 
     def feed_owns(first):
@@ -944,7 +947,6 @@
     grad_query, gate_piece, back, mixed = [
         work[name] for name in ("grad_query", "gate_piece", "back", "mixed")
     ]
-    output_total = own_half(back, mixed, other_half(back, mixed))
     output_parts = features_sent((middle + ffn_sum).astype(jnp.bfloat16))
     grad_keyvalue = pair_back(work["grad_parts"], cosine, sine, block)
     grad_joint = jnp.concatenate([grad_query, grad_keyvalue], axis=1)
@@ -962,20 +964,23 @@
             FF ** (-0.5),
             False,
         )
+        output_total = own_half(back, mixed, other_core(other_half(back, mixed)))
         close, work["output"], work["down_new"] = lax.optimization_barrier(
             (product(grad_joint, joint_weight)(first, last), output_total, down_new)
         )
         return close
 
     def joint_others(key):
-        key, rows, grad = lax.optimization_barrier((key, normed_one, grad_joint))
-        work["joint"] = (rows, grad, other_half(rows, grad))
+        key, work["output_parts"], other = lax.optimization_barrier(
+            (key, output_parts, other_half(normed_one, grad_joint))
+        )
+        work["joint"] = (normed_one, grad_joint, other_core(other))
         work["output_piece"] = scatter(work["output"])
         return key
 
     def joint_owns(first):
-        first, work["output_piece"], work["output_parts"], rows, grad, other = (
-            lax.optimization_barrier((first, work["output_piece"], output_parts, *work["joint"]))
+        first, work["output_piece"], rows, grad, other = lax.optimization_barrier(
+            (first, work["output_piece"], *work["joint"])
         )
         work["joint_total"] = own_half(rows, grad, other)
         return first
@@ -991,8 +996,8 @@
     )
     input_grad = grad_middle + norm_back(residual, scale_one, grad_normed_one, gains[0])
     gain_one = jnp.sum(grad_normed_one * residual * scale_one, axis=0)
-    input_parts, gateup_new = lax.optimization_barrier(
-        (features_sent(input_grad.astype(jnp.bfloat16)), gateup_new)
+    joint_piece, input_parts, gateup_new = lax.optimization_barrier(
+        (joint_piece, features_sent(input_grad.astype(jnp.bfloat16)), gateup_new)
     )
     layer_output = features_of(work["output_parts"])
     input_grad = features_of(input_parts).astype(jnp.float32)

time: 799 us -> 818 us (1.024)
  waiting for transfers between devices: 294 us -> 341 us
  local copies, waits for them, and re-layouts: 55.8 us -> 72.7 us
  starting transfers between devices: 91.3 us -> 75.2 us
  Pallas kernels: 179 us -> 167 us
  between operations: 26.7 us -> 15.9 us
    ppermute x25, waiting for transfers between devices: 106 us -> 138 us  [shift(): lax.ppermute(value, axis, [(i, (i + by) % size) for i in range(size)])]
    reduce_scatter x5, waiting for transfers between devices: 27.4 us -> 0.03 us  [scatter(): return lax.psum_scatter(total, 'col', scatter_dimension=0, tiled=True)]
    ppermute x5, waiting for transfers between devices: 0.01 us -> 25.9 us  [other_y(): return lax.ppermute(value, 'y', [(0, 1), (1, 0)])]
    unnamed x187 -> x213, local copies, waits for them, and re-layouts: 27.2 us -> 45.5 us
    all_gather x3, waiting for transfers between devices: 5.35 us -> 22.8 us  [gather_weight(): return lax.all_gather(piece, ('core', 'col'), axis=0, tiled=True)]
    ppermute x13, starting transfers between devices: 31.3 us -> 14.2 us  [other_core(): return lax.ppermute(value, 'core', [(0, 1), (1, 0)])]
    ppermute x4, waiting for transfers between devices: 10.9 us -> 20.9 us  [gather_tokens(): third = lax.ppermute(first, near, second_pairs)]
  transfers between devices with their start and end apart: 76 -> 76, of which waited for: 35 -> 31; matrix products, arithmetic and copies ran while one was open for 20% -> 20% of each run, Pallas kernels for 19% -> 19%
where the time goes in v2:
time: 818 us; the launch traced here: 803 us
  waiting for transfers between devices  341 us (42%)
  Pallas kernels  167 us (20%)
  matrix products  85.5 us (10%)
  starting transfers between devices  75.2 us (9%)
  local copies, waits for them, and re-layouts  72.7 us (9%)
  other arithmetic  45.9 us (6%)
  between operations  15.9 us (2%)
    ppermute x25, waiting for transfers between devices, shift(): lax.ppermute(value, axis, [(i, (i + by) % size) for i in range(size)])  138 us
    ppermute x4, waiting for transfers between devices, gather_tokens(): first = lax.ppermute(own, near, first_pairs)  70.3 us
    dot_general x10, matrix products, dot_tn(): lax.dot_general(left, right, (((0,), (0,)), ((), ())), preferred_element_...  54.6 us
    unnamed x213, local copies, waits for them, and re-layouts  45.5 us
    ppermute x25, starting transfers between devices, shift(): lax.ppermute(value, axis, [(i, (i + by) % size) for i in range(size)])  37.6 us
    pallas_call x1, Pallas kernels, gateup_update(): pl.pallas_call(gateup_update_kernel, grid_spec=pltpu.PrefetchScalarGridSp...  36.5 us
    pallas_call x2, Pallas kernels, widen_back(): pl.pallas_call(functools.partial(widen_back_kernel, slots, len(kept)), gr...  34.9 us
    dot_general x6, matrix products, dot_nt(): lax.dot_general(left, right, (((1,), (1,)), ((), ())), preferred_element_...  25.9 us
  transfers between devices with their start and end apart: 76, of which 31 were waited for; matrix products, arithmetic and copies ran while one was open for 20% of the time, Pallas kernels for 19%

profile of v2, /device:TPU:11, one launch (start us, length us, event | category | flops | bytes accessed | tf_op | source)
XLA Modules:
  0.0 803.3 jit_solution(10658839150535182049)
XLA Ops:
  47.5 20.1 %collective-permute-done.7.refs_1_ = bf16[256,2048]{1,0:T(8,128)(2,1)S(1)} collective-permute-done((bf16[256,2048]{1,0:T(8,128)(2,1)S(1)}, bf16[256,2048]{1,0:T(8,128)(2,1)S(1)}, u32[]{:S(2)}, u32[]{:S(2)}) %collective-permute-start.7) | collective-permute-done | bytes 1048608 | tf_op jit(solution)/shard_map/ppermute | solution.py:647
  80.3 13.4 %collective-permute-done.10 = bf16[256,512]{1,0:T(8,128)(2,1)} collective-permute-done((bf16[256,512]{1,0:T(8,128)(2,1)}, bf16[256,512]{1,0:T(8,128)(2,1)}, u32[]{:S(2)}, u32[]{:S(2)}) %collective-permute-start.10) | collective-permute-done | bytes 262176 | tf_op jit(solution)/shard_map/ppermute | solution.py:621
  93.7 17.7 %collective-permute-done.11 = bf16[256,512]{1,0:T(8,128)(2,1)} collective-permute-done((bf16[256,512]{1,0:T(8,128)(2,1)}, bf16[256,512]{1,0:T(8,128)(2,1)}, u32[]{:S(2)}, u32[]{:S(2)}) %collective-permute-start.11) | collective-permute-done | bytes 262176 | tf_op jit(solution)/shard_map/ppermute | solution.py:621
  134.8 19.8 %collective-permute-done.13.refs_1_ = bf16[256,2048]{1,0:T(8,128)(2,1)S(1)} collective-permute-done((bf16[256,2048]{1,0:T(8,128)(2,1)S(1)}, bf16[256,2048]{1,0:T(8,128)(2,1)S(1)}, u32[]{:S(2)}, u32[]{:S(2)}) %collective-permute-start.13) | collective-permute-done | bytes 1048608 | tf_op jit(solution)/shard_map/ppermute | solution.py:647
  174.8 12.7 %attend.1 = (bf16[1024,512]{1,0:T(8,128)(2,1)S(1)}, f32[4,2,1024]{2,1,0:T(2,128)S(1)}) custom-call(s32[17]{0:T(128)S(1)} %pad_add_fusion.7.meta_ref, bf16[1024,512]{1,0:T(8,128)(2,1)S(1)} %copy-done.41, bf16[4,4,256,256]{3,2,1,0:T(8,128)(2,1)S(1)} %copy-done.39, s32[4,2,256]{2,1,0:T(2,128)S(1)} %pad_add_fusion.2.info_ref.refs_4_), custom_call_target="tpu_custom_call" | custom-call | flops 3221225472 | bytes 4194304 | tf_op jit(solution)/shard_map/attend/pallas_call | solution.py:274
  197.0 9.6 %collective-permute-done.16 = bf16[256,2048]{1,0:T(8,128)(2,1)} collective-permute-done((bf16[256,2048]{1,0:T(8,128)(2,1)}, bf16[256,2048]{1,0:T(8,128)(2,1)}, u32[]{:S(2)}, u32[]{:S(2)}) %collective-permute-start.16) | collective-permute-done | bytes 1048608 | tf_op jit(solution)/shard_map/ppermute | solution.py:664
  206.6 11.2 %collective-permute-done.17 = bf16[256,2048]{1,0:T(8,128)(2,1)} collective-permute-done((bf16[256,2048]{1,0:T(8,128)(2,1)}, bf16[256,2048]{1,0:T(8,128)(2,1)}, u32[]{:S(2)}, u32[]{:S(2)}) %collective-permute-start.17) | collective-permute-done | bytes 1048608 | tf_op jit(solution)/shard_map/ppermute | solution.py:665
  220.8 12.8 %collective-permute-done.18 = bf16[256,2048]{1,0:T(8,128)(2,1)S(1)} collective-permute-done((bf16[256,2048]{1,0:T(8,128)(2,1)S(1)}, bf16[256,2048]{1,0:T(8,128)(2,1)S(1)}, u32[]{:S(2)}, u32[]{:S(2)}) %collective-permute-start.18) | collective-permute-done | bytes 1048608 | tf_op jit(solution)/shard_map/ppermute | solution.py:670
  238.3 18.3 %collective-permute-done.19.refs_1_ = bf16[256,2048]{1,0:T(8,128)(2,1)} collective-permute-done((bf16[256,2048]{1,0:T(8,128)(2,1)S(1)}, bf16[256,2048]{1,0:T(8,128)(2,1)}, u32[]{:S(2)}, u32[]{:S(2)}) %collective-permute-start.19) | collective-permute-done | bytes 1048608 | tf_op jit(solution)/shard_map/ppermute | solution.py:647
  282.7 19.8 %widen.1 = (bf16[1024,1408]{1,0:T(8,128)(2,1)}, bf16[1024,1408]{1,0:T(8,128)(2,1)}, bf16[1024,1408]{1,0:T(8,128)(2,1)}) custom-call(bf16[256,2048]{1,0:T(8,128)(2,1)S(1)} %copy-done.2, bf16[256,2048]{1,0:T(8,128)(2,1)} %collective-permute-done.19.refs_1_, bf16[256,2048]{1,0:T(8,128)(2,1)S(1)} %copy-done.28, ...), custom_call_target="tpu_custom_call" | custom-call | flops 11811160064 | bytes 24379392 | tf_op jit(solution)/shard_map/widen/pallas_call | solution.py:141
  324.1 17.5 %all-gather.11.cloned.1.call-done.refs_2_ = bf16[2048,1408]{1,0:T(8,128)(2,1)} async-done(((bf16[256,1408]{1,0:T(8,128)(2,1)}), bf16[2048,1408]{1,0:T(8,128)(2,1)}) %all-gather.11.cloned.1.call-update) | async-done | bytes 5767184 | tf_op jit(solution)/shard_map/all_gather | solution.py:740
  344.4 18.4 %widen_back.2 = (bf16[1024,1408]{1,0:T(8,128)(2,1)}, bf16[1024,1408]{1,0:T(8,128)(2,1)}, bf16[512,2048]{1,0:T(8,128)(2,1)S(1)}) custom-call(bf16[256,2048]{1,0:T(8,128)(2,1)S(1)} %collective-permute-done.14.refs_0_, bf16[256,2048]{1,0:T(8,128)(2,1)S(1)} %collective-permute-done.15.refs_1_, bf16[2048,1408]{1,0:T(8,128)(2,1)} %all-gather.11.cloned.1.call-done.refs_2_, ...), custom_call_target="tpu_custom_call" | custom-call | flops 1476395008 | bytes 5767168 | tf_op jit(solution)/shard_map/widen_back/pallas_call | solution.py:179
  364.6 16.5 %widen_back.3 = (bf16[1024,1408]{1,0:T(8,128)(2,1)}, bf16[1024,1408]{1,0:T(8,128)(2,1)}, bf16[512,2048]{1,0:T(8,128)(2,1)S(1)}) custom-call(bf16[256,2048]{1,0:T(8,128)(2,1)S(1)} %slice_dynamic-update-slice_fusion.refs_0_, bf16[256,2048]{1,0:T(8,128)(2,1)S(1)} %copy-done.5, ...), custom_call_target="tpu_custom_call", output_to_operand_aliasing={{0}: (6, {}), {1}: (7, {})} | custom-call | flops 1476395008 | bytes 5767168 | tf_op jit(solution)/shard_map/widen_back/pallas_call | solution.py:179
  393.3 12.9 %collective-permute-done.25 = bf16[256,2048]{1,0:T(8,128)(2,1)} collective-permute-done((bf16[256,2048]{1,0:T(8,128)(2,1)S(1)}, bf16[256,2048]{1,0:T(8,128)(2,1)}, u32[]{:S(2)}, u32[]{:S(2)}) %collective-permute-start.25) | collective-permute-done | bytes 1048608 | tf_op jit(solution)/shard_map/ppermute | solution.py:670
  436.8 12.1 %collective-permute-done.28 = bf16[256,2048]{1,0:T(8,128)(2,1)S(1)} collective-permute-done((bf16[256,2048]{1,0:T(8,128)(2,1)}, bf16[256,2048]{1,0:T(8,128)(2,1)S(1)}, u32[]{:S(2)}, u32[]{:S(2)}) %collective-permute-start.28) | collective-permute-done | bytes 1048608 | tf_op jit(solution)/shard_map/ppermute | solution.py:647
  474.8 24.3 %attend_back.1 = (bf16[1024,512]{1,0:T(8,128)(2,1)S(1)}, bf16[4,256,256]{2,1,0:T(8,128)(2,1)S(1)}, bf16[4,256,256]{2,1,0:T(8,128)(2,1)}, bf16[4,256,256]{2,1,0:T(8,128)(2,1)}, bf16[4,256,256]{2,1,0:T(8,128)(2,1)}) custom-call(s32[17]{0:T(128)S(1)} %pad_add_fusion.7.meta_ref, bf16[1024,512]{1,0:T(8,128)(2,1)S(1)} %copy-done.42, ...), custom_call_target="tpu_custom_call" | custom-call | flops 8053063680 | bytes 8388608 | tf_op jit(solution)/shard_map/attend_back/pallas_call | solution.py:378
  520.8 20.5 %collective-permute-done.34.refs_1_ = bf16[1024,256]{1,0:T(8,128)(2,1)S(1)} collective-permute-done((bf16[1024,256]{1,0:T(8,128)(2,1)}, bf16[1024,256]{1,0:T(8,128)(2,1)S(1)}, u32[]{:S(2)}, u32[]{:S(2)}) %collective-permute-start.34) | collective-permute-done | bytes 524320 | tf_op jit(solution)/shard_map/ppermute | solution.py:621
  547.5 15.3 %collective-permute-done.35.refs_2_ = bf16[1024,256]{1,0:T(8,128)(2,1)S(1)} collective-permute-done((bf16[1024,256]{1,0:T(8,128)(2,1)}, bf16[1024,256]{1,0:T(8,128)(2,1)S(1)}, u32[]{:S(2)}, u32[]{:S(2)}) %collective-permute-start.35) | collective-permute-done | bytes 524320 | tf_op jit(solution)/shard_map/ppermute | solution.py:621
  564.3 9.8 %collective-permute-done.36.refs_3_ = bf16[1024,256]{1,0:T(8,128)(2,1)S(1)} collective-permute-done((bf16[1024,256]{1,0:T(8,128)(2,1)}, bf16[1024,256]{1,0:T(8,128)(2,1)S(1)}, u32[]{:S(2)}, u32[]{:S(2)}) %collective-permute-start.36) | collective-permute-done | bytes 524320 | tf_op jit(solution)/shard_map/ppermute | solution.py:621
  612.0 15.0 %turned_update.2 = (f32[2816,512]{1,0:T(8,128)}, f32[2816,512]{1,0:T(8,128)}, f32[2816,512]{1,0:T(8,128)}) custom-call(s32[2]{0:T(128)S(1)} %pad_add_fusion.8.meta_ref, bf16[512,1408]{1,0:T(8,128)(2,1)S(1)} %constant_dynamic-update-slice_fusion.12.refs_0_, bf16[512,1408]{1,0:T(8,128)(2,1)S(1)} %collective-permute-done.40.refs_1_, ...), custom_call_target="tpu_custom_call" | custom-call | flops 28835840 | bytes 34603008 | tf_op jit(solution)/shard_map/turned_update/pallas_call | solution.py:531
  633.4 25.8 %collective-permute-done.51.refs_5_ = bf16[256,1408]{1,0:T(8,128)(2,1)} collective-permute-done((bf16[256,1408]{1,0:T(8,128)(2,1)}, bf16[256,1408]{1,0:T(8,128)(2,1)}, u32[]{:S(2)}, u32[]{:S(2)}) %collective-permute-start.51) | collective-permute-done | bytes 720928 | tf_op jit(solution)/shard_map/ppermute | solution.py:627
  678.3 43.1 %collective-permute-done.56 = f32[2,512]{1,0:T(2,128)S(1)} collective-permute-done((f32[2,512]{1,0:T(2,128)S(1)}, f32[2,512]{1,0:T(2,128)S(1)}, u32[]{:S(2)}, u32[]{:S(2)}) %collective-permute-start.56) | collective-permute-done | bytes 4128 | tf_op jit(solution)/shard_map/ppermute | solution.py:621
  721.6 36.5 %gateup_update.1 = (f32[512,2,2816]{2,1,0:T(2,128)}, f32[512,2,2816]{2,1,0:T(2,128)}, f32[512,2,2816]{2,1,0:T(2,128)}) custom-call(s32[2]{0:T(128)S(1)} %pad_add_fusion.8.meta_ref, bf16[512,1408]{1,0:T(8,128)(2,1)S(1)} %constant_dynamic-update-slice_fusion.12.refs_0_, bf16[512,1408]{1,0:T(8,128)(2,1)S(1)} %collective-permute-done.40.refs_1_, ...), custom_call_target="tpu_custom_call" | custom-call | flops 57671680 | bytes 80740352 | tf_op jit(solution)/shard_map/gateup_update/pallas_call | solution.py:568
  787.0 9.5 %joint_update.1 = (f32[512,1024]{1,0:T(8,128)}, f32[512,1024]{1,0:T(8,128)}, f32[512,1024]{1,0:T(8,128)}, f32[512,512]{1,0:T(8,128)}, f32[512,512]{1,0:T(8,128)}, /*index=5*/f32[512,512]{1,0:T(8,128)}) custom-call(s32[2]{0:T(128)S(1)} %pad_add_fusion.8.meta_ref, bf16[256,768]{1,0:T(8,128)(2,1)S(1)} %pad_maximum_fusion.12.refs_0_, ...), custom_call_target="tpu_custom_call" | custom-call | flops 15728640 | bytes 18874368 | tf_op jit(solution)/shard_map/joint_update/pallas_call | solution.py:489
  (520 shorter events, 354.8 us)
Async XLA Ops:
  7.2 108.9 %all-gather.5.cloned.1.call-start = ((), (), s32[]{:S(2)}) async-start(), calls=%async_computation.5 | async-start | bytes 5898240 | tf_op jit(solution)/shard_map/all_gather | solution.py:740
  35.7 135.8 %all-gather.7.cloned.1.call-start = ((), (), s32[]{:S(2)}) async-start(), calls=%async_computation.6 | async-start | bytes 2621440 | tf_op jit(solution)/shard_map/all_gather | solution.py:828
  71.6 42.2 %collective-permute-start.9 = (bf16[256,2048]{1,0:T(8,128)(2,1)S(1)}, bf16[256,2048]{1,0:T(8,128)(2,1)}, u32[]{:S(2)}, u32[]{:S(2)}) collective-permute-start(bf16[256,2048]{1,0:T(8,128)(2,1)S(1)} %collective-permute-done.7.refs_1_), channel_id=1, source_target_pairs={{0,16},{4,20},{8,12},{12,8},{16,0},{20,4},{24,28},{28,24},{1,17},{... | collective-permute-start | bytes 3145736 | tf_op jit(solution)/shard_map/ppermute | solution.py:650
  74.2 37.2 %collective-permute-start.11 = (bf16[256,512]{1,0:T(8,128)(2,1)}, bf16[256,512]{1,0:T(8,128)(2,1)}, u32[]{:S(2)}, u32[]{:S(2)}) collective-permute-start(bf16[256,512]{1,0:T(8,128)(2,1)} %get-tuple-element.337), channel_id=1, source_target_pairs={{0,2},{1,3},{2,0},{3,1},{4,6},{5,7},{6,4},{7,5},{8,10},{9,11},{10,... | collective-permute-start | bytes 786440 | tf_op jit(solution)/shard_map/ppermute | solution.py:621
  128.0 152.2 %all-gather.9.cloned.1.call-start = ((), (), s32[]{:S(2)}) async-start(), calls=%async_computation.7 | async-start | bytes 12976128 | tf_op jit(solution)/shard_map/all_gather | solution.py:740
  171.6 170.1 %all-gather.11.cloned.1.call-start = ((), (), s32[]{:S(2)}) async-start(), calls=%async_computation.8 | async-start | bytes 6488064 | tf_op jit(solution)/shard_map/all_gather | solution.py:740
  193.9 213.9 %reduce-scatter.6.cloned.1.call-start = ((), (), s32[]{:S(2)}) async-start(), calls=%async_computation.9 | async-start | bytes 3604480 | tf_op jit(solution)/shard_map/reduce_scatter | solution.py:852
  341.7 159.2 %reduce-scatter.8.cloned.1.call-start = ((), (), s32[]{:S(2)}) async-start(), calls=%async_computation.10 | async-start | bytes 3604480 | tf_op jit(solution)/shard_map/reduce_scatter | solution.py:852
  416.1 158.7 %reduce-scatter.10.cloned.1.call-start = ((), (), s32[]{:S(2)}) async-start(), calls=%async_computation.11 | async-start | bytes 3604480 | tf_op jit(solution)/shard_map/reduce_scatter | solution.py:852
  433.5 225.8 %reduce-scatter.12.cloned.1.call-start = ((), (), s32[]{:S(2)}) async-start(), calls=%async_computation.12 | async-start | bytes 1310720 | tf_op jit(solution)/shard_map/reduce_scatter | solution.py:852
  503.7 71.2 %collective-permute-start.33 = (bf16[256,2048]{1,0:T(8,128)(2,1)}, bf16[256,2048]{1,0:T(8,128)(2,1)}, u32[]{:S(2)}, u32[]{:S(2)}) collective-permute-start(bf16[256,2048]{1,0:T(8,128)(2,1)} %add_convert_fusion.7), channel_id=1, source_target_pairs={{0,4},{4,0},{8,24},{12,28},{16,20},{20,16},{24,8},{28,12},{1,5},{5... | collective-permute-start | bytes 3145736 | tf_op jit(solution)/shard_map/ppermute | solution.py:670
  506.3 56.6 %collective-permute-start.35 = (bf16[1024,256]{1,0:T(8,128)(2,1)}, bf16[1024,256]{1,0:T(8,128)(2,1)S(1)}, u32[]{:S(2)}, u32[]{:S(2)}) collective-permute-start(bf16[1024,256]{1,0:T(8,128)(2,1)} %bitcast.52), channel_id=1, source_target_pairs={{0,2},{1,3},{2,0},{3,1},{4,6},{5,7},{6,4},{7,5},{8,10},{9,11},{10,... | collective-permute-start | bytes 1572872 | tf_op jit(solution)/shard_map/ppermute | solution.py:621
  514.8 59.3 %collective-permute-start.36 = (bf16[1024,256]{1,0:T(8,128)(2,1)}, bf16[1024,256]{1,0:T(8,128)(2,1)S(1)}, u32[]{:S(2)}, u32[]{:S(2)}) collective-permute-start(bf16[1024,256]{1,0:T(8,128)(2,1)} %bitcast.53), channel_id=1, source_target_pairs={{0,1},{1,2},{2,3},{3,0},{4,5},{5,6},{6,7},{7,4},{8,9},{9,10},{10,1... | collective-permute-start | bytes 1572872 | tf_op jit(solution)/shard_map/ppermute | solution.py:621
  517.1 73.5 %collective-permute-start.40 = (bf16[512,1408]{1,0:T(8,128)(2,1)S(1)}, bf16[512,1408]{1,0:T(8,128)(2,1)S(1)}, u32[]{:S(2)}, u32[]{:S(2)}) collective-permute-start(bf16[512,1408]{1,0:T(8,128)(2,1)S(1)} %constant_dynamic-update-slice_fusion.12.refs_0_), channel_id=1, source_target_pairs={{0,16},{16,0},{1,17},{17,1},{2,18},{18,2},{3,19},{19,3},{4,20},{20... | collective-permute-start | bytes 4325384 | tf_op jit(solution)/shard_map/ppermute | solution.py:627
  542.1 66.1 %collective-permute-start.41 = (bf16[512,1408]{1,0:T(8,128)(2,1)S(1)}, bf16[512,1408]{1,0:T(8,128)(2,1)}, u32[]{:S(2)}, u32[]{:S(2)}) collective-permute-start(bf16[512,1408]{1,0:T(8,128)(2,1)S(1)} %constant_dynamic-update-slice_fusion.12.refs_0_), channel_id=1, source_target_pairs={{0,8},{8,0},{1,9},{9,1},{2,10},{10,2},{3,11},{11,3},{4,12},{12,4},... | collective-permute-start | bytes 4325384 | tf_op jit(solution)/shard_map/ppermute | solution.py:624
  586.8 40.2 %collective-permute-start.37 = (bf16[256,2048]{1,0:T(8,128)(2,1)}, bf16[256,2048]{1,0:T(8,128)(2,1)}, u32[]{:S(2)}, u32[]{:S(2)}) collective-permute-start(bf16[256,2048]{1,0:T(8,128)(2,1)} %get-tuple-element.291), channel_id=1, source_target_pairs={{0,16},{4,20},{8,12},{12,8},{16,0},{20,4},{24,28},{28,24},{1,17},{... | collective-permute-start | bytes 3145736 | tf_op jit(solution)/shard_map/ppermute | solution.py:664
  587.0 39.9 %collective-permute-start.38 = (bf16[256,2048]{1,0:T(8,128)(2,1)}, bf16[256,2048]{1,0:T(8,128)(2,1)}, u32[]{:S(2)}, u32[]{:S(2)}) collective-permute-start(bf16[256,2048]{1,0:T(8,128)(2,1)} %get-tuple-element.290), channel_id=1, source_target_pairs={{0,16},{4,20},{8,12},{12,8},{16,0},{20,4},{24,28},{28,24},{1,17},{... | collective-permute-start | bytes 3145736 | tf_op jit(solution)/shard_map/ppermute | solution.py:665
  627.0 133.4 %reduce-scatter.14.cloned.1.call-start = ((), (), s32[]{:S(2)}) async-start(), calls=%async_computation.13 | async-start | bytes 1966080 | tf_op jit(solution)/shard_map/reduce_scatter | solution.py:852
  631.5 44.0 %collective-permute-start.52 = (bf16[256,1408]{1,0:T(8,128)(2,1)}, bf16[256,1408]{1,0:T(8,128)(2,1)}, u32[]{:S(2)}, u32[]{:S(2)}) collective-permute-start(bf16[256,1408]{1,0:T(8,128)(2,1)} %reduce-scatter.10.cloned.1.call-done.refs_4_), channel_id=1, source_target_pairs={{0,8},{8,0},{1,9},{9,1},{2,10},{10,2},{3,11},{11,3},{4,12},{12,4},... | collective-permute-start | bytes 2162696 | tf_op jit(solution)/shard_map/ppermute | solution.py:624
  672.0 87.0 %collective-permute-start.48 = (bf16[256,512]{1,0:T(8,128)(2,1)S(1)}, bf16[256,512]{1,0:T(8,128)(2,1)S(1)}, u32[]{:S(2)}, u32[]{:S(2)}) collective-permute-start(bf16[256,512]{1,0:T(8,128)(2,1)S(1)} %get-tuple-element.306), channel_id=1, source_target_pairs={{0,1},{1,2},{2,3},{3,0},{4,5},{5,6},{6,7},{7,4},{8,9},{9,10},{10,1... | collective-permute-start | bytes 786440 | tf_op jit(solution)/shard_map/ppermute | solution.py:621
  673.8 85.2 %collective-permute-start.49 = (bf16[256,512]{1,0:T(8,128)(2,1)S(1)}, bf16[256,512]{1,0:T(8,128)(2,1)S(1)}, u32[]{:S(2)}, u32[]{:S(2)}) collective-permute-start(bf16[256,512]{1,0:T(8,128)(2,1)S(1)} %get-tuple-element.305), channel_id=1, source_target_pairs={{0,2},{1,3},{2,0},{3,1},{4,6},{5,7},{6,4},{7,5},{8,10},{9,11},{10,... | collective-permute-start | bytes 786440 | tf_op jit(solution)/shard_map/ppermute | solution.py:621
  675.4 85.0 %collective-permute-start.50 = (bf16[256,512]{1,0:T(8,128)(2,1)S(1)}, bf16[256,512]{1,0:T(8,128)(2,1)}, u32[]{:S(2)}, u32[]{:S(2)}) collective-permute-start(bf16[256,512]{1,0:T(8,128)(2,1)S(1)} %get-tuple-element.304), channel_id=1, source_target_pairs={{0,3},{1,0},{2,1},{3,2},{4,7},{5,4},{6,5},{7,6},{8,11},{9,8},{10,9... | collective-permute-start | bytes 786440 | tf_op jit(solution)/shard_map/ppermute | solution.py:621
  675.5 45.8 %collective-permute-start.56 = (f32[2,512]{1,0:T(2,128)S(1)}, f32[2,512]{1,0:T(2,128)S(1)}, u32[]{:S(2)}, u32[]{:S(2)}) collective-permute-start(f32[2,512]{1,0:T(2,128)S(1)} %get-tuple-element.379), channel_id=1, source_target_pairs={{0,3},{1,0},{2,1},{3,2},{4,7},{5,4},{6,5},{7,6},{8,11},{9,8},{10,9... | collective-permute-start | bytes 12296 | tf_op jit(solution)/shard_map/ppermute | solution.py:621
  677.6 80.6 %collective-permute-start.55 = (f32[2,512]{1,0:T(2,128)S(1)}, f32[2,512]{1,0:T(2,128)S(1)}, u32[]{:S(2)}, u32[]{:S(2)}) collective-permute-start(f32[2,512]{1,0:T(2,128)S(1)} %get-tuple-element.380), channel_id=1, source_target_pairs={{0,2},{1,3},{2,0},{3,1},{4,6},{5,7},{6,4},{7,5},{8,10},{9,11},{10,... | collective-permute-start | bytes 12296 | tf_op jit(solution)/shard_map/ppermute | solution.py:621
  (143 other events, 1764.1 us)
Sparse Core Ops, SparseCore 0:
  35.9 71.3 all-gather.4
  128.1 43.4 all-gather.6
  173.8 106.3 all-gather.8
  282.2 59.4 all-gather.10
  343.8 55.8 reduce-scatter.5
  416.3 56.7 reduce-scatter.7
  476.0 82.0 reduce-scatter.9
  627.1 25.5 reduce-scatter.11
  665.0 56.9 reduce-scatter.13

commit v3 on v2

--- a/solution.py
+++ b/solution.py
@@ -228,35 +228,36 @@
     base = chunk * (2 + parts)
     steps = meta_ref[base + 1] - meta_ref[base] + 1
     width = heads * block
-    outs = []
-    for which in range(2):
-        is_key = (lane < HEAD_DIM) if which == 0 else (lane >= HEAD_DIM)
-        queries = jnp.where(is_key, stacked, jnp.zeros_like(stacked))
-
-        def body(step, carry):
-            peak, total, mixed = carry
-            key_block, slot, at, _ = block_of(meta_ref, chunk, step, parts, lines)
+    key_lanes = lane < HEAD_DIM
+    queries = [
+        jnp.where(key_lanes if which == 0 else ~key_lanes, stacked, jnp.zeros_like(stacked))
+        for which in range(2)
+    ]
+
+    def body(step, carry):
+        key_block, slot, at, _ = block_of(meta_ref, chunk, step, parts, lines)
+        key_place = key_block * block + lax.broadcasted_iota(jnp.int32, (block, width), 0)
+        seen = (key_place <= place) & (key_place >= start)
+        result = []
+        for which in range(2):
+            peak, total, mixed = carry[which]
             pair = pair_ref[at, slot, :, which * LANES : (which + 1) * LANES]
-            scores = dot_nt(pair, queries)
-            key_place = key_block * block + lax.broadcasted_iota(jnp.int32, (block, width), 0)
-            scores = jnp.where((key_place <= place) & (key_place >= start), scores, MASKED)
+            scores = jnp.where(seen, dot_nt(pair, queries[which]), MASKED)
             new_peak = jnp.maximum(peak, jnp.max(scores, axis=0, keepdims=True))
             weights = jnp.exp(scores - new_peak)
             shrink = jnp.exp(peak - new_peak)
             total = total * shrink + jnp.sum(weights, axis=0, keepdims=True)
             mixed = mixed * shrink + dot_tn(pair, weights.astype(jnp.bfloat16))
-            return (new_peak, total, mixed)
-
-        peak, total, mixed = lax.fori_loop(
-            0,
-            steps,
-            body,
-            (
-                jnp.full((1, width), MASKED, jnp.float32),
-                jnp.zeros((1, width), jnp.float32),
-                jnp.zeros((LANES, width), jnp.float32),
-            ),
-        )
+            result.append((new_peak, total, mixed))
+        return tuple(result)
+
+    empty = (
+        jnp.full((1, width), MASKED, jnp.float32),
+        jnp.zeros((1, width), jnp.float32),
+        jnp.zeros((LANES, width), jnp.float32),
+    )
+    outs = []
+    for which, (peak, total, mixed) in enumerate(lax.fori_loop(0, steps, body, (empty, empty))):
         log_ref[0, which : which + 1, :] = peak + jnp.log(total)
         outs.append(mixed / total)
     joined = jnp.concatenate([outs[1][:HEAD_DIM], outs[0][HEAD_DIM:]], axis=0)
@@ -321,36 +322,44 @@
     base = chunk * (2 + parts)
     steps = meta_ref[base + 1] - meta_ref[base] + 1
     width = heads * block
-    grads = []
+    key_lanes = lane < HEAD_DIM
+    queries, grad, centre, logs = ([], [], [], [])
     for which in range(2):
-        is_key = (lane < HEAD_DIM) if which == 0 else (lane >= HEAD_DIM)
-        queries = jnp.where(is_key, stacked, jnp.zeros_like(stacked))
-        grad = jnp.where(is_key, jnp.zeros_like(stacked_grad), stacked_grad)
+        is_key = key_lanes if which == 0 else ~key_lanes
+        queries.append(jnp.where(is_key, stacked, jnp.zeros_like(stacked)))
+        grad.append(jnp.where(is_key, jnp.zeros_like(stacked_grad), stacked_grad))
         own = jnp.where(is_key, 0.0, product)
-        centre = lax.dot_general(
-            jnp.ones((8, LANES), jnp.float32),
-            own,
-            (((1,), (1,)), ((), ())),
-            precision=lax.Precision.HIGHEST,
-            preferred_element_type=jnp.float32,
-        )[0:1]
-        logs = log_ref[0, which : which + 1, :]
-
-        def body(step, grad_query):
-            key_block, slot, at, shift = block_of(meta_ref, chunk, step, parts, lines)
+        centre.append(
+            lax.dot_general(
+                jnp.ones((8, LANES), jnp.float32),
+                own,
+                (((1,), (1,)), ((), ())),
+                precision=lax.Precision.HIGHEST,
+                preferred_element_type=jnp.float32,
+            )[0:1]
+        )
+        logs.append(log_ref[0, which : which + 1, :])
+
+    def body(step, carry):
+        key_block, slot, at, shift = block_of(meta_ref, chunk, step, parts, lines)
+        key_place = key_block * block + lax.broadcasted_iota(jnp.int32, (block, width), 0)
+        seen = (key_place <= place) & (key_place >= start)
+        result = []
+        for which in range(2):
             columns = slice(which * LANES, (which + 1) * LANES)
             pair = pair_ref[at, slot, :, columns]
-            scores = dot_nt(pair, queries)
-            key_place = key_block * block + lax.broadcasted_iota(jnp.int32, (block, width), 0)
-            scores = jnp.where((key_place <= place) & (key_place >= start), scores, MASKED)
-            weights = jnp.exp(scores - logs)
-            grad_scores = (weights * (dot_nt(pair, grad) - centre)).astype(jnp.bfloat16)
-            sums[shift, slot, :, columns] += dot_nn(grad_scores, queries) + dot_nn(
-                weights.astype(jnp.bfloat16), grad
+            scores = jnp.where(seen, dot_nt(pair, queries[which]), MASKED)
+            weights = jnp.exp(scores - logs[which])
+            grad_weights = dot_nt(pair, grad[which]) - centre[which]
+            grad_scores = (weights * grad_weights).astype(jnp.bfloat16)
+            sums[shift, slot, :, columns] += dot_nn(grad_scores, queries[which]) + dot_nn(
+                weights.astype(jnp.bfloat16), grad[which]
             )
-            return grad_query + dot_tn(pair, grad_scores)
-
-        grads.append(lax.fori_loop(0, steps, body, jnp.zeros((LANES, width), jnp.float32)))
+            result.append(carry[which] + dot_tn(pair, grad_scores))
+        return tuple(result)
+
+    empty = jnp.zeros((LANES, width), jnp.float32)
+    grads = lax.fori_loop(0, steps, body, (empty, empty))
     joined = jnp.concatenate([grads[0][:HEAD_DIM], grads[1][HEAD_DIM:]], axis=0)
     rows = joined.T * SCORE_SCALE
     cosine, sine = cos_ref[...], sin_ref[...]
@@ -874,17 +883,19 @@
 
     def feed_others(key):
         gate, up = (work["grad_gate"], work["grad_up"])
-        key, gate_other, up_other = lax.optimization_barrier(
-            (key, other_half(normed_two, gate), other_half(normed_two, up))
+        key, work["down_piece"], gate_other, up_other = lax.optimization_barrier(
+            (key, down_piece, other_half(normed_two, gate), other_half(normed_two, up))
         )
         work["feed"] = (normed_two, gate, up, other_core(gate_other), other_core(up_other))
         return key
 
     def feed_owns(first):
-        first, work["down_piece"], rows, gate, up, gate_other, up_other = lax.optimization_barrier(
-            (first, down_piece, *work["feed"])
-        )
-        work["totals"] = (own_half(rows, gate, gate_other), own_half(rows, up, up_other))
+        rows, gate, up, gate_other, up_other = work["feed"]
+        gate_total = own_half(rows, gate, gate_other)
+        first, gate_total, rows, up, up_other = lax.optimization_barrier(
+            (first, gate_total, rows, up, up_other)
+        )
+        work["totals"] = (gate_total, own_half(rows, up, up_other))
         return first
 
     grad_normed_two = reduce_tokens(feed_back, feed_others, feed_owns)
@@ -905,6 +916,8 @@
     )
     gate_total, up_total = work["totals"]
     back = jnp.concatenate(gather_tokens(grad_middle_low, (gate_total, up_total)), axis=0)
+
+    meta_core = jnp.stack([y, core]).astype(jnp.int32)
 
     def back_here(products):
         products, work["back"] = lax.optimization_barrier((products, back))
@@ -951,12 +964,26 @@
     grad_keyvalue = pair_back(work["grad_parts"], cosine, sine, block)
     grad_joint = jnp.concatenate([grad_query, grad_keyvalue], axis=1)
     normed_one = jnp.concatenate(normed_parts, axis=0)
-    meta_core = jnp.stack([y, core]).astype(jnp.int32)
 
     def joint_products(first, last):
         if first:
             return product(grad_joint, joint_weight)(first, last)
-        work["shards"] = collect(jnp.concatenate([work["down_piece"], gate_piece], axis=0))
+        output_total = own_half(back, mixed, other_core(other_half(back, mixed)))
+        shards = collect(jnp.concatenate([work["down_piece"], work["gate_piece"]], axis=0))
+        close, work["output"], work["shards"] = lax.optimization_barrier(
+            (product(grad_joint, joint_weight)(first, last), output_total, shards)
+        )
+        return close
+
+    def joint_others(key):
+        key, work["output_parts"], other = lax.optimization_barrier(
+            (key, output_parts, other_half(normed_one, grad_joint))
+        )
+        work["joint"] = (normed_one, grad_joint, other_core(other))
+        work["output_piece"] = scatter(work["output"])
+        return key
+
+    def joint_owns(first):
         down_new = turned_update(
             meta_core,
             work["shards"],
@@ -964,23 +991,10 @@
             FF ** (-0.5),
             False,
         )
-        output_total = own_half(back, mixed, other_core(other_half(back, mixed)))
-        close, work["output"], work["down_new"] = lax.optimization_barrier(
-            (product(grad_joint, joint_weight)(first, last), output_total, down_new)
-        )
-        return close
-
-    def joint_others(key):
-        key, work["output_parts"], other = lax.optimization_barrier(
-            (key, output_parts, other_half(normed_one, grad_joint))
-        )
-        work["joint"] = (normed_one, grad_joint, other_core(other))
-        work["output_piece"] = scatter(work["output"])
-        return key
-
-    def joint_owns(first):
-        first, work["output_piece"], rows, grad, other = lax.optimization_barrier(
-            (first, work["output_piece"], *work["joint"])
+        first, work["output_piece"], work["up_piece"], work["down_new"], rows, grad, other = (
+            lax.optimization_barrier(
+                (first, work["output_piece"], work["up_piece"], down_new, *work["joint"])
+            )
         )
         work["joint_total"] = own_half(rows, grad, other)
         return first
@@ -1023,6 +1037,7 @@
     )
 
     gain_sums = jnp.stack([gain_one, gain_two])
+    gain_sums, gateup_new = lax.optimization_barrier((gain_sums, gateup_new))
     blocks = [
         jnp.concatenate(
             [

time: 818 us -> 788 us (0.963)
  waiting for transfers between devices: 341 us -> 312 us
    ppermute x5, waiting for transfers between devices: 25.9 us -> 13.4 us  [other_y(): return lax.ppermute(value, 'y', [(0, 1), (1, 0)])]
    ppermute x25, waiting for transfers between devices: 138 us -> 126 us  [shift(): lax.ppermute(value, axis, [(i, (i + by) % size) for i in range(size)])]
    ppermute x4, waiting for transfers between devices: 25.6 us -> 14.2 us  [reduce_tokens(): first = before_last(lax.ppermute(middle(key), near, first_pairs))]
    unnamed x213 -> x215, local copies, waits for them, and re-layouts: 45.5 us -> 43 us
  transfers between devices with their start and end apart: 76 -> 76, of which waited for: 31 -> 36; matrix products, arithmetic and copies ran while one was open for 20% -> 22% of each run, Pallas kernels for 19% -> 20%
where the time goes in v3:
time: 788 us; the launch traced here: 774 us
  waiting for transfers between devices  312 us (40%)
  Pallas kernels  171 us (22%)
  matrix products  86.8 us (11%)
  local copies, waits for them, and re-layouts  72.9 us (9%)
  starting transfers between devices  67.2 us (9%)
  other arithmetic  48.4 us (6%)
  between operations  15.9 us (2%)
    ppermute x25, waiting for transfers between devices, shift(): lax.ppermute(value, axis, [(i, (i + by) % size) for i in range(size)])  126 us
    ppermute x4, waiting for transfers between devices, gather_tokens(): first = lax.ppermute(own, near, first_pairs)  67 us
    dot_general x10, matrix products, dot_tn(): lax.dot_general(left, right, (((0,), (0,)), ((), ())), preferred_element_...  56 us
    unnamed x215, local copies, waits for them, and re-layouts  43 us
    pallas_call x1, Pallas kernels, gateup_update(): pl.pallas_call(gateup_update_kernel, grid_spec=pltpu.PrefetchScalarGridSp...  35.8 us
    pallas_call x2, Pallas kernels, widen_back(): pl.pallas_call(functools.partial(widen_back_kernel, slots, len(kept)), gr...  34.9 us
    ppermute x25, starting transfers between devices, shift(): lax.ppermute(value, axis, [(i, (i + by) % size) for i in range(size)])  34.5 us
    pallas_call x1, Pallas kernels, attend_back(): pl.pallas_call(functools.partial(attend_back_kernel, parts, lines), grid_...  26 us
  transfers between devices with their start and end apart: 76, of which 36 were waited for; matrix products, arithmetic and copies ran while one was open for 22% of the time, Pallas kernels for 20%

profile of v3, /device:TPU:11, one launch (start us, length us, event | category | flops | bytes accessed | tf_op | source)
XLA Modules:
  0.0 773.9 jit_solution(17381635113971724854)
XLA Ops:
  47.5 20.1 %collective-permute-done.7.refs_1_ = bf16[256,2048]{1,0:T(8,128)(2,1)S(1)} collective-permute-done((bf16[256,2048]{1,0:T(8,128)(2,1)S(1)}, bf16[256,2048]{1,0:T(8,128)(2,1)S(1)}, u32[]{:S(2)}, u32[]{:S(2)}) %collective-permute-start.7) | collective-permute-done | bytes 1048608 | tf_op jit(solution)/shard_map/ppermute | solution.py:656
  80.3 13.4 %collective-permute-done.10 = bf16[256,512]{1,0:T(8,128)(2,1)} collective-permute-done((bf16[256,512]{1,0:T(8,128)(2,1)}, bf16[256,512]{1,0:T(8,128)(2,1)}, u32[]{:S(2)}, u32[]{:S(2)}) %collective-permute-start.10) | collective-permute-done | bytes 262176 | tf_op jit(solution)/shard_map/ppermute | solution.py:630
  93.7 17.7 %collective-permute-done.11 = bf16[256,512]{1,0:T(8,128)(2,1)} collective-permute-done((bf16[256,512]{1,0:T(8,128)(2,1)}, bf16[256,512]{1,0:T(8,128)(2,1)}, u32[]{:S(2)}, u32[]{:S(2)}) %collective-permute-start.11) | collective-permute-done | bytes 262176 | tf_op jit(solution)/shard_map/ppermute | solution.py:630
  134.8 19.8 %collective-permute-done.13.refs_1_ = bf16[256,2048]{1,0:T(8,128)(2,1)S(1)} collective-permute-done((bf16[256,2048]{1,0:T(8,128)(2,1)S(1)}, bf16[256,2048]{1,0:T(8,128)(2,1)S(1)}, u32[]{:S(2)}, u32[]{:S(2)}) %collective-permute-start.13) | collective-permute-done | bytes 1048608 | tf_op jit(solution)/shard_map/ppermute | solution.py:656
  174.8 14.2 %attend.1 = (bf16[1024,512]{1,0:T(8,128)(2,1)S(1)}, f32[4,2,1024]{2,1,0:T(2,128)S(1)}) custom-call(s32[17]{0:T(128)S(1)} %pad_add_fusion.7.meta_ref, bf16[1024,512]{1,0:T(8,128)(2,1)S(1)} %copy-done.42, bf16[4,4,256,256]{3,2,1,0:T(8,128)(2,1)S(1)} %copy-done.40, s32[4,2,256]{2,1,0:T(2,128)S(1)} %pad_add_fusion.2.info_ref.refs_4_), custom_call_target="tpu_custom_call" | custom-call | flops 3221225472 | bytes 4194304 | tf_op jit(solution)/shard_map/attend/pallas_call | solution.py:275
  198.5 9.7 %collective-permute-done.16 = bf16[256,2048]{1,0:T(8,128)(2,1)} collective-permute-done((bf16[256,2048]{1,0:T(8,128)(2,1)}, bf16[256,2048]{1,0:T(8,128)(2,1)}, u32[]{:S(2)}, u32[]{:S(2)}) %collective-permute-start.16) | collective-permute-done | bytes 1048608 | tf_op jit(solution)/shard_map/ppermute | solution.py:673
  208.1 11.2 %collective-permute-done.17 = bf16[256,2048]{1,0:T(8,128)(2,1)} collective-permute-done((bf16[256,2048]{1,0:T(8,128)(2,1)}, bf16[256,2048]{1,0:T(8,128)(2,1)}, u32[]{:S(2)}, u32[]{:S(2)}) %collective-permute-start.17) | collective-permute-done | bytes 1048608 | tf_op jit(solution)/shard_map/ppermute | solution.py:674
  222.3 14.2 %collective-permute-done.18 = bf16[256,2048]{1,0:T(8,128)(2,1)S(1)} collective-permute-done((bf16[256,2048]{1,0:T(8,128)(2,1)S(1)}, bf16[256,2048]{1,0:T(8,128)(2,1)S(1)}, u32[]{:S(2)}, u32[]{:S(2)}) %collective-permute-start.18) | collective-permute-done | bytes 1048608 | tf_op jit(solution)/shard_map/ppermute | solution.py:679
  240.7 14.1 %collective-permute-done.19.refs_1_ = bf16[256,2048]{1,0:T(8,128)(2,1)} collective-permute-done((bf16[256,2048]{1,0:T(8,128)(2,1)S(1)}, bf16[256,2048]{1,0:T(8,128)(2,1)}, u32[]{:S(2)}, u32[]{:S(2)}) %collective-permute-start.19) | collective-permute-done | bytes 1048608 | tf_op jit(solution)/shard_map/ppermute | solution.py:656
  264.8 12.0 %collective-permute-done.21.refs_3_ = bf16[256,2048]{1,0:T(8,128)(2,1)} collective-permute-done((bf16[256,2048]{1,0:T(8,128)(2,1)}, bf16[256,2048]{1,0:T(8,128)(2,1)}, u32[]{:S(2)}, u32[]{:S(2)}) %collective-permute-start.21) | collective-permute-done | bytes 1048608 | tf_op jit(solution)/shard_map/ppermute | solution.py:659
  282.6 19.8 %widen.1 = (bf16[1024,1408]{1,0:T(8,128)(2,1)}, bf16[1024,1408]{1,0:T(8,128)(2,1)}, bf16[1024,1408]{1,0:T(8,128)(2,1)}) custom-call(bf16[256,2048]{1,0:T(8,128)(2,1)S(1)} %copy-done.2, bf16[256,2048]{1,0:T(8,128)(2,1)} %collective-permute-done.19.refs_1_, bf16[256,2048]{1,0:T(8,128)(2,1)S(1)} %copy-done.28, ...), custom_call_target="tpu_custom_call" | custom-call | flops 11811160064 | bytes 24379392 | tf_op jit(solution)/shard_map/widen/pallas_call | solution.py:141
  328.7 13.0 %all-gather.11.cloned.1.call-done.refs_2_ = bf16[2048,1408]{1,0:T(8,128)(2,1)} async-done(((bf16[256,1408]{1,0:T(8,128)(2,1)}), bf16[2048,1408]{1,0:T(8,128)(2,1)}) %all-gather.11.cloned.1.call-update) | async-done | bytes 5767184 | tf_op jit(solution)/shard_map/all_gather | solution.py:749
  344.4 18.4 %widen_back.2 = (bf16[1024,1408]{1,0:T(8,128)(2,1)}, bf16[1024,1408]{1,0:T(8,128)(2,1)}, bf16[512,2048]{1,0:T(8,128)(2,1)S(1)}) custom-call(bf16[256,2048]{1,0:T(8,128)(2,1)S(1)} %collective-permute-done.14.refs_0_, bf16[256,2048]{1,0:T(8,128)(2,1)S(1)} %collective-permute-done.15.refs_1_, bf16[2048,1408]{1,0:T(8,128)(2,1)} %all-gather.11.cloned.1.call-done.refs_2_, ...), custom_call_target="tpu_custom_call" | custom-call | flops 1476395008 | bytes 5767168 | tf_op jit(solution)/shard_map/widen_back/pallas_call | solution.py:179
  364.6 16.5 %widen_back.3 = (bf16[1024,1408]{1,0:T(8,128)(2,1)}, bf16[1024,1408]{1,0:T(8,128)(2,1)}, bf16[512,2048]{1,0:T(8,128)(2,1)S(1)}) custom-call(bf16[256,2048]{1,0:T(8,128)(2,1)S(1)} %slice_dynamic-update-slice_fusion.refs_0_, bf16[256,2048]{1,0:T(8,128)(2,1)S(1)} %copy-done.5, ...), custom_call_target="tpu_custom_call", output_to_operand_aliasing={{0}: (6, {}), {1}: (7, {})} | custom-call | flops 1476395008 | bytes 5767168 | tf_op jit(solution)/shard_map/widen_back/pallas_call | solution.py:179
  437.8 13.0 %collective-permute-done.28 = bf16[256,2048]{1,0:T(8,128)(2,1)S(1)} collective-permute-done((bf16[256,2048]{1,0:T(8,128)(2,1)}, bf16[256,2048]{1,0:T(8,128)(2,1)S(1)}, u32[]{:S(2)}, u32[]{:S(2)}) %collective-permute-start.28) | collective-permute-done | bytes 1048608 | tf_op jit(solution)/shard_map/ppermute | solution.py:656
  475.9 26.0 %attend_back.1 = (bf16[1024,512]{1,0:T(8,128)(2,1)S(1)}, bf16[4,256,256]{2,1,0:T(8,128)(2,1)S(1)}, bf16[4,256,256]{2,1,0:T(8,128)(2,1)}, bf16[4,256,256]{2,1,0:T(8,128)(2,1)}, bf16[4,256,256]{2,1,0:T(8,128)(2,1)}) custom-call(s32[17]{0:T(128)S(1)} %pad_add_fusion.7.meta_ref, bf16[1024,512]{1,0:T(8,128)(2,1)S(1)} %copy-done.43, ...), custom_call_target="tpu_custom_call" | custom-call | flops 8053063680 | bytes 8388608 | tf_op jit(solution)/shard_map/attend_back/pallas_call | solution.py:387
  520.6 23.7 %collective-permute-done.34.refs_1_ = bf16[1024,256]{1,0:T(8,128)(2,1)S(1)} collective-permute-done((bf16[1024,256]{1,0:T(8,128)(2,1)}, bf16[1024,256]{1,0:T(8,128)(2,1)S(1)}, u32[]{:S(2)}, u32[]{:S(2)}) %collective-permute-start.34) | collective-permute-done | bytes 524320 | tf_op jit(solution)/shard_map/ppermute | solution.py:630
  545.8 17.3 %collective-permute-done.35.refs_2_ = bf16[1024,256]{1,0:T(8,128)(2,1)S(1)} collective-permute-done((bf16[1024,256]{1,0:T(8,128)(2,1)}, bf16[1024,256]{1,0:T(8,128)(2,1)S(1)}, u32[]{:S(2)}, u32[]{:S(2)}) %collective-permute-start.35) | collective-permute-done | bytes 524320 | tf_op jit(solution)/shard_map/ppermute | solution.py:630
  564.0 10.2 %collective-permute-done.36.refs_3_ = bf16[1024,256]{1,0:T(8,128)(2,1)S(1)} collective-permute-done((bf16[1024,256]{1,0:T(8,128)(2,1)}, bf16[1024,256]{1,0:T(8,128)(2,1)S(1)}, u32[]{:S(2)}, u32[]{:S(2)}) %collective-permute-start.36) | collective-permute-done | bytes 524320 | tf_op jit(solution)/shard_map/ppermute | solution.py:630
  614.6 25.7 %collective-permute-done.44 = bf16[256,512]{1,0:T(8,128)(2,1)} collective-permute-done((bf16[256,512]{1,0:T(8,128)(2,1)}, bf16[256,512]{1,0:T(8,128)(2,1)}, u32[]{:S(2)}, u32[]{:S(2)}) %collective-permute-start.44) | collective-permute-done | bytes 262176 | tf_op jit(solution)/shard_map/ppermute | solution.py:630
  646.3 15.2 %turned_update.2 = (f32[2816,512]{1,0:T(8,128)}, f32[2816,512]{1,0:T(8,128)}, f32[2816,512]{1,0:T(8,128)}) custom-call(s32[2]{0:T(128)S(1)} %pad_add_fusion.8.meta_ref, bf16[512,1408]{1,0:T(8,128)(2,1)S(1)} %constant_dynamic-update-slice_fusion.12.refs_0_, bf16[512,1408]{1,0:T(8,128)(2,1)S(1)} %collective-permute-done.40.refs_1_, ...), custom_call_target="tpu_custom_call" | custom-call | flops 28835840 | bytes 34603008 | tf_op jit(solution)/shard_map/turned_update/pallas_call | solution.py:540
  676.3 10.5 %collective-permute-done.51.refs_5_ = bf16[256,1408]{1,0:T(8,128)(2,1)S(1)} collective-permute-done((bf16[256,1408]{1,0:T(8,128)(2,1)S(1)}, bf16[256,1408]{1,0:T(8,128)(2,1)S(1)}, u32[]{:S(2)}, u32[]{:S(2)}) %collective-permute-start.51) | collective-permute-done | bytes 720928 | tf_op jit(solution)/shard_map/ppermute | solution.py:636
  693.6 35.8 %gateup_update.1 = (f32[512,2,2816]{2,1,0:T(2,128)}, f32[512,2,2816]{2,1,0:T(2,128)}, f32[512,2,2816]{2,1,0:T(2,128)}) custom-call(s32[2]{0:T(128)S(1)} %pad_add_fusion.8.meta_ref, bf16[512,1408]{1,0:T(8,128)(2,1)S(1)} %constant_dynamic-update-slice_fusion.12.refs_0_, bf16[512,1408]{1,0:T(8,128)(2,1)S(1)} %collective-permute-done.40.refs_1_, ...), custom_call_target="tpu_custom_call" | custom-call | flops 57671680 | bytes 80740352 | tf_op jit(solution)/shard_map/gateup_update/pallas_call | solution.py:577
  757.6 9.5 %joint_update.1 = (f32[512,1024]{1,0:T(8,128)}, f32[512,1024]{1,0:T(8,128)}, f32[512,1024]{1,0:T(8,128)}, f32[512,512]{1,0:T(8,128)}, f32[512,512]{1,0:T(8,128)}, /*index=5*/f32[512,512]{1,0:T(8,128)}) custom-call(s32[2]{0:T(128)S(1)} %pad_add_fusion.8.meta_ref, bf16[256,768]{1,0:T(8,128)(2,1)S(1)} %pad_maximum_fusion.12.refs_0_, ...), custom_call_target="tpu_custom_call" | custom-call | flops 15728640 | bytes 18874368 | tf_op jit(solution)/shard_map/joint_update/pallas_call | solution.py:498
  (522 shorter events, 357.1 us)
Async XLA Ops:
  7.2 108.9 %all-gather.5.cloned.1.call-start = ((), (), s32[]{:S(2)}) async-start(), calls=%async_computation.5 | async-start | bytes 5898240 | tf_op jit(solution)/shard_map/all_gather | solution.py:749
  35.7 135.8 %all-gather.7.cloned.1.call-start = ((), (), s32[]{:S(2)}) async-start(), calls=%async_computation.6 | async-start | bytes 2621440 | tf_op jit(solution)/shard_map/all_gather | solution.py:837
  71.6 42.2 %collective-permute-start.9 = (bf16[256,2048]{1,0:T(8,128)(2,1)S(1)}, bf16[256,2048]{1,0:T(8,128)(2,1)}, u32[]{:S(2)}, u32[]{:S(2)}) collective-permute-start(bf16[256,2048]{1,0:T(8,128)(2,1)S(1)} %collective-permute-done.7.refs_1_), channel_id=1, source_target_pairs={{0,16},{4,20},{8,12},{12,8},{16,0},{20,4},{24,28},{28,24},{1,17},{... | collective-permute-start | bytes 3145736 | tf_op jit(solution)/shard_map/ppermute | solution.py:659
  74.2 37.2 %collective-permute-start.11 = (bf16[256,512]{1,0:T(8,128)(2,1)}, bf16[256,512]{1,0:T(8,128)(2,1)}, u32[]{:S(2)}, u32[]{:S(2)}) collective-permute-start(bf16[256,512]{1,0:T(8,128)(2,1)} %get-tuple-element.353), channel_id=1, source_target_pairs={{0,2},{1,3},{2,0},{3,1},{4,6},{5,7},{6,4},{7,5},{8,10},{9,11},{10,... | collective-permute-start | bytes 786440 | tf_op jit(solution)/shard_map/ppermute | solution.py:630
  77.2 36.6 %collective-permute-start.12 = (bf16[256,512]{1,0:T(8,128)(2,1)}, bf16[256,512]{1,0:T(8,128)(2,1)}, u32[]{:S(2)}, u32[]{:S(2)}) collective-permute-start(bf16[256,512]{1,0:T(8,128)(2,1)} %get-tuple-element.352), channel_id=1, source_target_pairs={{0,3},{1,0},{2,1},{3,2},{4,7},{5,4},{6,5},{7,6},{8,11},{9,8},{10,9... | collective-permute-start | bytes 786440 | tf_op jit(solution)/shard_map/ppermute | solution.py:630
  128.0 152.2 %all-gather.9.cloned.1.call-start = ((), (), s32[]{:S(2)}) async-start(), calls=%async_computation.7 | async-start | bytes 12976128 | tf_op jit(solution)/shard_map/all_gather | solution.py:749
  171.6 170.1 %all-gather.11.cloned.1.call-start = ((), (), s32[]{:S(2)}) async-start(), calls=%async_computation.8 | async-start | bytes 6488064 | tf_op jit(solution)/shard_map/all_gather | solution.py:749
  195.4 204.3 %reduce-scatter.6.cloned.1.call-start = ((), (), s32[]{:S(2)}) async-start(), calls=%async_computation.9 | async-start | bytes 3604480 | tf_op jit(solution)/shard_map/reduce_scatter | solution.py:861
  341.7 161.9 %reduce-scatter.8.cloned.1.call-start = ((), (), s32[]{:S(2)}) async-start(), calls=%async_computation.10 | async-start | bytes 3604480 | tf_op jit(solution)/shard_map/reduce_scatter | solution.py:861
  417.1 157.8 %reduce-scatter.10.cloned.1.call-start = ((), (), s32[]{:S(2)}) async-start(), calls=%async_computation.11 | async-start | bytes 3604480 | tf_op jit(solution)/shard_map/reduce_scatter | solution.py:861
  434.5 227.0 %reduce-scatter.12.cloned.1.call-start = ((), (), s32[]{:S(2)}) async-start(), calls=%async_computation.12 | async-start | bytes 1310720 | tf_op jit(solution)/shard_map/reduce_scatter | solution.py:861
  469.1 34.5 %collective-permute-start.31 = (bf16[256,2048]{1,0:T(8,128)(2,1)S(1)}, bf16[256,2048]{1,0:T(8,128)(2,1)}, u32[]{:S(2)}, u32[]{:S(2)}) collective-permute-start(bf16[256,2048]{1,0:T(8,128)(2,1)S(1)} %get-tuple-element.309), channel_id=1, source_target_pairs={{0,16},{4,20},{8,12},{12,8},{16,0},{20,4},{24,28},{28,24},{1,17},{... | collective-permute-start | bytes 3145736 | tf_op jit(solution)/shard_map/ppermute | solution.py:673
  506.4 68.6 %collective-permute-start.33 = (bf16[256,2048]{1,0:T(8,128)(2,1)}, bf16[256,2048]{1,0:T(8,128)(2,1)}, u32[]{:S(2)}, u32[]{:S(2)}) collective-permute-start(bf16[256,2048]{1,0:T(8,128)(2,1)} %add_convert_fusion.7), channel_id=1, source_target_pairs={{0,4},{4,0},{8,24},{12,28},{16,20},{20,16},{24,8},{28,12},{1,5},{5... | collective-permute-start | bytes 3145736 | tf_op jit(solution)/shard_map/ppermute | solution.py:679
  509.0 35.3 %collective-permute-start.34 = (bf16[1024,256]{1,0:T(8,128)(2,1)}, bf16[1024,256]{1,0:T(8,128)(2,1)S(1)}, u32[]{:S(2)}, u32[]{:S(2)}) collective-permute-start(bf16[1024,256]{1,0:T(8,128)(2,1)} %bitcast.51), channel_id=1, source_target_pairs={{0,3},{1,0},{2,1},{3,2},{4,7},{5,4},{6,5},{7,6},{8,11},{9,8},{10,9... | collective-permute-start | bytes 1572872 | tf_op jit(solution)/shard_map/ppermute | solution.py:630
  509.1 53.9 %collective-permute-start.35 = (bf16[1024,256]{1,0:T(8,128)(2,1)}, bf16[1024,256]{1,0:T(8,128)(2,1)S(1)}, u32[]{:S(2)}, u32[]{:S(2)}) collective-permute-start(bf16[1024,256]{1,0:T(8,128)(2,1)} %bitcast.52), channel_id=1, source_target_pairs={{0,2},{1,3},{2,0},{3,1},{4,6},{5,7},{6,4},{7,5},{8,10},{9,11},{10,... | collective-permute-start | bytes 1572872 | tf_op jit(solution)/shard_map/ppermute | solution.py:630
  516.9 57.3 %collective-permute-start.36 = (bf16[1024,256]{1,0:T(8,128)(2,1)}, bf16[1024,256]{1,0:T(8,128)(2,1)S(1)}, u32[]{:S(2)}, u32[]{:S(2)}) collective-permute-start(bf16[1024,256]{1,0:T(8,128)(2,1)} %bitcast.53), channel_id=1, source_target_pairs={{0,1},{1,2},{2,3},{3,0},{4,5},{5,6},{6,7},{7,4},{8,9},{9,10},{10,1... | collective-permute-start | bytes 1572872 | tf_op jit(solution)/shard_map/ppermute | solution.py:630
  517.0 73.7 %collective-permute-start.40 = (bf16[512,1408]{1,0:T(8,128)(2,1)S(1)}, bf16[512,1408]{1,0:T(8,128)(2,1)S(1)}, u32[]{:S(2)}, u32[]{:S(2)}) collective-permute-start(bf16[512,1408]{1,0:T(8,128)(2,1)S(1)} %constant_dynamic-update-slice_fusion.12.refs_0_), channel_id=1, source_target_pairs={{0,16},{16,0},{1,17},{17,1},{2,18},{18,2},{3,19},{19,3},{4,20},{20... | collective-permute-start | bytes 4325384 | tf_op jit(solution)/shard_map/ppermute | solution.py:636
  545.1 63.0 %collective-permute-start.41 = (bf16[512,1408]{1,0:T(8,128)(2,1)S(1)}, bf16[512,1408]{1,0:T(8,128)(2,1)}, u32[]{:S(2)}, u32[]{:S(2)}) collective-permute-start(bf16[512,1408]{1,0:T(8,128)(2,1)S(1)} %constant_dynamic-update-slice_fusion.12.refs_0_), channel_id=1, source_target_pairs={{0,8},{8,0},{1,9},{9,1},{2,10},{10,2},{3,11},{11,3},{4,12},{12,4},... | collective-permute-start | bytes 4325384 | tf_op jit(solution)/shard_map/ppermute | solution.py:633
  612.4 118.3 %reduce-scatter.14.cloned.1.call-start = ((), (), s32[]{:S(2)}) async-start(), calls=%async_computation.13 | async-start | bytes 1966080 | tf_op jit(solution)/shard_map/reduce_scatter | solution.py:861
  687.8 41.6 %collective-permute-start.48 = (bf16[256,512]{1,0:T(8,128)(2,1)S(1)}, bf16[256,512]{1,0:T(8,128)(2,1)S(1)}, u32[]{:S(2)}, u32[]{:S(2)}) collective-permute-start(bf16[256,512]{1,0:T(8,128)(2,1)S(1)} %get-tuple-element.322), channel_id=1, source_target_pairs={{0,1},{1,2},{2,3},{3,0},{4,5},{5,6},{6,7},{7,4},{8,9},{9,10},{10,1... | collective-permute-start | bytes 786440 | tf_op jit(solution)/shard_map/ppermute | solution.py:630
  687.8 41.6 %collective-permute-start.49 = (bf16[256,512]{1,0:T(8,128)(2,1)S(1)}, bf16[256,512]{1,0:T(8,128)(2,1)S(1)}, u32[]{:S(2)}, u32[]{:S(2)}) collective-permute-start(bf16[256,512]{1,0:T(8,128)(2,1)S(1)} %get-tuple-element.321), channel_id=1, source_target_pairs={{0,2},{1,3},{2,0},{3,1},{4,6},{5,7},{6,4},{7,5},{8,10},{9,11},{10,... | collective-permute-start | bytes 786440 | tf_op jit(solution)/shard_map/ppermute | solution.py:630
  692.0 38.8 %collective-permute-start.50 = (bf16[256,512]{1,0:T(8,128)(2,1)S(1)}, bf16[256,512]{1,0:T(8,128)(2,1)}, u32[]{:S(2)}, u32[]{:S(2)}) collective-permute-start(bf16[256,512]{1,0:T(8,128)(2,1)S(1)} %get-tuple-element.320), channel_id=1, source_target_pairs={{0,3},{1,0},{2,1},{3,2},{4,7},{5,4},{6,5},{7,6},{8,11},{9,8},{10,9... | collective-permute-start | bytes 786440 | tf_op jit(solution)/shard_map/ppermute | solution.py:630
  693.0 46.4 %collective-permute-start.65 = (bf16[256,512]{1,0:T(8,128)(2,1)S(1)}, bf16[256,512]{1,0:T(8,128)(2,1)}, u32[]{:S(2)}, u32[]{:S(2)}) collective-permute-start(bf16[256,512]{1,0:T(8,128)(2,1)S(1)} %copy-done.39), channel_id=1, source_target_pairs={{0,8},{8,0},{1,9},{9,1},{2,10},{10,2},{3,11},{11,3},{4,12},{12,4},... | collective-permute-start | bytes 786440 | tf_op jit(solution)/shard_map/ppermute | solution.py:633
  693.1 49.1 %collective-permute-start.66 = (bf16[256,512]{1,0:T(8,128)(2,1)S(1)}, bf16[256,512]{1,0:T(8,128)(2,1)}, u32[]{:S(2)}, u32[]{:S(2)}) collective-permute-start(bf16[256,512]{1,0:T(8,128)(2,1)S(1)} %collective-permute-done.64.refs_1_), channel_id=1, source_target_pairs={{0,8},{8,0},{1,9},{9,1},{2,10},{10,2},{3,11},{11,3},{4,12},{12,4},... | collective-permute-start | bytes 786440 | tf_op jit(solution)/shard_map/ppermute | solution.py:633
  (143 other events, 1656.8 us)
Sparse Core Ops, SparseCore 0:
  35.9 71.3 all-gather.4
  128.1 43.4 all-gather.6
  173.8 106.3 all-gather.8
  282.2 59.4 all-gather.10
  343.8 55.8 reduce-scatter.5
  417.2 55.7 reduce-scatter.7
  475.9 82.7 reduce-scatter.9
  612.6 33.6 reduce-scatter.11
  667.2 47.9 reduce-scatter.13

commit v4 on v3

--- a/solution.py
+++ b/solution.py
@@ -970,15 +970,18 @@
             return product(grad_joint, joint_weight)(first, last)
         output_total = own_half(back, mixed, other_core(other_half(back, mixed)))
         shards = collect(jnp.concatenate([work["down_piece"], work["gate_piece"]], axis=0))
-        close, work["output"], work["shards"] = lax.optimization_barrier(
-            (product(grad_joint, joint_weight)(first, last), output_total, shards)
+        close, work["output"], work["shards"], work["up_shards"] = lax.optimization_barrier(
+            (
+                product(grad_joint, joint_weight)(first, last),
+                output_total,
+                shards,
+                collect(work["up_piece"]),
+            )
         )
         return close
 
     def joint_others(key):
-        key, work["output_parts"], other = lax.optimization_barrier(
-            (key, output_parts, other_half(normed_one, grad_joint))
-        )
+        key, other = lax.optimization_barrier((key, other_half(normed_one, grad_joint)))
         work["joint"] = (normed_one, grad_joint, other_core(other))
         work["output_piece"] = scatter(work["output"])
         return key
@@ -991,11 +994,18 @@
             FF ** (-0.5),
             False,
         )
-        first, work["output_piece"], work["up_piece"], work["down_new"], rows, grad, other = (
-            lax.optimization_barrier(
-                (first, work["output_piece"], work["up_piece"], down_new, *work["joint"])
+        names = ("output_piece", "output_parts", "down_new", "up_shards")
+        first, rows, grad, other, *values = lax.optimization_barrier(
+            (
+                first,
+                *work["joint"],
+                work["output_piece"],
+                output_parts,
+                down_new,
+                work["up_shards"],
             )
         )
+        work.update(zip(names, values))
         work["joint_total"] = own_half(rows, grad, other)
         return first
 
@@ -1004,7 +1014,7 @@
     gateup_new = gateup_update(
         meta_core,
         work["shards"],
-        collect(work["up_piece"]),
+        work["up_shards"],
         [w_gateup, gateup_moment, gateup_square],
         32,
     )

time: 788 us -> 786 us (level)
  waiting for transfers between devices: 312 us -> 286 us
  starting transfers between devices: 67.2 us -> 84.2 us
    ppermute x5, waiting for transfers between devices: 13.4 us -> 0.01 us  [other_y(): return lax.ppermute(value, 'y', [(0, 1), (1, 0)])]
    all_gather x3, waiting for transfers between devices: 16.5 us -> 5.13 us  [gather_weight(): return lax.all_gather(piece, ('core', 'col'), axis=0, tiled=True)]
    ppermute x25, waiting for transfers between devices: 126 us -> 115 us  [shift(): lax.ppermute(value, axis, [(i, (i + by) % size) for i in range(size)])]
    all_gather x3, starting transfers between devices: 0.46 us -> 11 us  [gather_weight(): return lax.all_gather(piece, ('core', 'col'), axis=0, tiled=True)]
    unnamed x215 -> x233, local copies, waits for them, and re-layouts: 43 us -> 45.2 us
  transfers between devices with their start and end apart: 76 -> 76, of which waited for: 36 -> 34; matrix products, arithmetic and copies ran while one was open for 22% -> 23% of each run, Pallas kernels for 20% -> 20%
where the time goes in v4:
time: 786 us; the launch traced here: 772 us
  waiting for transfers between devices  286 us (36%)
  Pallas kernels  173 us (22%)
  matrix products  89.6 us (11%)
  starting transfers between devices  84.2 us (11%)
  local copies, waits for them, and re-layouts  74.8 us (10%)
  other arithmetic  49 us (6%)
  between operations  15.9 us (2%)
    ppermute x25, waiting for transfers between devices, shift(): lax.ppermute(value, axis, [(i, (i + by) % size) for i in range(size)])  115 us
    ppermute x4, waiting for transfers between devices, gather_tokens(): first = lax.ppermute(own, near, first_pairs)  73.1 us
    dot_general x10, matrix products, dot_tn(): lax.dot_general(left, right, (((0,), (0,)), ((), ())), preferred_element_...  57.9 us
    unnamed x233, local copies, waits for them, and re-layouts  45.2 us
    ppermute x25, starting transfers between devices, shift(): lax.ppermute(value, axis, [(i, (i + by) % size) for i in range(size)])  36.4 us
    pallas_call x1, Pallas kernels, gateup_update(): pl.pallas_call(gateup_update_kernel, grid_spec=pltpu.PrefetchScalarGridSp...  36 us
    pallas_call x2, Pallas kernels, widen_back(): pl.pallas_call(functools.partial(widen_back_kernel, slots, len(kept)), gr...  34.8 us
    dot_general x6, matrix products, dot_nt(): lax.dot_general(left, right, (((1,), (1,)), ((), ())), preferred_element_...  26.8 us
  transfers between devices with their start and end apart: 76, of which 34 were waited for; matrix products, arithmetic and copies ran while one was open for 23% of the time, Pallas kernels for 20%

profile of v4, /device:TPU:11, one launch (start us, length us, event | category | flops | bytes accessed | tf_op | source)
XLA Modules:
  0.0 772.2 jit_solution(9952111188921834215)
XLA Ops:
  47.5 20.1 %collective-permute-done.7.refs_1_ = bf16[256,2048]{1,0:T(8,128)(2,1)} collective-permute-done((bf16[256,2048]{1,0:T(8,128)(2,1)S(1)}, bf16[256,2048]{1,0:T(8,128)(2,1)}, u32[]{:S(2)}, u32[]{:S(2)}) %collective-permute-start.7) | collective-permute-done | bytes 1048608 | tf_op jit(solution)/shard_map/ppermute | solution.py:656
  78.2 9.5 %collective-permute-done.10 = bf16[256,512]{1,0:T(8,128)(2,1)} collective-permute-done((bf16[256,512]{1,0:T(8,128)(2,1)}, bf16[256,512]{1,0:T(8,128)(2,1)}, u32[]{:S(2)}, u32[]{:S(2)}) %collective-permute-start.10) | collective-permute-done | bytes 262176 | tf_op jit(solution)/shard_map/ppermute | solution.py:630
  87.7 23.2 %collective-permute-done.11 = bf16[256,512]{1,0:T(8,128)(2,1)} collective-permute-done((bf16[256,512]{1,0:T(8,128)(2,1)}, bf16[256,512]{1,0:T(8,128)(2,1)}, u32[]{:S(2)}, u32[]{:S(2)}) %collective-permute-start.11) | collective-permute-done | bytes 262176 | tf_op jit(solution)/shard_map/ppermute | solution.py:630
  133.7 19.2 %collective-permute-done.13.refs_1_ = bf16[256,2048]{1,0:T(8,128)(2,1)S(1)} collective-permute-done((bf16[256,2048]{1,0:T(8,128)(2,1)S(1)}, bf16[256,2048]{1,0:T(8,128)(2,1)S(1)}, u32[]{:S(2)}, u32[]{:S(2)}) %collective-permute-start.13) | collective-permute-done | bytes 1048608 | tf_op jit(solution)/shard_map/ppermute | solution.py:656
  161.6 8.6 %collective-permute-done.15.refs_1_ = bf16[256,2048]{1,0:T(8,128)(2,1)S(1)} collective-permute-done((bf16[256,2048]{1,0:T(8,128)(2,1)}, bf16[256,2048]{1,0:T(8,128)(2,1)S(1)}, u32[]{:S(2)}, u32[]{:S(2)}) %collective-permute-start.15) | collective-permute-done | bytes 1048608 | tf_op jit(solution)/shard_map/ppermute | solution.py:659
  170.7 11.0 %all-gather.11.cloned.1.call-start = ((), (), s32[]{:S(2)}) async-start(), calls=%async_computation.8 | async-start | bytes 6488064 | tf_op jit(solution)/shard_map/all_gather | solution.py:749
  185.1 15.4 %attend.1 = (bf16[1024,512]{1,0:T(8,128)(2,1)S(1)}, f32[4,2,1024]{2,1,0:T(2,128)S(1)}) custom-call(s32[17]{0:T(128)S(1)} %pad_add_fusion.7.meta_ref, bf16[1024,512]{1,0:T(8,128)(2,1)S(1)} %copy-done.50, bf16[4,4,256,256]{3,2,1,0:T(8,128)(2,1)S(1)} %copy-done.42, s32[4,2,256]{2,1,0:T(2,128)S(1)} %pad_add_fusion.2.info_ref.refs_4_), custom_call_target="tpu_custom_call" | custom-call | flops 3221225472 | bytes 4194304 | tf_op jit(solution)/shard_map/attend/pallas_call | solution.py:275
  210.0 9.6 %collective-permute-done.16 = bf16[256,2048]{1,0:T(8,128)(2,1)} collective-permute-done((bf16[256,2048]{1,0:T(8,128)(2,1)}, bf16[256,2048]{1,0:T(8,128)(2,1)}, u32[]{:S(2)}, u32[]{:S(2)}) %collective-permute-start.16) | collective-permute-done | bytes 1048608 | tf_op jit(solution)/shard_map/ppermute | solution.py:673
  219.6 11.2 %collective-permute-done.17 = bf16[256,2048]{1,0:T(8,128)(2,1)} collective-permute-done((bf16[256,2048]{1,0:T(8,128)(2,1)}, bf16[256,2048]{1,0:T(8,128)(2,1)}, u32[]{:S(2)}, u32[]{:S(2)}) %collective-permute-start.17) | collective-permute-done | bytes 1048608 | tf_op jit(solution)/shard_map/ppermute | solution.py:674
  233.8 12.9 %collective-permute-done.18 = bf16[256,2048]{1,0:T(8,128)(2,1)S(1)} collective-permute-done((bf16[256,2048]{1,0:T(8,128)(2,1)S(1)}, bf16[256,2048]{1,0:T(8,128)(2,1)S(1)}, u32[]{:S(2)}, u32[]{:S(2)}) %collective-permute-start.18) | collective-permute-done | bytes 1048608 | tf_op jit(solution)/shard_map/ppermute | solution.py:679
  251.5 18.8 %collective-permute-done.19.refs_1_ = bf16[256,2048]{1,0:T(8,128)(2,1)} collective-permute-done((bf16[256,2048]{1,0:T(8,128)(2,1)S(1)}, bf16[256,2048]{1,0:T(8,128)(2,1)}, u32[]{:S(2)}, u32[]{:S(2)}) %collective-permute-start.19) | collective-permute-done | bytes 1048608 | tf_op jit(solution)/shard_map/ppermute | solution.py:656
  279.2 9.3 %collective-permute-done.21.refs_3_ = bf16[256,2048]{1,0:T(8,128)(2,1)} collective-permute-done((bf16[256,2048]{1,0:T(8,128)(2,1)}, bf16[256,2048]{1,0:T(8,128)(2,1)}, u32[]{:S(2)}, u32[]{:S(2)}) %collective-permute-start.21) | collective-permute-done | bytes 1048608 | tf_op jit(solution)/shard_map/ppermute | solution.py:659
  291.1 19.9 %widen.1 = (bf16[1024,1408]{1,0:T(8,128)(2,1)}, bf16[1024,1408]{1,0:T(8,128)(2,1)}, bf16[1024,1408]{1,0:T(8,128)(2,1)}) custom-call(bf16[256,2048]{1,0:T(8,128)(2,1)S(1)} %copy-done.2, bf16[256,2048]{1,0:T(8,128)(2,1)} %collective-permute-done.19.refs_1_, bf16[256,2048]{1,0:T(8,128)(2,1)S(1)} %copy-done.26, ...), custom_call_target="tpu_custom_call" | custom-call | flops 11811160064 | bytes 24379392 | tf_op jit(solution)/shard_map/widen/pallas_call | solution.py:141
  327.2 8.5 %add_convert_fusion.2 = bf16[1024,1408]{1,0:T(8,128)(2,1)} fusion(bf16[1024,1408]{1,0:T(8,128)(2,1)} %collective-permute-done.22, bf16[1024,1408]{1,0:T(8,128)(2,1)} %get-tuple-element.213, bf16[1024,2048]{1,0:T(8,128)(2,1)} %constant_dynamic-update-slice_fusion.8, s32[]{:T(128)S(6)} %select_n.357), kind=kOutput, calls=%fused_computation.2 | convolution fusion | flops 2957115392 | bytes 10747908 | tf_op jit(solution)/shard_map/dot_general | solution.py:36
  343.7 18.4 %widen_back.2 = (bf16[1024,1408]{1,0:T(8,128)(2,1)}, bf16[1024,1408]{1,0:T(8,128)(2,1)}, bf16[512,2048]{1,0:T(8,128)(2,1)S(1)}) custom-call(bf16[256,2048]{1,0:T(8,128)(2,1)S(1)} %collective-permute-done.14.refs_0_, bf16[256,2048]{1,0:T(8,128)(2,1)S(1)} %collective-permute-done.15.refs_1_, bf16[2048,1408]{1,0:T(8,128)(2,1)} %all-gather.11.cloned.1.call-done.refs_2_, ...), custom_call_target="tpu_custom_call" | custom-call | flops 1476395008 | bytes 5767168 | tf_op jit(solution)/shard_map/widen_back/pallas_call | solution.py:179
  363.9 16.5 %widen_back.3 = (bf16[1024,1408]{1,0:T(8,128)(2,1)}, bf16[1024,1408]{1,0:T(8,128)(2,1)}, bf16[512,2048]{1,0:T(8,128)(2,1)S(1)}) custom-call(bf16[256,2048]{1,0:T(8,128)(2,1)S(1)} %slice_dynamic-update-slice_fusion.refs_0_, bf16[256,2048]{1,0:T(8,128)(2,1)S(1)} %copy-done.5, ...), custom_call_target="tpu_custom_call", output_to_operand_aliasing={{0}: (6, {}), {1}: (7, {})} | custom-call | flops 1476395008 | bytes 5767168 | tf_op jit(solution)/shard_map/widen_back/pallas_call | solution.py:179
  434.7 15.1 %collective-permute-done.28 = bf16[256,2048]{1,0:T(8,128)(2,1)S(1)} collective-permute-done((bf16[256,2048]{1,0:T(8,128)(2,1)}, bf16[256,2048]{1,0:T(8,128)(2,1)S(1)}, u32[]{:S(2)}, u32[]{:S(2)}) %collective-permute-start.28) | collective-permute-done | bytes 1048608 | tf_op jit(solution)/shard_map/ppermute | solution.py:656
  475.0 26.4 %attend_back.1 = (bf16[1024,512]{1,0:T(8,128)(2,1)S(1)}, bf16[4,256,256]{2,1,0:T(8,128)(2,1)S(1)}, bf16[4,256,256]{2,1,0:T(8,128)(2,1)S(1)}, bf16[4,256,256]{2,1,0:T(8,128)(2,1)S(1)}, bf16[4,256,256]{2,1,0:T(8,128)(2,1)S(1)}) custom-call(s32[17]{0:T(128)S(1)} %pad_add_fusion.7.meta_ref, bf16[1024,512]{1,0:T(8,128)(2,1)S(1)} %copy-done.51, ...), custom_call_target="tpu_custom_call" | custom-call | flops 8053063680 | bytes 8388608 | tf_op jit(solution)/shard_map/attend_back/pallas_call | solution.py:387
  522.7 17.8 %collective-permute-done.34.refs_1_ = bf16[1024,256]{1,0:T(8,128)(2,1)S(1)} collective-permute-done((bf16[1024,256]{1,0:T(8,128)(2,1)S(1)}, bf16[1024,256]{1,0:T(8,128)(2,1)S(1)}, u32[]{:S(2)}, u32[]{:S(2)}) %collective-permute-start.34) | collective-permute-done | bytes 524320 | tf_op jit(solution)/shard_map/ppermute | solution.py:630
  544.7 17.1 %collective-permute-done.35.refs_2_ = bf16[1024,256]{1,0:T(8,128)(2,1)S(1)} collective-permute-done((bf16[1024,256]{1,0:T(8,128)(2,1)S(1)}, bf16[1024,256]{1,0:T(8,128)(2,1)S(1)}, u32[]{:S(2)}, u32[]{:S(2)}) %collective-permute-start.35) | collective-permute-done | bytes 524320 | tf_op jit(solution)/shard_map/ppermute | solution.py:630
  632.5 15.2 %turned_update.2 = (f32[2816,512]{1,0:T(8,128)}, f32[2816,512]{1,0:T(8,128)}, f32[2816,512]{1,0:T(8,128)}) custom-call(s32[2]{0:T(128)S(1)} %pad_add_fusion.8.meta_ref, bf16[512,1408]{1,0:T(8,128)(2,1)S(1)} %constant_dynamic-update-slice_fusion.12.refs_0_, bf16[512,1408]{1,0:T(8,128)(2,1)S(1)} %collective-permute-done.40.refs_1_, ...), custom_call_target="tpu_custom_call" | custom-call | flops 28835840 | bytes 34603008 | tf_op jit(solution)/shard_map/turned_update/pallas_call | solution.py:540
  647.7 17.3 %collective-permute-done.49 = bf16[256,512]{1,0:T(8,128)(2,1)S(1)} collective-permute-done((bf16[256,512]{1,0:T(8,128)(2,1)S(1)}, bf16[256,512]{1,0:T(8,128)(2,1)S(1)}, u32[]{:S(2)}, u32[]{:S(2)}) %collective-permute-start.49) | collective-permute-done | bytes 262176 | tf_op jit(solution)/shard_map/ppermute | solution.py:630
  687.6 36.0 %gateup_update.1 = (f32[512,2,2816]{2,1,0:T(2,128)}, f32[512,2,2816]{2,1,0:T(2,128)}, f32[512,2,2816]{2,1,0:T(2,128)}) custom-call(s32[2]{0:T(128)S(1)} %pad_add_fusion.8.meta_ref, bf16[512,1408]{1,0:T(8,128)(2,1)S(1)} %constant_dynamic-update-slice_fusion.12.refs_0_, bf16[512,1408]{1,0:T(8,128)(2,1)S(1)} %collective-permute-done.40.refs_1_, ...), custom_call_target="tpu_custom_call" | custom-call | flops 57671680 | bytes 80740352 | tf_op jit(solution)/shard_map/gateup_update/pallas_call | solution.py:577
  756.0 9.5 %joint_update.1 = (f32[512,1024]{1,0:T(8,128)}, f32[512,1024]{1,0:T(8,128)}, f32[512,1024]{1,0:T(8,128)}, f32[512,512]{1,0:T(8,128)}, f32[512,512]{1,0:T(8,128)}, /*index=5*/f32[512,512]{1,0:T(8,128)}) custom-call(s32[2]{0:T(128)S(1)} %pad_add_fusion.8.meta_ref, bf16[256,768]{1,0:T(8,128)(2,1)S(1)} %pad_maximum_fusion.12.refs_0_, ...), custom_call_target="tpu_custom_call" | custom-call | flops 15728640 | bytes 18874368 | tf_op jit(solution)/shard_map/joint_update/pallas_call | solution.py:498
  (540 shorter events, 369.9 us)
Async XLA Ops:
  7.2 108.5 %all-gather.5.cloned.1.call-start = ((), (), s32[]{:S(2)}) async-start(), calls=%async_computation.5 | async-start | bytes 5898240 | tf_op jit(solution)/shard_map/all_gather | solution.py:749
  35.8 134.9 %all-gather.7.cloned.1.call-start = ((), (), s32[]{:S(2)}) async-start(), calls=%async_computation.6 | async-start | bytes 2621440 | tf_op jit(solution)/shard_map/all_gather | solution.py:837
  70.8 42.7 %collective-permute-start.9 = (bf16[256,2048]{1,0:T(8,128)(2,1)}, bf16[256,2048]{1,0:T(8,128)(2,1)}, u32[]{:S(2)}, u32[]{:S(2)}) collective-permute-start(bf16[256,2048]{1,0:T(8,128)(2,1)} %collective-permute-done.7.refs_1_), channel_id=1, source_target_pairs={{0,16},{4,20},{8,12},{12,8},{16,0},{20,4},{24,28},{28,24},{1,17},{... | collective-permute-start | bytes 3145736 | tf_op jit(solution)/shard_map/ppermute | solution.py:659
  72.1 38.8 %collective-permute-start.11 = (bf16[256,512]{1,0:T(8,128)(2,1)}, bf16[256,512]{1,0:T(8,128)(2,1)}, u32[]{:S(2)}, u32[]{:S(2)}) collective-permute-start(bf16[256,512]{1,0:T(8,128)(2,1)} %get-tuple-element.367), channel_id=1, source_target_pairs={{0,2},{1,3},{2,0},{3,1},{4,6},{5,7},{6,4},{7,5},{8,10},{9,11},{10,... | collective-permute-start | bytes 786440 | tf_op jit(solution)/shard_map/ppermute | solution.py:630
  75.2 38.2 %collective-permute-start.12 = (bf16[256,512]{1,0:T(8,128)(2,1)}, bf16[256,512]{1,0:T(8,128)(2,1)}, u32[]{:S(2)}, u32[]{:S(2)}) collective-permute-start(bf16[256,512]{1,0:T(8,128)(2,1)} %get-tuple-element.366), channel_id=1, source_target_pairs={{0,3},{1,0},{2,1},{3,2},{4,7},{5,4},{6,5},{7,6},{8,11},{9,8},{10,9... | collective-permute-start | bytes 786440 | tf_op jit(solution)/shard_map/ppermute | solution.py:630
  126.7 161.8 %all-gather.9.cloned.1.call-start = ((), (), s32[]{:S(2)}) async-start(), calls=%async_computation.7 | async-start | bytes 12976128 | tf_op jit(solution)/shard_map/all_gather | solution.py:749
  170.7 170.1 %all-gather.11.cloned.1.call-start = ((), (), s32[]{:S(2)}) async-start(), calls=%async_computation.8 | async-start | bytes 6488064 | tf_op jit(solution)/shard_map/all_gather | solution.py:749
  206.9 191.9 %reduce-scatter.6.cloned.1.call-start = ((), (), s32[]{:S(2)}) async-start(), calls=%async_computation.9 | async-start | bytes 3604480 | tf_op jit(solution)/shard_map/reduce_scatter | solution.py:861
  340.8 164.0 %reduce-scatter.8.cloned.1.call-start = ((), (), s32[]{:S(2)}) async-start(), calls=%async_computation.10 | async-start | bytes 3604480 | tf_op jit(solution)/shard_map/reduce_scatter | solution.py:861
  416.2 157.5 %reduce-scatter.10.cloned.1.call-start = ((), (), s32[]{:S(2)}) async-start(), calls=%async_computation.11 | async-start | bytes 3604480 | tf_op jit(solution)/shard_map/reduce_scatter | solution.py:861
  433.6 234.0 %reduce-scatter.12.cloned.1.call-start = ((), (), s32[]{:S(2)}) async-start(), calls=%async_computation.12 | async-start | bytes 1310720 | tf_op jit(solution)/shard_map/reduce_scatter | solution.py:861
  507.9 65.8 %collective-permute-start.33 = (bf16[256,2048]{1,0:T(8,128)(2,1)}, bf16[256,2048]{1,0:T(8,128)(2,1)}, u32[]{:S(2)}, u32[]{:S(2)}) collective-permute-start(bf16[256,2048]{1,0:T(8,128)(2,1)} %add_convert_fusion.7), channel_id=1, source_target_pairs={{0,4},{4,0},{8,24},{12,28},{16,20},{20,16},{24,8},{28,12},{1,5},{5... | collective-permute-start | bytes 3145736 | tf_op jit(solution)/shard_map/ppermute | solution.py:679
  509.5 75.9 %collective-permute-start.40 = (bf16[512,1408]{1,0:T(8,128)(2,1)S(1)}, bf16[512,1408]{1,0:T(8,128)(2,1)S(1)}, u32[]{:S(2)}, u32[]{:S(2)}) collective-permute-start(bf16[512,1408]{1,0:T(8,128)(2,1)S(1)} %constant_dynamic-update-slice_fusion.12.refs_0_), channel_id=1, source_target_pairs={{0,16},{16,0},{1,17},{17,1},{2,18},{18,2},{3,19},{19,3},{4,20},{20... | collective-permute-start | bytes 4325384 | tf_op jit(solution)/shard_map/ppermute | solution.py:636
  513.0 48.7 %collective-permute-start.35 = (bf16[1024,256]{1,0:T(8,128)(2,1)S(1)}, bf16[1024,256]{1,0:T(8,128)(2,1)S(1)}, u32[]{:S(2)}, u32[]{:S(2)}) collective-permute-start(bf16[1024,256]{1,0:T(8,128)(2,1)S(1)} %bitcast.188), channel_id=1, source_target_pairs={{0,2},{1,3},{2,0},{3,1},{4,6},{5,7},{6,4},{7,5},{8,10},{9,11},{10,... | collective-permute-start | bytes 1572872 | tf_op jit(solution)/shard_map/ppermute | solution.py:630
  520.4 52.6 %collective-permute-start.36 = (bf16[1024,256]{1,0:T(8,128)(2,1)S(1)}, bf16[1024,256]{1,0:T(8,128)(2,1)S(1)}, u32[]{:S(2)}, u32[]{:S(2)}) collective-permute-start(bf16[1024,256]{1,0:T(8,128)(2,1)S(1)} %bitcast.187), channel_id=1, source_target_pairs={{0,1},{1,2},{2,3},{3,0},{4,5},{5,6},{6,7},{7,4},{8,9},{9,10},{10,1... | collective-permute-start | bytes 1572872 | tf_op jit(solution)/shard_map/ppermute | solution.py:630
  541.3 51.6 %collective-permute-start.41 = (bf16[512,1408]{1,0:T(8,128)(2,1)S(1)}, bf16[512,1408]{1,0:T(8,128)(2,1)}, u32[]{:S(2)}, u32[]{:S(2)}) collective-permute-start(bf16[512,1408]{1,0:T(8,128)(2,1)S(1)} %constant_dynamic-update-slice_fusion.12.refs_0_), channel_id=1, source_target_pairs={{0,8},{8,0},{1,9},{9,1},{2,10},{10,2},{3,11},{11,3},{4,12},{12,4},... | collective-permute-start | bytes 4325384 | tf_op jit(solution)/shard_map/ppermute | solution.py:633
  613.5 115.7 %reduce-scatter.14.cloned.1.call-start = ((), (), s32[]{:S(2)}) async-start(), calls=%async_computation.13 | async-start | bytes 1966080 | tf_op jit(solution)/shard_map/reduce_scatter | solution.py:861
  615.6 52.0 %collective-permute-start.47 = (bf16[1024,768]{1,0:T(8,128)(2,1)}, bf16[1024,768]{1,0:T(8,128)(2,1)}, u32[]{:S(2)}, u32[]{:S(2)}) collective-permute-start(bf16[1024,768]{1,0:T(8,128)(2,1)} %fusion.25), channel_id=1, source_target_pairs={{0,8},{8,0},{1,9},{9,1},{2,10},{10,2},{3,11},{11,3},{4,12},{12,4},... | collective-permute-start | bytes 4718600 | tf_op jit(solution)/shard_map/ppermute | solution.py:633
  619.9 47.0 %collective-permute-start.46 = (bf16[256,2048]{1,0:T(8,128)(2,1)S(1)}, bf16[256,2048]{1,0:T(8,128)(2,1)}, u32[]{:S(2)}, u32[]{:S(2)}) collective-permute-start(bf16[256,2048]{1,0:T(8,128)(2,1)S(1)} %add_convert_fusion.5), channel_id=1, source_target_pairs={{0,4},{4,0},{8,24},{12,28},{16,20},{20,16},{24,8},{28,12},{1,5},{5... | collective-permute-start | bytes 3145736 | tf_op jit(solution)/shard_map/ppermute | solution.py:679
  673.2 50.5 %collective-permute-start.64 = (bf16[256,512]{1,0:T(8,128)(2,1)S(1)}, bf16[256,512]{1,0:T(8,128)(2,1)S(1)}, u32[]{:S(2)}, u32[]{:S(2)}) collective-permute-start(bf16[256,512]{1,0:T(8,128)(2,1)S(1)} %copy-done.41), channel_id=1, source_target_pairs={{0,16},{16,0},{1,17},{17,1},{2,18},{18,2},{3,19},{19,3},{4,20},{20... | collective-permute-start | bytes 786440 | tf_op jit(solution)/shard_map/ppermute | solution.py:636
  674.3 62.5 %collective-permute-start.65 = (bf16[256,512]{1,0:T(8,128)(2,1)S(1)}, bf16[256,512]{1,0:T(8,128)(2,1)}, u32[]{:S(2)}, u32[]{:S(2)}) collective-permute-start(bf16[256,512]{1,0:T(8,128)(2,1)S(1)} %copy-done.41), channel_id=1, source_target_pairs={{0,8},{8,0},{1,9},{9,1},{2,10},{10,2},{3,11},{11,3},{4,12},{12,4},... | collective-permute-start | bytes 786440 | tf_op jit(solution)/shard_map/ppermute | solution.py:633
  683.2 41.4 %collective-permute-start.51 = (bf16[256,512]{1,0:T(8,128)(2,1)S(1)}, bf16[256,512]{1,0:T(8,128)(2,1)S(1)}, u32[]{:S(2)}, u32[]{:S(2)}) collective-permute-start(bf16[256,512]{1,0:T(8,128)(2,1)S(1)} %get-tuple-element.336), channel_id=1, source_target_pairs={{0,1},{1,2},{2,3},{3,0},{4,5},{5,6},{6,7},{7,4},{8,9},{9,10},{10,1... | collective-permute-start | bytes 786440 | tf_op jit(solution)/shard_map/ppermute | solution.py:630
  683.2 43.9 %collective-permute-start.52 = (bf16[256,512]{1,0:T(8,128)(2,1)S(1)}, bf16[256,512]{1,0:T(8,128)(2,1)S(1)}, u32[]{:S(2)}, u32[]{:S(2)}) collective-permute-start(bf16[256,512]{1,0:T(8,128)(2,1)S(1)} %get-tuple-element.335), channel_id=1, source_target_pairs={{0,2},{1,3},{2,0},{3,1},{4,6},{5,7},{6,4},{7,5},{8,10},{9,11},{10,... | collective-permute-start | bytes 786440 | tf_op jit(solution)/shard_map/ppermute | solution.py:630
  684.2 44.9 %collective-permute-start.53 = (bf16[256,512]{1,0:T(8,128)(2,1)S(1)}, bf16[256,512]{1,0:T(8,128)(2,1)}, u32[]{:S(2)}, u32[]{:S(2)}) collective-permute-start(bf16[256,512]{1,0:T(8,128)(2,1)S(1)} %get-tuple-element.334), channel_id=1, source_target_pairs={{0,3},{1,0},{2,1},{3,2},{4,7},{5,4},{6,5},{7,6},{8,11},{9,8},{10,9... | collective-permute-start | bytes 786440 | tf_op jit(solution)/shard_map/ppermute | solution.py:630
  (152 other events, 1688.6 us)
Sparse Core Ops, SparseCore 0:
  35.9 72.4 all-gather.4
  126.8 43.8 all-gather.6
  172.9 106.3 all-gather.8
  281.3 59.4 all-gather.10
  342.9 55.8 reduce-scatter.5
  416.3 55.7 reduce-scatter.7
  475.0 79.7 reduce-scatter.9
  613.6 48.6 reduce-scatter.11
  673.3 54.8 reduce-scatter.13

commit v5 on v4

--- a/solution.py
+++ b/solution.py
@@ -970,7 +970,8 @@
             return product(grad_joint, joint_weight)(first, last)
         output_total = own_half(back, mixed, other_core(other_half(back, mixed)))
         shards = collect(jnp.concatenate([work["down_piece"], work["gate_piece"]], axis=0))
-        close, work["output"], work["shards"], work["up_shards"] = lax.optimization_barrier(
+        names = ("output", "shards", "up_shards")
+        close, *values = lax.optimization_barrier(
             (
                 product(grad_joint, joint_weight)(first, last),
                 output_total,
@@ -978,6 +979,7 @@
                 collect(work["up_piece"]),
             )
         )
+        work.update(zip(names, values))
         return close
 
     def joint_others(key):
@@ -994,13 +996,12 @@
             FF ** (-0.5),
             False,
         )
-        names = ("output_piece", "output_parts", "down_new", "up_shards")
+        names = ("output_piece", "down_new", "up_shards")
         first, rows, grad, other, *values = lax.optimization_barrier(
             (
                 first,
                 *work["joint"],
                 work["output_piece"],
-                output_parts,
                 down_new,
                 work["up_shards"],
             )
@@ -1020,35 +1021,8 @@
     )
     input_grad = grad_middle + norm_back(residual, scale_one, grad_normed_one, gains[0])
     gain_one = jnp.sum(grad_normed_one * residual * scale_one, axis=0)
-    joint_piece, input_parts, gateup_new = lax.optimization_barrier(
-        (joint_piece, features_sent(input_grad.astype(jnp.bfloat16)), gateup_new)
-    )
-    layer_output = features_of(work["output_parts"])
-    input_grad = features_of(input_parts).astype(jnp.float32)
-    pair_piece = joint_piece[:, query_width:]
-    pair_total = pair_piece.astype(jnp.float32)
-    for by in range(1, rows_on):
-        pair_total = pair_total + shift(pair_piece, "row", rows_on, by).astype(jnp.float32)
-    joint_piece = jnp.concatenate(
-        [joint_piece[:, :query_width], pair_total.astype(jnp.bfloat16)], axis=1
-    )
-    joint_new = joint_update(
-        meta_core,
-        collect(joint_piece),
-        [w_query, query_moment, query_square],
-        [w_keyvalue, keyvalue_moment, keyvalue_square],
-    )
-    output_new = turned_update(
-        meta_core,
-        collect(work["output_piece"]),
-        [w_output, output_moment, output_square],
-        (HEADS * HEAD_DIM // 64) ** (-0.5),
-        True,
-    )
-
     gain_sums = jnp.stack([gain_one, gain_two])
-    gain_sums, gateup_new = lax.optimization_barrier((gain_sums, gateup_new))
-    blocks = [
+    gain_blocks = [
         jnp.concatenate(
             [
                 gain_sums[:, at * half : (at + 1) * half],
@@ -1058,13 +1032,40 @@
         )
         for at in range(lines)
     ]
-    grad_gains = pick(blocks, line)
-    for by in range(1, lines):
-        grad_gains = grad_gains + shift(pick(blocks, (line + by) % lines), "col", lines, by)
+    gain_parts = [pick(gain_blocks, line)] + [
+        shift(pick(gain_blocks, (line + by) % lines), "col", lines, by) for by in range(1, lines)
+    ]
+    joint_piece, input_grad, gateup_new, output_parts, gain_parts = lax.optimization_barrier(
+        (joint_piece, input_grad.astype(jnp.bfloat16), gateup_new, output_parts, gain_parts)
+    )
+    grad_gains = sum(gain_parts[1:], gain_parts[0])
     for axis, size in (("core", 2), ("y", 2), ("row", rows_on)):
-        blocks_total = grad_gains
+        own_gains = grad_gains
         for by in range(1, size):
-            grad_gains = grad_gains + shift(blocks_total, axis, size, by)
+            grad_gains = grad_gains + shift(own_gains, axis, size, by)
+    input_parts = features_sent(input_grad)
+    layer_output = features_of(output_parts)
+    input_grad = features_of(input_parts).astype(jnp.float32)
+    pair_piece = joint_piece[:, query_width:]
+    pair_total = pair_piece.astype(jnp.float32)
+    for by in range(1, rows_on):
+        pair_total = pair_total + shift(pair_piece, "row", rows_on, by).astype(jnp.float32)
+    joint_piece = jnp.concatenate(
+        [joint_piece[:, :query_width], pair_total.astype(jnp.bfloat16)], axis=1
+    )
+    joint_new = joint_update(
+        meta_core,
+        collect(joint_piece),
+        [w_query, query_moment, query_square],
+        [w_keyvalue, keyvalue_moment, keyvalue_square],
+    )
+    output_new = turned_update(
+        meta_core,
+        collect(work["output_piece"]),
+        [w_output, output_moment, output_square],
+        (HEADS * HEAD_DIM // 64) ** (-0.5),
+        True,
+    )
 
     gains_new = adamw_step(norm_gains, grad_gains, gains_moment, gains_square, 0.6, 0.0)
     return (

time: 786 us -> 791 us (level)
  starting transfers between devices: 84.2 us -> 94.5 us
  Pallas kernels: 173 us -> 165 us
  waiting for transfers between devices: 286 us -> 294 us
    ppermute x25, starting transfers between devices: 36.4 us -> 46.4 us  [shift(): lax.ppermute(value, axis, [(i, (i + by) % size) for i in range(size)])]
    unnamed x233 -> x215, local copies, waits for them, and re-layouts: 45.2 us -> 43.8 us
  transfers between devices with their start and end apart: 76 -> 76, of which waited for: 34 -> 35; matrix products, arithmetic and copies ran while one was open for 23% -> 22% of each run, Pallas kernels for 20% -> 19%
where the time goes in v5:
time: 791 us; the launch traced here: 779 us
  waiting for transfers between devices  294 us (37%)
  Pallas kernels  165 us (21%)
  starting transfers between devices  94.5 us (12%)
  matrix products  89.5 us (11%)
  local copies, waits for them, and re-layouts  69.8 us (9%)
  other arithmetic  49.7 us (6%)
  between operations  15.8 us (2%)
    ppermute x25, waiting for transfers between devices, shift(): lax.ppermute(value, axis, [(i, (i + by) % size) for i in range(size)])  113 us
    ppermute x4, waiting for transfers between devices, gather_tokens(): first = lax.ppermute(own, near, first_pairs)  72.9 us
    dot_general x10, matrix products, dot_tn(): lax.dot_general(left, right, (((0,), (0,)), ((), ())), preferred_element_...  57.8 us
    ppermute x25, starting transfers between devices, shift(): lax.ppermute(value, axis, [(i, (i + by) % size) for i in range(size)])  46.4 us
    unnamed x215, local copies, waits for them, and re-layouts  43.8 us
    pallas_call x1, Pallas kernels, gateup_update(): pl.pallas_call(gateup_update_kernel, grid_spec=pltpu.PrefetchScalarGridSp...  36 us
    pallas_call x2, Pallas kernels, widen_back(): pl.pallas_call(functools.partial(widen_back_kernel, slots, len(kept)), gr...  34.8 us
    dot_general x6, matrix products, dot_nt(): lax.dot_general(left, right, (((1,), (1,)), ((), ())), preferred_element_...  26.7 us
  transfers between devices with their start and end apart: 76, of which 35 were waited for; matrix products, arithmetic and copies ran while one was open for 22% of the time, Pallas kernels for 19%

profile of v5, /device:TPU:11, one launch (start us, length us, event | category | flops | bytes accessed | tf_op | source)
XLA Modules:
  0.0 778.5 jit_solution(3637557329592973311)
XLA Ops:
  47.5 20.1 %collective-permute-done.7.refs_1_ = bf16[256,2048]{1,0:T(8,128)(2,1)} collective-permute-done((bf16[256,2048]{1,0:T(8,128)(2,1)S(1)}, bf16[256,2048]{1,0:T(8,128)(2,1)}, u32[]{:S(2)}, u32[]{:S(2)}) %collective-permute-start.7) | collective-permute-done | bytes 1048608 | tf_op jit(solution)/shard_map/ppermute | solution.py:656
  78.2 9.5 %collective-permute-done.10 = bf16[256,512]{1,0:T(8,128)(2,1)} collective-permute-done((bf16[256,512]{1,0:T(8,128)(2,1)}, bf16[256,512]{1,0:T(8,128)(2,1)}, u32[]{:S(2)}, u32[]{:S(2)}) %collective-permute-start.10) | collective-permute-done | bytes 262176 | tf_op jit(solution)/shard_map/ppermute | solution.py:630
  87.7 23.2 %collective-permute-done.11 = bf16[256,512]{1,0:T(8,128)(2,1)} collective-permute-done((bf16[256,512]{1,0:T(8,128)(2,1)}, bf16[256,512]{1,0:T(8,128)(2,1)}, u32[]{:S(2)}, u32[]{:S(2)}) %collective-permute-start.11) | collective-permute-done | bytes 262176 | tf_op jit(solution)/shard_map/ppermute | solution.py:630
  133.7 19.2 %collective-permute-done.13.refs_1_ = bf16[256,2048]{1,0:T(8,128)(2,1)S(1)} collective-permute-done((bf16[256,2048]{1,0:T(8,128)(2,1)S(1)}, bf16[256,2048]{1,0:T(8,128)(2,1)S(1)}, u32[]{:S(2)}, u32[]{:S(2)}) %collective-permute-start.13) | collective-permute-done | bytes 1048608 | tf_op jit(solution)/shard_map/ppermute | solution.py:656
  161.5 8.6 %collective-permute-done.15.refs_1_ = bf16[256,2048]{1,0:T(8,128)(2,1)S(1)} collective-permute-done((bf16[256,2048]{1,0:T(8,128)(2,1)}, bf16[256,2048]{1,0:T(8,128)(2,1)S(1)}, u32[]{:S(2)}, u32[]{:S(2)}) %collective-permute-start.15) | collective-permute-done | bytes 1048608 | tf_op jit(solution)/shard_map/ppermute | solution.py:659
  170.7 10.9 %all-gather.11.cloned.1.call-start = ((), (), s32[]{:S(2)}) async-start(), calls=%async_computation.8 | async-start | bytes 6488064 | tf_op jit(solution)/shard_map/all_gather | solution.py:749
  185.0 11.7 %attend.1 = (bf16[1024,512]{1,0:T(8,128)(2,1)S(1)}, f32[4,2,1024]{2,1,0:T(2,128)S(1)}) custom-call(s32[17]{0:T(128)S(1)} %pad_add_fusion.7.meta_ref, bf16[1024,512]{1,0:T(8,128)(2,1)S(1)} %copy-done.49, bf16[4,4,256,256]{3,2,1,0:T(8,128)(2,1)S(1)} %copy-done.41, s32[4,2,256]{2,1,0:T(2,128)S(1)} %pad_add_fusion.2.info_ref.refs_4_), custom_call_target="tpu_custom_call" | custom-call | flops 3221225472 | bytes 4194304 | tf_op jit(solution)/shard_map/attend/pallas_call | solution.py:275
  206.1 9.7 %collective-permute-done.16 = bf16[256,2048]{1,0:T(8,128)(2,1)} collective-permute-done((bf16[256,2048]{1,0:T(8,128)(2,1)}, bf16[256,2048]{1,0:T(8,128)(2,1)}, u32[]{:S(2)}, u32[]{:S(2)}) %collective-permute-start.16) | collective-permute-done | bytes 1048608 | tf_op jit(solution)/shard_map/ppermute | solution.py:673
  215.8 11.2 %collective-permute-done.17 = bf16[256,2048]{1,0:T(8,128)(2,1)} collective-permute-done((bf16[256,2048]{1,0:T(8,128)(2,1)}, bf16[256,2048]{1,0:T(8,128)(2,1)}, u32[]{:S(2)}, u32[]{:S(2)}) %collective-permute-start.17) | collective-permute-done | bytes 1048608 | tf_op jit(solution)/shard_map/ppermute | solution.py:674
  229.9 12.9 %collective-permute-done.18 = bf16[256,2048]{1,0:T(8,128)(2,1)S(1)} collective-permute-done((bf16[256,2048]{1,0:T(8,128)(2,1)S(1)}, bf16[256,2048]{1,0:T(8,128)(2,1)S(1)}, u32[]{:S(2)}, u32[]{:S(2)}) %collective-permute-start.18) | collective-permute-done | bytes 1048608 | tf_op jit(solution)/shard_map/ppermute | solution.py:679
  247.6 18.5 %collective-permute-done.19.refs_1_ = bf16[256,2048]{1,0:T(8,128)(2,1)} collective-permute-done((bf16[256,2048]{1,0:T(8,128)(2,1)S(1)}, bf16[256,2048]{1,0:T(8,128)(2,1)}, u32[]{:S(2)}, u32[]{:S(2)}) %collective-permute-start.19) | collective-permute-done | bytes 1048608 | tf_op jit(solution)/shard_map/ppermute | solution.py:656
  275.0 9.3 %collective-permute-done.21.refs_3_ = bf16[256,2048]{1,0:T(8,128)(2,1)} collective-permute-done((bf16[256,2048]{1,0:T(8,128)(2,1)}, bf16[256,2048]{1,0:T(8,128)(2,1)}, u32[]{:S(2)}, u32[]{:S(2)}) %collective-permute-start.21) | collective-permute-done | bytes 1048608 | tf_op jit(solution)/shard_map/ppermute | solution.py:659
  286.8 20.7 %widen.1 = (bf16[1024,1408]{1,0:T(8,128)(2,1)}, bf16[1024,1408]{1,0:T(8,128)(2,1)}, bf16[1024,1408]{1,0:T(8,128)(2,1)}) custom-call(bf16[256,2048]{1,0:T(8,128)(2,1)S(1)} %copy-done.2, bf16[256,2048]{1,0:T(8,128)(2,1)} %collective-permute-done.19.refs_1_, bf16[256,2048]{1,0:T(8,128)(2,1)S(1)} %copy-done.25, ...), custom_call_target="tpu_custom_call" | custom-call | flops 11811160064 | bytes 24379392 | tf_op jit(solution)/shard_map/widen/pallas_call | solution.py:141
  343.7 18.4 %widen_back.2 = (bf16[1024,1408]{1,0:T(8,128)(2,1)}, bf16[1024,1408]{1,0:T(8,128)(2,1)}, bf16[512,2048]{1,0:T(8,128)(2,1)S(1)}) custom-call(bf16[256,2048]{1,0:T(8,128)(2,1)S(1)} %collective-permute-done.14.refs_0_, bf16[256,2048]{1,0:T(8,128)(2,1)S(1)} %collective-permute-done.15.refs_1_, bf16[2048,1408]{1,0:T(8,128)(2,1)} %all-gather.11.cloned.1.call-done.refs_2_, ...), custom_call_target="tpu_custom_call" | custom-call | flops 1476395008 | bytes 5767168 | tf_op jit(solution)/shard_map/widen_back/pallas_call | solution.py:179
  363.9 16.4 %widen_back.3 = (bf16[1024,1408]{1,0:T(8,128)(2,1)}, bf16[1024,1408]{1,0:T(8,128)(2,1)}, bf16[512,2048]{1,0:T(8,128)(2,1)S(1)}) custom-call(bf16[256,2048]{1,0:T(8,128)(2,1)S(1)} %slice_dynamic-update-slice_fusion.refs_0_, bf16[256,2048]{1,0:T(8,128)(2,1)S(1)} %copy-done.5, ...), custom_call_target="tpu_custom_call", output_to_operand_aliasing={{0}: (6, {}), {1}: (7, {})} | custom-call | flops 1476395008 | bytes 5767168 | tf_op jit(solution)/shard_map/widen_back/pallas_call | solution.py:179
  434.7 15.1 %collective-permute-done.28 = bf16[256,2048]{1,0:T(8,128)(2,1)S(1)} collective-permute-done((bf16[256,2048]{1,0:T(8,128)(2,1)}, bf16[256,2048]{1,0:T(8,128)(2,1)S(1)}, u32[]{:S(2)}, u32[]{:S(2)}) %collective-permute-start.28) | collective-permute-done | bytes 1048608 | tf_op jit(solution)/shard_map/ppermute | solution.py:656
  474.9 21.7 %attend_back.1 = (bf16[1024,512]{1,0:T(8,128)(2,1)S(1)}, bf16[4,256,256]{2,1,0:T(8,128)(2,1)S(1)}, bf16[4,256,256]{2,1,0:T(8,128)(2,1)S(1)}, bf16[4,256,256]{2,1,0:T(8,128)(2,1)S(1)}, bf16[4,256,256]{2,1,0:T(8,128)(2,1)S(1)}) custom-call(s32[17]{0:T(128)S(1)} %pad_add_fusion.7.meta_ref, bf16[1024,512]{1,0:T(8,128)(2,1)S(1)} %copy-done.50, ...), custom_call_target="tpu_custom_call" | custom-call | flops 8053063680 | bytes 8388608 | tf_op jit(solution)/shard_map/attend_back/pallas_call | solution.py:387
  508.3 9.6 %collective-permute-start.35 = (bf16[1024,256]{1,0:T(8,128)(2,1)S(1)}, bf16[1024,256]{1,0:T(8,128)(2,1)S(1)}, u32[]{:S(2)}, u32[]{:S(2)}) collective-permute-start(bf16[1024,256]{1,0:T(8,128)(2,1)S(1)} %bitcast.179), channel_id=1, source_target_pairs={{0,2},{1,3},{2,0},{3,1},{4,6},{5,7},{6,4},{7,5},{8,10},{9,11},{10,... | collective-permute-start | bytes 1572872 | tf_op jit(solution)/shard_map/ppermute | solution.py:630
  523.4 18.0 %collective-permute-done.34.refs_1_ = bf16[1024,256]{1,0:T(8,128)(2,1)S(1)} collective-permute-done((bf16[1024,256]{1,0:T(8,128)(2,1)S(1)}, bf16[1024,256]{1,0:T(8,128)(2,1)S(1)}, u32[]{:S(2)}, u32[]{:S(2)}) %collective-permute-start.34) | collective-permute-done | bytes 524320 | tf_op jit(solution)/shard_map/ppermute | solution.py:630
  542.6 19.1 %collective-permute-done.35.refs_2_ = bf16[1024,256]{1,0:T(8,128)(2,1)S(1)} collective-permute-done((bf16[1024,256]{1,0:T(8,128)(2,1)S(1)}, bf16[1024,256]{1,0:T(8,128)(2,1)S(1)}, u32[]{:S(2)}, u32[]{:S(2)}) %collective-permute-start.35) | collective-permute-done | bytes 524320 | tf_op jit(solution)/shard_map/ppermute | solution.py:630
  621.5 15.0 %turned_update.2 = (f32[2816,512]{1,0:T(8,128)}, f32[2816,512]{1,0:T(8,128)}, f32[2816,512]{1,0:T(8,128)}) custom-call(s32[2]{0:T(128)S(1)} %pad_add_fusion.8.meta_ref, bf16[512,1408]{1,0:T(8,128)(2,1)S(1)} %constant_dynamic-update-slice_fusion.12.refs_0_, bf16[512,1408]{1,0:T(8,128)(2,1)S(1)} %collective-permute-done.40.refs_1_, ...), custom_call_target="tpu_custom_call" | custom-call | flops 28835840 | bytes 34603008 | tf_op jit(solution)/shard_map/turned_update/pallas_call | solution.py:540
  678.5 36.0 %gateup_update.1 = (f32[512,2,2816]{2,1,0:T(2,128)}, f32[512,2,2816]{2,1,0:T(2,128)}, f32[512,2,2816]{2,1,0:T(2,128)}) custom-call(s32[2]{0:T(128)S(1)} %pad_add_fusion.8.meta_ref, bf16[512,1408]{1,0:T(8,128)(2,1)S(1)} %constant_dynamic-update-slice_fusion.12.refs_0_, bf16[512,1408]{1,0:T(8,128)(2,1)S(1)} %collective-permute-done.40.refs_1_, ...), custom_call_target="tpu_custom_call" | custom-call | flops 57671680 | bytes 80740352 | tf_op jit(solution)/shard_map/gateup_update/pallas_call | solution.py:577
  745.2 8.7 %collective-permute-done.55 = bf16[256,512]{1,0:T(8,128)(2,1)S(1)} collective-permute-done((bf16[256,512]{1,0:T(8,128)(2,1)S(1)}, bf16[256,512]{1,0:T(8,128)(2,1)S(1)}, u32[]{:S(2)}, u32[]{:S(2)}) %collective-permute-start.55) | collective-permute-done | bytes 262176 | tf_op jit(solution)/shard_map/ppermute | solution.py:630
  762.3 9.5 %joint_update.1 = (f32[512,1024]{1,0:T(8,128)}, f32[512,1024]{1,0:T(8,128)}, f32[512,1024]{1,0:T(8,128)}, f32[512,512]{1,0:T(8,128)}, f32[512,512]{1,0:T(8,128)}, /*index=5*/f32[512,512]{1,0:T(8,128)}) custom-call(s32[2]{0:T(128)S(1)} %pad_add_fusion.8.meta_ref, bf16[256,768]{1,0:T(8,128)(2,1)S(1)} %pad_maximum_fusion.12.refs_0_, ...), custom_call_target="tpu_custom_call" | custom-call | flops 15728640 | bytes 18874368 | tf_op jit(solution)/shard_map/joint_update/pallas_call | solution.py:498
  (522 shorter events, 389.7 us)
Async XLA Ops:
  7.2 108.5 %all-gather.5.cloned.1.call-start = ((), (), s32[]{:S(2)}) async-start(), calls=%async_computation.5 | async-start | bytes 5898240 | tf_op jit(solution)/shard_map/all_gather | solution.py:749
  35.7 134.9 %all-gather.7.cloned.1.call-start = ((), (), s32[]{:S(2)}) async-start(), calls=%async_computation.6 | async-start | bytes 2621440 | tf_op jit(solution)/shard_map/all_gather | solution.py:837
  70.7 42.7 %collective-permute-start.9 = (bf16[256,2048]{1,0:T(8,128)(2,1)}, bf16[256,2048]{1,0:T(8,128)(2,1)}, u32[]{:S(2)}, u32[]{:S(2)}) collective-permute-start(bf16[256,2048]{1,0:T(8,128)(2,1)} %collective-permute-done.7.refs_1_), channel_id=1, source_target_pairs={{0,16},{4,20},{8,12},{12,8},{16,0},{20,4},{24,28},{28,24},{1,17},{... | collective-permute-start | bytes 3145736 | tf_op jit(solution)/shard_map/ppermute | solution.py:659
  72.1 38.8 %collective-permute-start.11 = (bf16[256,512]{1,0:T(8,128)(2,1)}, bf16[256,512]{1,0:T(8,128)(2,1)}, u32[]{:S(2)}, u32[]{:S(2)}) collective-permute-start(bf16[256,512]{1,0:T(8,128)(2,1)} %get-tuple-element.361), channel_id=1, source_target_pairs={{0,2},{1,3},{2,0},{3,1},{4,6},{5,7},{6,4},{7,5},{8,10},{9,11},{10,... | collective-permute-start | bytes 786440 | tf_op jit(solution)/shard_map/ppermute | solution.py:630
  75.2 38.2 %collective-permute-start.12 = (bf16[256,512]{1,0:T(8,128)(2,1)}, bf16[256,512]{1,0:T(8,128)(2,1)}, u32[]{:S(2)}, u32[]{:S(2)}) collective-permute-start(bf16[256,512]{1,0:T(8,128)(2,1)} %get-tuple-element.360), channel_id=1, source_target_pairs={{0,3},{1,0},{2,1},{3,2},{4,7},{5,4},{6,5},{7,6},{8,11},{9,8},{10,9... | collective-permute-start | bytes 786440 | tf_op jit(solution)/shard_map/ppermute | solution.py:630
  126.7 157.7 %all-gather.9.cloned.1.call-start = ((), (), s32[]{:S(2)}) async-start(), calls=%async_computation.7 | async-start | bytes 12976128 | tf_op jit(solution)/shard_map/all_gather | solution.py:749
  170.7 170.1 %all-gather.11.cloned.1.call-start = ((), (), s32[]{:S(2)}) async-start(), calls=%async_computation.8 | async-start | bytes 6488064 | tf_op jit(solution)/shard_map/all_gather | solution.py:749
  203.0 195.7 %reduce-scatter.6.cloned.1.call-start = ((), (), s32[]{:S(2)}) async-start(), calls=%async_computation.9 | async-start | bytes 3604480 | tf_op jit(solution)/shard_map/reduce_scatter | solution.py:861
  340.8 159.3 %reduce-scatter.8.cloned.1.call-start = ((), (), s32[]{:S(2)}) async-start(), calls=%async_computation.10 | async-start | bytes 3604480 | tf_op jit(solution)/shard_map/reduce_scatter | solution.py:861
  416.2 157.6 %reduce-scatter.10.cloned.1.call-start = ((), (), s32[]{:S(2)}) async-start(), calls=%async_computation.11 | async-start | bytes 3604480 | tf_op jit(solution)/shard_map/reduce_scatter | solution.py:861
  433.5 210.9 %reduce-scatter.12.cloned.1.call-start = ((), (), s32[]{:S(2)}) async-start(), calls=%async_computation.12 | async-start | bytes 1310720 | tf_op jit(solution)/shard_map/reduce_scatter | solution.py:861
  468.2 31.8 %collective-permute-start.31 = (bf16[256,2048]{1,0:T(8,128)(2,1)S(1)}, bf16[256,2048]{1,0:T(8,128)(2,1)}, u32[]{:S(2)}, u32[]{:S(2)}) collective-permute-start(bf16[256,2048]{1,0:T(8,128)(2,1)S(1)} %get-tuple-element.317), channel_id=1, source_target_pairs={{0,16},{4,20},{8,12},{12,8},{16,0},{20,4},{24,28},{28,24},{1,17},{... | collective-permute-start | bytes 3145736 | tf_op jit(solution)/shard_map/ppermute | solution.py:673
  503.2 70.6 %collective-permute-start.33 = (bf16[256,2048]{1,0:T(8,128)(2,1)}, bf16[256,2048]{1,0:T(8,128)(2,1)}, u32[]{:S(2)}, u32[]{:S(2)}) collective-permute-start(bf16[256,2048]{1,0:T(8,128)(2,1)} %add_convert_fusion.7), channel_id=1, source_target_pairs={{0,4},{4,0},{8,24},{12,28},{16,20},{20,16},{24,8},{28,12},{1,5},{5... | collective-permute-start | bytes 3145736 | tf_op jit(solution)/shard_map/ppermute | solution.py:679
  504.7 80.4 %collective-permute-start.40 = (bf16[512,1408]{1,0:T(8,128)(2,1)S(1)}, bf16[512,1408]{1,0:T(8,128)(2,1)S(1)}, u32[]{:S(2)}, u32[]{:S(2)}) collective-permute-start(bf16[512,1408]{1,0:T(8,128)(2,1)S(1)} %constant_dynamic-update-slice_fusion.12.refs_0_), channel_id=1, source_target_pairs={{0,16},{16,0},{1,17},{17,1},{2,18},{18,2},{3,19},{19,3},{4,20},{20... | collective-permute-start | bytes 4325384 | tf_op jit(solution)/shard_map/ppermute | solution.py:636
  508.3 33.2 %collective-permute-start.34 = (bf16[1024,256]{1,0:T(8,128)(2,1)S(1)}, bf16[1024,256]{1,0:T(8,128)(2,1)S(1)}, u32[]{:S(2)}, u32[]{:S(2)}) collective-permute-start(bf16[1024,256]{1,0:T(8,128)(2,1)S(1)} %bitcast.180), channel_id=1, source_target_pairs={{0,3},{1,0},{2,1},{3,2},{4,7},{5,4},{6,5},{7,6},{8,11},{9,8},{10,9... | collective-permute-start | bytes 1572872 | tf_op jit(solution)/shard_map/ppermute | solution.py:630
  508.3 53.5 %collective-permute-start.35 = (bf16[1024,256]{1,0:T(8,128)(2,1)S(1)}, bf16[1024,256]{1,0:T(8,128)(2,1)S(1)}, u32[]{:S(2)}, u32[]{:S(2)}) collective-permute-start(bf16[1024,256]{1,0:T(8,128)(2,1)S(1)} %bitcast.179), channel_id=1, source_target_pairs={{0,2},{1,3},{2,0},{3,1},{4,6},{5,7},{6,4},{7,5},{8,10},{9,11},{10,... | collective-permute-start | bytes 1572872 | tf_op jit(solution)/shard_map/ppermute | solution.py:630
  518.9 54.1 %collective-permute-start.36 = (bf16[1024,256]{1,0:T(8,128)(2,1)S(1)}, bf16[1024,256]{1,0:T(8,128)(2,1)S(1)}, u32[]{:S(2)}, u32[]{:S(2)}) collective-permute-start(bf16[1024,256]{1,0:T(8,128)(2,1)S(1)} %bitcast.178), channel_id=1, source_target_pairs={{0,1},{1,2},{2,3},{3,0},{4,5},{5,6},{6,7},{7,4},{8,9},{9,10},{10,1... | collective-permute-start | bytes 1572872 | tf_op jit(solution)/shard_map/ppermute | solution.py:630
  542.2 50.7 %collective-permute-start.41 = (bf16[512,1408]{1,0:T(8,128)(2,1)S(1)}, bf16[512,1408]{1,0:T(8,128)(2,1)}, u32[]{:S(2)}, u32[]{:S(2)}) collective-permute-start(bf16[512,1408]{1,0:T(8,128)(2,1)S(1)} %constant_dynamic-update-slice_fusion.12.refs_0_), channel_id=1, source_target_pairs={{0,8},{8,0},{1,9},{9,1},{2,10},{10,2},{3,11},{11,3},{4,12},{12,4},... | collective-permute-start | bytes 4325384 | tf_op jit(solution)/shard_map/ppermute | solution.py:633
  613.5 107.4 %reduce-scatter.14.cloned.1.call-start = ((), (), s32[]{:S(2)}) async-start(), calls=%async_computation.13 | async-start | bytes 1966080 | tf_op jit(solution)/shard_map/reduce_scatter | solution.py:861
  656.2 64.6 %collective-permute-start.49 = (bf16[256,512]{1,0:T(8,128)(2,1)}, bf16[256,512]{1,0:T(8,128)(2,1)}, u32[]{:S(2)}, u32[]{:S(2)}) collective-permute-start(bf16[256,512]{1,0:T(8,128)(2,1)} %get-tuple-element.345), channel_id=1, source_target_pairs={{0,2},{1,3},{2,0},{3,1},{4,6},{5,7},{6,4},{7,5},{8,10},{9,11},{10,... | collective-permute-start | bytes 786440 | tf_op jit(solution)/shard_map/ppermute | solution.py:630
  658.5 62.3 %collective-permute-start.50 = (bf16[256,512]{1,0:T(8,128)(2,1)S(1)}, bf16[256,512]{1,0:T(8,128)(2,1)}, u32[]{:S(2)}, u32[]{:S(2)}) collective-permute-start(bf16[256,512]{1,0:T(8,128)(2,1)S(1)} %get-tuple-element.344), channel_id=1, source_target_pairs={{0,3},{1,0},{2,1},{3,2},{4,7},{5,4},{6,5},{7,6},{8,11},{9,8},{10,9... | collective-permute-start | bytes 786440 | tf_op jit(solution)/shard_map/ppermute | solution.py:630
  671.5 49.3 %collective-permute-start.51 = (f32[2,512]{1,0:T(2,128)S(1)}, f32[2,512]{1,0:T(2,128)S(1)}, u32[]{:S(2)}, u32[]{:S(2)}) collective-permute-start(f32[2,512]{1,0:T(2,128)S(1)} %get-tuple-element.404), channel_id=1, source_target_pairs={{0,1},{1,2},{2,3},{3,0},{4,5},{5,6},{6,7},{7,4},{8,9},{9,10},{10,1... | collective-permute-start | bytes 12296 | tf_op jit(solution)/shard_map/ppermute | solution.py:630
  677.1 43.7 %collective-permute-start.52 = (f32[2,512]{1,0:T(2,128)S(1)}, f32[2,512]{1,0:T(2,128)S(1)}, u32[]{:S(2)}, u32[]{:S(2)}) collective-permute-start(f32[2,512]{1,0:T(2,128)S(1)} %get-tuple-element.403), channel_id=1, source_target_pairs={{0,2},{1,3},{2,0},{3,1},{4,6},{5,7},{6,4},{7,5},{8,10},{9,11},{10,... | collective-permute-start | bytes 12296 | tf_op jit(solution)/shard_map/ppermute | solution.py:630
  677.2 43.7 %collective-permute-start.53 = (f32[2,512]{1,0:T(2,128)S(1)}, f32[2,512]{1,0:T(2,128)S(1)}, u32[]{:S(2)}, u32[]{:S(2)}) collective-permute-start(f32[2,512]{1,0:T(2,128)S(1)} %get-tuple-element.402), channel_id=1, source_target_pairs={{0,3},{1,0},{2,1},{3,2},{4,7},{5,4},{6,5},{7,6},{8,11},{9,8},{10,9... | collective-permute-start | bytes 12296 | tf_op jit(solution)/shard_map/ppermute | solution.py:630
  (144 other events, 1705.1 us)
Sparse Core Ops, SparseCore 0:
  35.9 72.4 all-gather.4
  126.8 43.8 all-gather.6
  172.8 106.3 all-gather.8
  281.3 59.4 all-gather.10
  342.9 55.8 reduce-scatter.5
  416.3 55.7 reduce-scatter.7
  475.0 80.1 reduce-scatter.9
  613.6 30.7 reduce-scatter.11
  650.1 58.0 reduce-scatter.13

commit v6 on v5

--- a/solution.py
+++ b/solution.py
@@ -585,7 +585,7 @@
         out_shape=[jax.ShapeDtypeStruct(shape, jnp.float32)] * 3,
         compiler_params=pltpu.CompilerParams(vmem_limit_bytes=VMEM_LIMIT),
         cost_estimate=pl.CostEstimate(
-            flops=20 * weights[0].size, bytes_accessed=28 * weights[0].size, transcendentals=0
+            flops=20 * weights[0].size, bytes_accessed=4 * weights[0].size, transcendentals=0
         ),
         name="gateup_update",
     )(meta, *gates, *ups, *weights)
@@ -1011,11 +1011,12 @@
         return first
 
     grad_normed_one = reduce_tokens(joint_products, joint_others, joint_owns)
-    joint_piece = scatter(work["joint_total"])
+    joint_total, up_shards = lax.optimization_barrier((work["joint_total"], work["up_shards"]))
+    joint_piece = scatter(joint_total)
     gateup_new = gateup_update(
         meta_core,
         work["shards"],
-        work["up_shards"],
+        up_shards,
         [w_gateup, gateup_moment, gateup_square],
         32,
     )
@@ -1035,9 +1036,11 @@
     gain_parts = [pick(gain_blocks, line)] + [
         shift(pick(gain_blocks, (line + by) % lines), "col", lines, by) for by in range(1, lines)
     ]
-    joint_piece, input_grad, gateup_new, output_parts, gain_parts = lax.optimization_barrier(
-        (joint_piece, input_grad.astype(jnp.bfloat16), gateup_new, output_parts, gain_parts)
-    )
+    output_shards = collect(work["output_piece"])
+    joint_piece, input_grad, gateup_new, output_parts, output_shards = lax.optimization_barrier(
+        (joint_piece, input_grad.astype(jnp.bfloat16), gateup_new, output_parts, output_shards)
+    )
+    gain_parts, output_shards = lax.optimization_barrier((gain_parts, output_shards))
     grad_gains = sum(gain_parts[1:], gain_parts[0])
     for axis, size in (("core", 2), ("y", 2), ("row", rows_on)):
         own_gains = grad_gains
@@ -1061,7 +1064,7 @@
     )
     output_new = turned_update(
         meta_core,
-        collect(work["output_piece"]),
+        output_shards,
         [w_output, output_moment, output_square],
         (HEADS * HEAD_DIM // 64) ** (-0.5),
         True,

time: 791 us -> 775 us (0.980)
  starting transfers between devices: 94.5 us -> 78.1 us
  waiting for transfers between devices: 294 us -> 281 us
  Pallas kernels: 165 us -> 175 us
    ppermute x25, starting transfers between devices: 46.4 us -> 34.8 us  [shift(): lax.ppermute(value, axis, [(i, (i + by) % size) for i in range(size)])]
    ppermute x25, waiting for transfers between devices: 113 us -> 103 us  [shift(): lax.ppermute(value, axis, [(i, (i + by) % size) for i in range(size)])]
    unnamed x215 -> x231, local copies, waits for them, and re-layouts: 43.8 us -> 46.1 us
  transfers between devices with their start and end apart: 76 -> 76, of which waited for: 35 -> 33; matrix products, arithmetic and copies ran while one was open for 22% -> 23% of each run, Pallas kernels for 19% -> 21%
where the time goes in v6:
time: 775 us; the launch traced here: 762 us
  waiting for transfers between devices  281 us (36%)
  Pallas kernels  175 us (23%)
  matrix products  89.4 us (12%)
  starting transfers between devices  78.1 us (10%)
  local copies, waits for them, and re-layouts  73.4 us (9%)
  other arithmetic  48.6 us (6%)
  between operations  15.9 us (2%)
    ppermute x25, waiting for transfers between devices, shift(): lax.ppermute(value, axis, [(i, (i + by) % size) for i in range(size)])  103 us
    ppermute x4, waiting for transfers between devices, gather_tokens(): first = lax.ppermute(own, near, first_pairs)  75 us
    dot_general x10, matrix products, dot_tn(): lax.dot_general(left, right, (((0,), (0,)), ((), ())), preferred_element_...  57.7 us
    unnamed x231, local copies, waits for them, and re-layouts  46.1 us
    pallas_call x1, Pallas kernels, gateup_update(): pl.pallas_call(gateup_update_kernel, grid_spec=pltpu.PrefetchScalarGridSp...  36 us
    pallas_call x2, Pallas kernels, widen_back(): pl.pallas_call(functools.partial(widen_back_kernel, slots, len(kept)), gr...  34.8 us
    ppermute x25, starting transfers between devices, shift(): lax.ppermute(value, axis, [(i, (i + by) % size) for i in range(size)])  34.8 us
    pallas_call x1, Pallas kernels, attend_back(): pl.pallas_call(functools.partial(attend_back_kernel, parts, lines), grid_...  28 us
  transfers between devices with their start and end apart: 76, of which 33 were waited for; matrix products, arithmetic and copies ran while one was open for 23% of the time, Pallas kernels for 21%

profile of v6, /device:TPU:11, one launch (start us, length us, event | category | flops | bytes accessed | tf_op | source)
XLA Modules:
  0.0 762.2 jit_solution(14886215553949796726)
XLA Ops:
  47.5 20.1 %collective-permute-done.7.refs_1_ = bf16[256,2048]{1,0:T(8,128)(2,1)} collective-permute-done((bf16[256,2048]{1,0:T(8,128)(2,1)S(1)}, bf16[256,2048]{1,0:T(8,128)(2,1)}, u32[]{:S(2)}, u32[]{:S(2)}) %collective-permute-start.7) | collective-permute-done | bytes 1048608 | tf_op jit(solution)/shard_map/ppermute | solution.py:656
  78.2 9.5 %collective-permute-done.10 = bf16[256,512]{1,0:T(8,128)(2,1)} collective-permute-done((bf16[256,512]{1,0:T(8,128)(2,1)}, bf16[256,512]{1,0:T(8,128)(2,1)}, u32[]{:S(2)}, u32[]{:S(2)}) %collective-permute-start.10) | collective-permute-done | bytes 262176 | tf_op jit(solution)/shard_map/ppermute | solution.py:630
  87.7 23.2 %collective-permute-done.11 = bf16[256,512]{1,0:T(8,128)(2,1)} collective-permute-done((bf16[256,512]{1,0:T(8,128)(2,1)}, bf16[256,512]{1,0:T(8,128)(2,1)}, u32[]{:S(2)}, u32[]{:S(2)}) %collective-permute-start.11) | collective-permute-done | bytes 262176 | tf_op jit(solution)/shard_map/ppermute | solution.py:630
  133.7 19.2 %collective-permute-done.13.refs_1_ = bf16[256,2048]{1,0:T(8,128)(2,1)S(1)} collective-permute-done((bf16[256,2048]{1,0:T(8,128)(2,1)S(1)}, bf16[256,2048]{1,0:T(8,128)(2,1)S(1)}, u32[]{:S(2)}, u32[]{:S(2)}) %collective-permute-start.13) | collective-permute-done | bytes 1048608 | tf_op jit(solution)/shard_map/ppermute | solution.py:656
  161.5 8.6 %collective-permute-done.15.refs_1_ = bf16[256,2048]{1,0:T(8,128)(2,1)S(1)} collective-permute-done((bf16[256,2048]{1,0:T(8,128)(2,1)}, bf16[256,2048]{1,0:T(8,128)(2,1)S(1)}, u32[]{:S(2)}, u32[]{:S(2)}) %collective-permute-start.15) | collective-permute-done | bytes 1048608 | tf_op jit(solution)/shard_map/ppermute | solution.py:659
  170.7 10.9 %all-gather.11.cloned.1.call-start = ((), (), s32[]{:S(2)}) async-start(), calls=%async_computation.8 | async-start | bytes 6488064 | tf_op jit(solution)/shard_map/all_gather | solution.py:749
  185.0 16.7 %attend.1 = (bf16[1024,512]{1,0:T(8,128)(2,1)S(1)}, f32[4,2,1024]{2,1,0:T(2,128)S(1)}) custom-call(s32[17]{0:T(128)S(1)} %pad_add_fusion.7.meta_ref, bf16[1024,512]{1,0:T(8,128)(2,1)S(1)} %copy-done.53, bf16[4,4,256,256]{3,2,1,0:T(8,128)(2,1)S(1)} %copy-done.45, s32[4,2,256]{2,1,0:T(2,128)S(1)} %pad_add_fusion.2.info_ref.refs_4_), custom_call_target="tpu_custom_call" | custom-call | flops 3221225472 | bytes 4194304 | tf_op jit(solution)/shard_map/attend/pallas_call | solution.py:275
  211.1 9.6 %collective-permute-done.16 = bf16[256,2048]{1,0:T(8,128)(2,1)} collective-permute-done((bf16[256,2048]{1,0:T(8,128)(2,1)}, bf16[256,2048]{1,0:T(8,128)(2,1)}, u32[]{:S(2)}, u32[]{:S(2)}) %collective-permute-start.16) | collective-permute-done | bytes 1048608 | tf_op jit(solution)/shard_map/ppermute | solution.py:673
  220.8 10.9 %collective-permute-done.17 = bf16[256,2048]{1,0:T(8,128)(2,1)} collective-permute-done((bf16[256,2048]{1,0:T(8,128)(2,1)}, bf16[256,2048]{1,0:T(8,128)(2,1)}, u32[]{:S(2)}, u32[]{:S(2)}) %collective-permute-start.17) | collective-permute-done | bytes 1048608 | tf_op jit(solution)/shard_map/ppermute | solution.py:674
  234.6 12.7 %collective-permute-done.18 = bf16[256,2048]{1,0:T(8,128)(2,1)S(1)} collective-permute-done((bf16[256,2048]{1,0:T(8,128)(2,1)S(1)}, bf16[256,2048]{1,0:T(8,128)(2,1)S(1)}, u32[]{:S(2)}, u32[]{:S(2)}) %collective-permute-start.18) | collective-permute-done | bytes 1048608 | tf_op jit(solution)/shard_map/ppermute | solution.py:679
  252.2 20.7 %collective-permute-done.19.refs_1_ = bf16[256,2048]{1,0:T(8,128)(2,1)} collective-permute-done((bf16[256,2048]{1,0:T(8,128)(2,1)S(1)}, bf16[256,2048]{1,0:T(8,128)(2,1)}, u32[]{:S(2)}, u32[]{:S(2)}) %collective-permute-start.19) | collective-permute-done | bytes 1048608 | tf_op jit(solution)/shard_map/ppermute | solution.py:656
  281.9 9.2 %collective-permute-done.21.refs_3_ = bf16[256,2048]{1,0:T(8,128)(2,1)} collective-permute-done((bf16[256,2048]{1,0:T(8,128)(2,1)}, bf16[256,2048]{1,0:T(8,128)(2,1)}, u32[]{:S(2)}, u32[]{:S(2)}) %collective-permute-start.21) | collective-permute-done | bytes 1048608 | tf_op jit(solution)/shard_map/ppermute | solution.py:659
  293.6 19.9 %widen.1 = (bf16[1024,1408]{1,0:T(8,128)(2,1)}, bf16[1024,1408]{1,0:T(8,128)(2,1)}, bf16[1024,1408]{1,0:T(8,128)(2,1)}) custom-call(bf16[256,2048]{1,0:T(8,128)(2,1)S(1)} %copy-done.2, bf16[256,2048]{1,0:T(8,128)(2,1)} %collective-permute-done.19.refs_1_, bf16[256,2048]{1,0:T(8,128)(2,1)S(1)} %copy-done.25, ...), custom_call_target="tpu_custom_call" | custom-call | flops 11811160064 | bytes 24379392 | tf_op jit(solution)/shard_map/widen/pallas_call | solution.py:141
  327.9 8.5 %add_convert_fusion.2 = bf16[1024,1408]{1,0:T(8,128)(2,1)} fusion(bf16[1024,1408]{1,0:T(8,128)(2,1)} %collective-permute-done.22, bf16[1024,1408]{1,0:T(8,128)(2,1)} %get-tuple-element.223, bf16[1024,2048]{1,0:T(8,128)(2,1)} %constant_dynamic-update-slice_fusion.8, s32[]{:T(128)S(6)} %select_n.357), kind=kOutput, calls=%fused_computation.2 | convolution fusion | flops 2957115392 | bytes 10747908 | tf_op jit(solution)/shard_map/dot_general | solution.py:36
  343.7 18.4 %widen_back.2 = (bf16[1024,1408]{1,0:T(8,128)(2,1)}, bf16[1024,1408]{1,0:T(8,128)(2,1)}, bf16[512,2048]{1,0:T(8,128)(2,1)S(1)}) custom-call(bf16[256,2048]{1,0:T(8,128)(2,1)S(1)} %collective-permute-done.14.refs_0_, bf16[256,2048]{1,0:T(8,128)(2,1)S(1)} %collective-permute-done.15.refs_1_, bf16[2048,1408]{1,0:T(8,128)(2,1)} %all-gather.11.cloned.1.call-done.refs_2_, ...), custom_call_target="tpu_custom_call" | custom-call | flops 1476395008 | bytes 5767168 | tf_op jit(solution)/shard_map/widen_back/pallas_call | solution.py:179
  363.9 16.4 %widen_back.3 = (bf16[1024,1408]{1,0:T(8,128)(2,1)}, bf16[1024,1408]{1,0:T(8,128)(2,1)}, bf16[512,2048]{1,0:T(8,128)(2,1)S(1)}) custom-call(bf16[256,2048]{1,0:T(8,128)(2,1)S(1)} %slice_dynamic-update-slice_fusion.refs_0_, bf16[256,2048]{1,0:T(8,128)(2,1)S(1)} %copy-done.5, ...), custom_call_target="tpu_custom_call", output_to_operand_aliasing={{0}: (6, {}), {1}: (7, {})} | custom-call | flops 1476395008 | bytes 5767168 | tf_op jit(solution)/shard_map/widen_back/pallas_call | solution.py:179
  434.7 15.1 %collective-permute-done.28 = bf16[256,2048]{1,0:T(8,128)(2,1)S(1)} collective-permute-done((bf16[256,2048]{1,0:T(8,128)(2,1)}, bf16[256,2048]{1,0:T(8,128)(2,1)S(1)}, u32[]{:S(2)}, u32[]{:S(2)}) %collective-permute-start.28) | collective-permute-done | bytes 1048608 | tf_op jit(solution)/shard_map/ppermute | solution.py:656
  474.9 28.0 %attend_back.1 = (bf16[1024,512]{1,0:T(8,128)(2,1)S(1)}, bf16[4,256,256]{2,1,0:T(8,128)(2,1)S(1)}, bf16[4,256,256]{2,1,0:T(8,128)(2,1)S(1)}, bf16[4,256,256]{2,1,0:T(8,128)(2,1)S(1)}, bf16[4,256,256]{2,1,0:T(8,128)(2,1)S(1)}) custom-call(s32[17]{0:T(128)S(1)} %pad_add_fusion.7.meta_ref, bf16[1024,512]{1,0:T(8,128)(2,1)S(1)} %copy-done.54, ...), custom_call_target="tpu_custom_call" | custom-call | flops 8053063680 | bytes 8388608 | tf_op jit(solution)/shard_map/attend_back/pallas_call | solution.py:387
  525.7 15.8 %collective-permute-done.34.refs_1_ = bf16[1024,256]{1,0:T(8,128)(2,1)S(1)} collective-permute-done((bf16[1024,256]{1,0:T(8,128)(2,1)S(1)}, bf16[1024,256]{1,0:T(8,128)(2,1)S(1)}, u32[]{:S(2)}, u32[]{:S(2)}) %collective-permute-start.34) | collective-permute-done | bytes 524320 | tf_op jit(solution)/shard_map/ppermute | solution.py:630
  542.4 19.6 %collective-permute-done.35.refs_2_ = bf16[1024,256]{1,0:T(8,128)(2,1)S(1)} collective-permute-done((bf16[1024,256]{1,0:T(8,128)(2,1)S(1)}, bf16[1024,256]{1,0:T(8,128)(2,1)S(1)}, u32[]{:S(2)}, u32[]{:S(2)}) %collective-permute-start.35) | collective-permute-done | bytes 524320 | tf_op jit(solution)/shard_map/ppermute | solution.py:630
  605.2 8.2 %collective-permute-done.38 = bf16[256,2048]{1,0:T(8,128)(2,1)} collective-permute-done((bf16[256,2048]{1,0:T(8,128)(2,1)}, bf16[256,2048]{1,0:T(8,128)(2,1)}, u32[]{:S(2)}, u32[]{:S(2)}) %collective-permute-start.38) | collective-permute-done | bytes 1048608 | tf_op jit(solution)/shard_map/ppermute | solution.py:674
  622.0 15.0 %turned_update.2 = (f32[2816,512]{1,0:T(8,128)}, f32[2816,512]{1,0:T(8,128)}, f32[2816,512]{1,0:T(8,128)}) custom-call(s32[2]{0:T(128)S(1)} %pad_add_fusion.8.meta_ref, bf16[512,1408]{1,0:T(8,128)(2,1)S(1)} %constant_dynamic-update-slice_fusion.12.refs_0_, bf16[512,1408]{1,0:T(8,128)(2,1)S(1)} %collective-permute-done.40.refs_1_, ...), custom_call_target="tpu_custom_call" | custom-call | flops 28835840 | bytes 34603008 | tf_op jit(solution)/shard_map/turned_update/pallas_call | solution.py:540
  668.7 36.0 %gateup_update.1 = (f32[512,2,2816]{2,1,0:T(2,128)}, f32[512,2,2816]{2,1,0:T(2,128)}, f32[512,2,2816]{2,1,0:T(2,128)}) custom-call(s32[2]{0:T(128)S(1)} %pad_add_fusion.8.meta_ref, bf16[512,1408]{1,0:T(8,128)(2,1)S(1)} %constant_dynamic-update-slice_fusion.12.refs_0_, bf16[512,1408]{1,0:T(8,128)(2,1)S(1)} %collective-permute-done.40.refs_1_, ...), custom_call_target="tpu_custom_call" | custom-call | flops 57671680 | bytes 11534336 | tf_op jit(solution)/shard_map/gateup_update/pallas_call | solution.py:577
  746.1 9.5 %joint_update.1 = (f32[512,1024]{1,0:T(8,128)}, f32[512,1024]{1,0:T(8,128)}, f32[512,1024]{1,0:T(8,128)}, f32[512,512]{1,0:T(8,128)}, f32[512,512]{1,0:T(8,128)}, /*index=5*/f32[512,512]{1,0:T(8,128)}) custom-call(s32[2]{0:T(128)S(1)} %pad_add_fusion.8.meta_ref, bf16[256,768]{1,0:T(8,128)(2,1)S(1)} %pad_maximum_fusion.12.refs_0_, ...), custom_call_target="tpu_custom_call" | custom-call | flops 15728640 | bytes 18874368 | tf_op jit(solution)/shard_map/joint_update/pallas_call | solution.py:498
  (538 shorter events, 364.5 us)
Async XLA Ops:
  7.2 108.5 %all-gather.5.cloned.1.call-start = ((), (), s32[]{:S(2)}) async-start(), calls=%async_computation.5 | async-start | bytes 5898240 | tf_op jit(solution)/shard_map/all_gather | solution.py:749
  35.7 134.9 %all-gather.7.cloned.1.call-start = ((), (), s32[]{:S(2)}) async-start(), calls=%async_computation.6 | async-start | bytes 2621440 | tf_op jit(solution)/shard_map/all_gather | solution.py:837
  70.7 42.7 %collective-permute-start.9 = (bf16[256,2048]{1,0:T(8,128)(2,1)}, bf16[256,2048]{1,0:T(8,128)(2,1)}, u32[]{:S(2)}, u32[]{:S(2)}) collective-permute-start(bf16[256,2048]{1,0:T(8,128)(2,1)} %collective-permute-done.7.refs_1_), channel_id=1, source_target_pairs={{0,16},{4,20},{8,12},{12,8},{16,0},{20,4},{24,28},{28,24},{1,17},{... | collective-permute-start | bytes 3145736 | tf_op jit(solution)/shard_map/ppermute | solution.py:659
  72.1 38.8 %collective-permute-start.11 = (bf16[256,512]{1,0:T(8,128)(2,1)}, bf16[256,512]{1,0:T(8,128)(2,1)}, u32[]{:S(2)}, u32[]{:S(2)}) collective-permute-start(bf16[256,512]{1,0:T(8,128)(2,1)} %get-tuple-element.387), channel_id=1, source_target_pairs={{0,2},{1,3},{2,0},{3,1},{4,6},{5,7},{6,4},{7,5},{8,10},{9,11},{10,... | collective-permute-start | bytes 786440 | tf_op jit(solution)/shard_map/ppermute | solution.py:630
  75.2 38.2 %collective-permute-start.12 = (bf16[256,512]{1,0:T(8,128)(2,1)}, bf16[256,512]{1,0:T(8,128)(2,1)}, u32[]{:S(2)}, u32[]{:S(2)}) collective-permute-start(bf16[256,512]{1,0:T(8,128)(2,1)} %get-tuple-element.386), channel_id=1, source_target_pairs={{0,3},{1,0},{2,1},{3,2},{4,7},{5,4},{6,5},{7,6},{8,11},{9,8},{10,9... | collective-permute-start | bytes 786440 | tf_op jit(solution)/shard_map/ppermute | solution.py:630
  126.7 164.4 %all-gather.9.cloned.1.call-start = ((), (), s32[]{:S(2)}) async-start(), calls=%async_computation.7 | async-start | bytes 12976128 | tf_op jit(solution)/shard_map/all_gather | solution.py:749
  170.7 170.1 %all-gather.11.cloned.1.call-start = ((), (), s32[]{:S(2)}) async-start(), calls=%async_computation.8 | async-start | bytes 6488064 | tf_op jit(solution)/shard_map/all_gather | solution.py:749
  208.0 190.8 %reduce-scatter.6.cloned.1.call-start = ((), (), s32[]{:S(2)}) async-start(), calls=%async_computation.9 | async-start | bytes 3604480 | tf_op jit(solution)/shard_map/reduce_scatter | solution.py:861
  340.8 165.5 %reduce-scatter.8.cloned.1.call-start = ((), (), s32[]{:S(2)}) async-start(), calls=%async_computation.10 | async-start | bytes 3604480 | tf_op jit(solution)/shard_map/reduce_scatter | solution.py:861
  416.2 157.8 %reduce-scatter.10.cloned.1.call-start = ((), (), s32[]{:S(2)}) async-start(), calls=%async_computation.11 | async-start | bytes 3604480 | tf_op jit(solution)/shard_map/reduce_scatter | solution.py:861
  433.5 210.9 %reduce-scatter.12.cloned.1.call-start = ((), (), s32[]{:S(2)}) async-start(), calls=%async_computation.12 | async-start | bytes 1310720 | tf_op jit(solution)/shard_map/reduce_scatter | solution.py:861
  468.2 38.1 %collective-permute-start.31 = (bf16[256,2048]{1,0:T(8,128)(2,1)S(1)}, bf16[256,2048]{1,0:T(8,128)(2,1)}, u32[]{:S(2)}, u32[]{:S(2)}) collective-permute-start(bf16[256,2048]{1,0:T(8,128)(2,1)S(1)} %get-tuple-element.343), channel_id=1, source_target_pairs={{0,16},{4,20},{8,12},{12,8},{16,0},{20,4},{24,28},{28,24},{1,17},{... | collective-permute-start | bytes 3145736 | tf_op jit(solution)/shard_map/ppermute | solution.py:673
  468.5 37.7 %collective-permute-start.32 = (bf16[256,2048]{1,0:T(8,128)(2,1)S(1)}, bf16[256,2048]{1,0:T(8,128)(2,1)}, u32[]{:S(2)}, u32[]{:S(2)}) collective-permute-start(bf16[256,2048]{1,0:T(8,128)(2,1)S(1)} %get-tuple-element.342), channel_id=1, source_target_pairs={{0,16},{4,20},{8,12},{12,8},{16,0},{20,4},{24,28},{28,24},{1,17},{... | collective-permute-start | bytes 3145736 | tf_op jit(solution)/shard_map/ppermute | solution.py:674
  509.4 64.5 %collective-permute-start.33 = (bf16[256,2048]{1,0:T(8,128)(2,1)}, bf16[256,2048]{1,0:T(8,128)(2,1)}, u32[]{:S(2)}, u32[]{:S(2)}) collective-permute-start(bf16[256,2048]{1,0:T(8,128)(2,1)} %add_convert_fusion.7), channel_id=1, source_target_pairs={{0,4},{4,0},{8,24},{12,28},{16,20},{20,16},{24,8},{28,12},{1,5},{5... | collective-permute-start | bytes 3145736 | tf_op jit(solution)/shard_map/ppermute | solution.py:679
  510.9 74.7 %collective-permute-start.40 = (bf16[512,1408]{1,0:T(8,128)(2,1)S(1)}, bf16[512,1408]{1,0:T(8,128)(2,1)S(1)}, u32[]{:S(2)}, u32[]{:S(2)}) collective-permute-start(bf16[512,1408]{1,0:T(8,128)(2,1)S(1)} %constant_dynamic-update-slice_fusion.12.refs_0_), channel_id=1, source_target_pairs={{0,16},{16,0},{1,17},{17,1},{2,18},{18,2},{3,19},{19,3},{4,20},{20... | collective-permute-start | bytes 4325384 | tf_op jit(solution)/shard_map/ppermute | solution.py:636
  514.5 47.5 %collective-permute-start.35 = (bf16[1024,256]{1,0:T(8,128)(2,1)S(1)}, bf16[1024,256]{1,0:T(8,128)(2,1)S(1)}, u32[]{:S(2)}, u32[]{:S(2)}) collective-permute-start(bf16[1024,256]{1,0:T(8,128)(2,1)S(1)} %bitcast.179), channel_id=1, source_target_pairs={{0,2},{1,3},{2,0},{3,1},{4,6},{5,7},{6,4},{7,5},{8,10},{9,11},{10,... | collective-permute-start | bytes 1572872 | tf_op jit(solution)/shard_map/ppermute | solution.py:630
  523.5 49.7 %collective-permute-start.36 = (bf16[1024,256]{1,0:T(8,128)(2,1)S(1)}, bf16[1024,256]{1,0:T(8,128)(2,1)S(1)}, u32[]{:S(2)}, u32[]{:S(2)}) collective-permute-start(bf16[1024,256]{1,0:T(8,128)(2,1)S(1)} %bitcast.178), channel_id=1, source_target_pairs={{0,1},{1,2},{2,3},{3,0},{4,5},{5,6},{6,7},{7,4},{8,9},{9,10},{10,1... | collective-permute-start | bytes 1572872 | tf_op jit(solution)/shard_map/ppermute | solution.py:630
  542.4 50.5 %collective-permute-start.41 = (bf16[512,1408]{1,0:T(8,128)(2,1)S(1)}, bf16[512,1408]{1,0:T(8,128)(2,1)}, u32[]{:S(2)}, u32[]{:S(2)}) collective-permute-start(bf16[512,1408]{1,0:T(8,128)(2,1)S(1)} %constant_dynamic-update-slice_fusion.12.refs_0_), channel_id=1, source_target_pairs={{0,8},{8,0},{1,9},{9,1},{2,10},{10,2},{3,11},{11,3},{4,12},{12,4},... | collective-permute-start | bytes 4325384 | tf_op jit(solution)/shard_map/ppermute | solution.py:633
  613.4 96.9 %reduce-scatter.14.cloned.1.call-start = ((), (), s32[]{:S(2)}) async-start(), calls=%async_computation.13 | async-start | bytes 1966080 | tf_op jit(solution)/shard_map/reduce_scatter | solution.py:861
  654.3 50.5 %collective-permute-start.48 = (bf16[256,512]{1,0:T(8,128)(2,1)S(1)}, bf16[256,512]{1,0:T(8,128)(2,1)S(1)}, u32[]{:S(2)}, u32[]{:S(2)}) collective-permute-start(bf16[256,512]{1,0:T(8,128)(2,1)S(1)} %get-tuple-element.372), channel_id=1, source_target_pairs={{0,1},{1,2},{2,3},{3,0},{4,5},{5,6},{6,7},{7,4},{8,9},{9,10},{10,1... | collective-permute-start | bytes 786440 | tf_op jit(solution)/shard_map/ppermute | solution.py:630
  656.2 50.3 %collective-permute-start.49 = (bf16[256,512]{1,0:T(8,128)(2,1)S(1)}, bf16[256,512]{1,0:T(8,128)(2,1)S(1)}, u32[]{:S(2)}, u32[]{:S(2)}) collective-permute-start(bf16[256,512]{1,0:T(8,128)(2,1)S(1)} %get-tuple-element.371), channel_id=1, source_target_pairs={{0,2},{1,3},{2,0},{3,1},{4,6},{5,7},{6,4},{7,5},{8,10},{9,11},{10,... | collective-permute-start | bytes 786440 | tf_op jit(solution)/shard_map/ppermute | solution.py:630
  658.5 49.7 %collective-permute-start.50 = (bf16[256,512]{1,0:T(8,128)(2,1)S(1)}, bf16[256,512]{1,0:T(8,128)(2,1)S(1)}, u32[]{:S(2)}, u32[]{:S(2)}) collective-permute-start(bf16[256,512]{1,0:T(8,128)(2,1)S(1)} %get-tuple-element.370), channel_id=1, source_target_pairs={{0,3},{1,0},{2,1},{3,2},{4,7},{5,4},{6,5},{7,6},{8,11},{9,8},{10,9... | collective-permute-start | bytes 786440 | tf_op jit(solution)/shard_map/ppermute | solution.py:630
  659.9 48.3 %collective-permute-start.52 = (bf16[256,512]{1,0:T(8,128)(2,1)S(1)}, bf16[256,512]{1,0:T(8,128)(2,1)S(1)}, u32[]{:S(2)}, u32[]{:S(2)}) collective-permute-start(bf16[256,512]{1,0:T(8,128)(2,1)S(1)} %copy-done.40), channel_id=1, source_target_pairs={{0,8},{8,0},{1,9},{9,1},{2,10},{10,2},{3,11},{11,3},{4,12},{12,4},... | collective-permute-start | bytes 786440 | tf_op jit(solution)/shard_map/ppermute | solution.py:633
  668.6 41.0 %collective-permute-start.53 = (bf16[256,512]{1,0:T(8,128)(2,1)S(1)}, bf16[256,512]{1,0:T(8,128)(2,1)S(1)}, u32[]{:S(2)}, u32[]{:S(2)}) collective-permute-start(bf16[256,512]{1,0:T(8,128)(2,1)S(1)} %collective-permute-done.51.refs_1_), channel_id=1, source_target_pairs={{0,8},{8,0},{1,9},{9,1},{2,10},{10,2},{3,11},{11,3},{4,12},{12,4},... | collective-permute-start | bytes 786440 | tf_op jit(solution)/shard_map/ppermute | solution.py:633
  (152 other events, 1582.9 us)
Sparse Core Ops, SparseCore 0:
  35.9 72.4 all-gather.4
  126.8 43.8 all-gather.6
  172.8 106.3 all-gather.8
  281.3 59.4 all-gather.10
  342.9 55.8 reduce-scatter.5
  416.3 55.7 reduce-scatter.7
  475.0 81.0 reduce-scatter.9
  613.6 30.7 reduce-scatter.11
  650.1 57.4 reduce-scatter.13
